TPU v7x, 128 devices: a whole 4x4x4 slice. The times are simulated.
128 devices in a mesh: wide: 32 (over y_hi, z, x), tp: 4 (over y_lo, core).
Axes of the slice: x: 4, y: 4 (y_hi: 2, y_lo: 2; y = y_hi * 2 + y_lo), z: 4, core: 2. Of those that a mesh axis runs over, the one named last changes fastest.
Arguments:
- inputs: bfloat16 [16384, 2048], P(('wide', 'tp')), may hold values from -24 to 24
- positions: int32 [16384], P('wide'), may hold values from 0 to 2047, as said below
- attn_gain: bfloat16 [2048], P('wide'), may hold values from 0.5 to 1.5
- query_weight: bfloat16 [2048, 2048], P('wide', 'tp'), may hold values from -0.125 to 0.125
- key_weight: bfloat16 [2048, 256], P('wide', 'tp'), may hold values from -0.125 to 0.125
- value_weight: bfloat16 [2048, 256], P('wide', 'tp'), may hold values from -0.125 to 0.125
- out_weight: bfloat16 [2048, 2048], P('tp', 'wide'), may hold values from -2 to 2
- mlp_gain: bfloat16 [2048], P('wide'), may hold values from 0.5 to 1.5
- gate_weight: bfloat16 [2048, 5632], P('wide', 'tp'), may hold values from -0.125 to 0.125
- up_weight: bfloat16 [2048, 5632], P('wide', 'tp'), may hold values from -0.125 to 0.125
- down_weight: bfloat16 [5632, 2048], P('tp', 'wide'), may hold values from -0.078125 to 0.078125
- cotangent: bfloat16 [16384, 2048], P(('wide', 'tp')), may hold values from -24 to 24
Outputs:
- output: bfloat16 [16384, 2048], P(('wide', 'tp'))
- input_grad: float32 [16384, 2048], P(('wide', 'tp'))
- attn_gain_grad: float32 [2048], P('wide')
- query_weight_grad: float32 [2048, 2048], P('wide', 'tp')
- key_weight_grad: float32 [2048, 256], P('wide', 'tp')
- value_weight_grad: float32 [2048, 256], P('wide', 'tp')
- out_weight_grad: float32 [2048, 2048], P('tp', 'wide')
- mlp_gain_grad: float32 [2048], P('wide')
- gate_weight_grad: float32 [2048, 5632], P('wide', 'tp')
- up_weight_grad: float32 [2048, 5632], P('wide', 'tp')
- down_weight_grad: float32 [5632, 2048], P('tp', 'wide')
Inputs may be any that keep to these rules, and one draw needn't show every extreme that they name: positions[t] is the index of token t within its document; every sequence of 2048 tokens begins a document at its first token and holds one to four documents; exactly one sequence, drawn from the seed, is a single document.
All inputs are finite; a program needn't handle non-finite values.
Results may differ from a plain program's by a relative error of at most 0.03.
Values may be sent and summed in bfloat16 or wider, within the bound.
No kernel may reach another device: no remote copies, remote signals or barrier semaphores. Data moves between devices by JAX's collectives and lax.ppermute only.
A program may use at most 256 MiB of HBM per device.

v0:
```python
import functools

import jax
import jax.numpy as jnp
from jax import lax
from jax.experimental import pallas as pl
from jax.experimental.pallas import tpu as pltpu
from jax.sharding import Mesh, PartitionSpec as P

HEADS = 32
KV = 4
HD = 64
SEQ_DEVS = 4
WIDE = ("yh", "z", "x")
TP = ("yl", "core")
RING = ("yh", "yl")
BF = jnp.bfloat16
F32 = jnp.float32

epsilon = 1e-05
masked_fill = -1e30
MIB = 1024 * 1024


def after(value, *earlier):
    return lax.optimization_barrier((value, earlier))[0]


def shift(block, axis, distance):
    n = 4 if axis == RING else lax.axis_size(axis)
    return lax.ppermute(block, axis, [(i, (i + distance) % n) for i in range(n)])


def swap(block, axis):
    return shift(block, axis, 1)


def place(axis, step=0):
    n = lax.axis_size(axis)
    return ((lax.axis_index(axis) + (step + n)) & (n - 1)).astype(jnp.uint32)


def pick(array, index, dim):
    return lax.dynamic_index_in_dim(array, index, dim, keepdims=False)


def send_stage(block, axis):
    n = lax.axis_size(axis)
    return [block] + [shift(block, axis, d) for d in (1, n - 1, *range(2, n - 1))]


def stack_stage(arrived, axis, dim):
    n = len(arrived)
    block = arrived[0]
    out = jnp.zeros(block.shape[:dim] + (n,) + block.shape[dim:], block.dtype)
    for d, piece in zip((0, 1, n - 1, *range(2, n - 1)), arrived):
        out = lax.dynamic_update_index_in_dim(out, piece, place(axis, -d), dim)
    return out


def join_sides(shard, other):
    first = lax.axis_index("yh") == 0
    return jnp.concatenate([jnp.where(first, shard, other), jnp.where(first, other, shard)], 0)


def flat(blocks):
    return blocks.reshape(-1, blocks.shape[-1])


def gather_rows(rows):
    across = swap(rows, "yl")
    return [rows, swap(rows, "core"), across, swap(across, "core")]


def gather_eight(rows):
    near = [rows, shift(rows, RING, 1), shift(rows, RING, 2), shift(rows, RING, -1)]
    return near + [swap(piece, "core") for piece in near]


def scatter_eight(own_core, other_core):
    quarter, d = own_core.shape[0] // 4, own_core.shape[1]
    own, *others = call(
        add_pieces_kernel, "add_pieces",
        [((quarter, d), F32)] + [((quarter, d), BF)] * 3, [own_core, swap(other_core, "core")],
    )
    return own, others


def send_back(others):
    one, two, three = others
    return [shift(one, RING, -1), shift(three, RING, 1), shift(two, RING, 2)]


def scatter_rows(partial):
    own, across, cores = partial
    n = own.shape[0]
    arrived = swap(cores, "core")
    other = (across.astype(F32) + arrived[n:].astype(F32)).astype(BF)
    return [own, arrived[:n], swap(other, "yl")]


def total(first, parts):
    for part in parts:
        first = first + part.astype(F32)
    return first


def exchange_sum(parts, axis, hold=()):
    near = parts[0].astype(F32)
    for d in (1, 3):
        near = near + after(shift(parts[d], axis, d), *hold).astype(F32)
    return near + after(shift(parts[2], axis, 2), *hold).astype(F32)


def wide_sum_next(part, axis, hold=()):
    n = lax.axis_size(axis)
    part = part.reshape(n, part.shape[0] // n, part.shape[1])
    pieces = [pick(part, place(axis, d), 0) for d in range(n)]
    return exchange_sum(pieces, axis, hold).astype(BF)


def mm(left, right):
    return jnp.dot(left, right, preferred_element_type=F32)


def mm_last(left, right):
    return lax.dot_general(left, right, (((1,), (1,)), ((), ())), preferred_element_type=F32)


def normed_rows(piece):
    values = piece.astype(F32)
    factor = lax.rsqrt(jnp.mean(values * values, -1, keepdims=True) + epsilon)
    return values * factor, factor


def scale_rows(piece_refs, gain, scaled_ref):
    for n, ref in enumerate(piece_refs):
        for at in range(0, ref.shape[0], 32):
            normed, _ = normed_rows(ref[at : at + 32, :])
            rows = n * ref.shape[0] + at
            scaled_ref[rows : rows + 32, :] = (normed * gain).astype(BF)


def turned(block, cos, sin):
    a, b = block[: HD // 2], block[HD // 2 :]
    return jnp.concatenate([a * cos - b * sin, b * cos + a * sin], 0)


def keys_values_kernel(*refs):
    piece_refs, (w_ref, cos_ref, sin_ref, kv_ref, scaled_ref, gains_ref) = refs[:4], refs[4:]
    gains_ref[...] = w_ref[:, 128:].T[:8].astype(F32)
    scale_rows(piece_refs, gains_ref[0:1, :], scaled_ref)
    both = mm(scaled_ref[...], w_ref[:, :128]).T
    keys = turned(both[:HD], cos_ref[...], sin_ref[...])
    kv_ref[...] = jnp.concatenate([keys, both[HD:]], 0).T.astype(BF)


def queries_kernel(x_ref, w_ref, cos_ref, sin_ref, q_ref):
    for at in range(0, q_ref.shape[0], 256):
        piece = mm(x_ref[...], w_ref[:, at : at + 256]).T
        for sub in range(0, 256, HD):
            low = turned(piece[sub : sub + HD], cos_ref[...], sin_ref[...]).astype(BF)
            q_ref[at + sub : at + sub + HD, :] = low * 0.125


def to_inner(ref, out_ref):
    half = ref.shape[1] // 2
    for at in range(0, half, 128):
        low, high = ref[:, at : at + 128], ref[:, half + at : half + at + 128]
        out_ref[:, 2 * at : 2 * at + 128] = jnp.concatenate([low[:, :HD], high[:, :HD]], 1)
        out_ref[:, 2 * at + 128 : 2 * at + 256] = jnp.concatenate([low[:, HD:], high[:, HD:]], 1)


def pack_kernel(inputs_ref, cot_ref, again_ref, mgain_ref, k_ref, v_ref, g_ref, u_ref, d_ref,
                rows_ref, cots_ref, kv_ref, mlp_ref):
    to_inner(inputs_ref, rows_ref)
    to_inner(cot_ref, cots_ref)
    kv_ref[:, :128] = jnp.concatenate([k_ref[...], v_ref[...]], 1)
    gains = jnp.concatenate(
        [again_ref[...].astype(F32), mgain_ref[...].astype(F32), jnp.zeros((126, HD), F32)], 0
    )
    kv_ref[:, 128:] = gains.T.astype(BF)
    width = g_ref.shape[1]
    down = d_ref[...]
    whole_units = 128 * (width // 256)
    tail = 2 * whole_units
    for side in range(2):
        units = slice(side * whole_units, (side + 1) * whole_units)
        ends = slice(tail + 64 * side, tail + 64 * side + 64)
        mlp_ref[side, :, :whole_units] = g_ref[:, units]
        mlp_ref[side, :, whole_units:tail] = u_ref[:, units]
        mlp_ref[side, :, tail : tail + 128] = jnp.concatenate([g_ref[:, ends], u_ref[:, ends]], 1)
        mlp_ref[side, :, tail + 128 : tail + 128 + whole_units] = down[:, units]
        mlp_ref[side, :, tail + 128 + whole_units :] = jnp.concatenate(
            [down[:, ends], jnp.zeros_like(down[:, ends])], 1
        )


def finish_mlp_kernel(side_ref, pair_ref, other_ref, gate_ref, up_ref, down_ref):
    rows = pl.ds(pl.multiple_of(side_ref[0, 0] * HD, HD), HD)
    own, other = pair_ref[rows, :].astype(F32), other_ref[...].astype(F32)
    here = side_ref[0, 0] == 0
    halves = jnp.where(here, own, other), jnp.where(here, other, own)
    units = 128 * (gate_ref.shape[1] // 256)
    tail = 2 * units
    down = []
    for n, half in enumerate(halves):
        gate_ref[:, n * units : (n + 1) * units] = half[:, :units]
        up_ref[:, n * units : (n + 1) * units] = half[:, units:tail]
        down.append(half[:, tail + 128 : tail + 128 + units])
    ends = [half[:, tail : tail + 128] for half in halves]
    gate_ref[:, tail:] = jnp.concatenate([end[:, :64] for end in ends], 1)
    up_ref[:, tail:] = jnp.concatenate([end[:, 64:] for end in ends], 1)
    down += [half[:, tail + 128 + units : tail + 192 + units] for half in halves]
    for n in range(2):
        down_ref[:, n * units : (n + 1) * units] = down[n]
    down_ref[:, tail:] = jnp.concatenate(down[2:], 1)


def finish_attn_kernel(side_ref, pair_ref, other_ref, q_ref, k_ref, v_ref, o_ref):
    rows = pl.ds(pl.multiple_of(side_ref[0, 0] * HD, HD), HD)
    both = pair_ref[rows, :].astype(F32) + other_ref[...].astype(F32)
    width = q_ref.shape[1]
    q_ref[...] = both[:, :width]
    k_ref[...] = both[:, width : width + HD]
    v_ref[...] = both[:, width + HD : width + 2 * HD]
    o_ref[...] = both[:, width + 2 * HD :]


def add_pieces_kernel(one_ref, two_ref, *outs):
    for n, out in enumerate(outs):
        rows = slice(n * out.shape[0], (n + 1) * out.shape[0])
        out[...] = (one_ref[rows, :].astype(F32) + two_ref[rows, :].astype(F32)).astype(out.dtype)


def pair_pieces_kernel(odd_ref, one_ref, two_ref, own_ref, beside_ref, far_ref):
    size = own_ref.shape[0]
    back = 3 - 2 * odd_ref[0, 0]
    for out, at, step in (
        (own_ref, 0, 0), (beside_ref, 0, back), (beside_ref, size, 4 - back), (far_ref, 0, 2)
    ):
        rows = pl.ds(pl.multiple_of(step * size, size), size)
        value = one_ref[rows, :].astype(F32) + two_ref[rows, :].astype(F32)
        out[at : at + size, :] = value.astype(out.dtype)


def middle_kernel(base_ref, *refs):
    parts, (gain_ref, sum_ref, scaled_ref) = refs[:-3], refs[-3:]
    for at in range(0, base_ref.shape[0], 32):
        rows = slice(at, at + 32)
        value = base_ref[rows, :].astype(F32)
        for ref in parts:
            value = value + ref[rows, :].astype(F32)
        sum_ref[rows, :] = value
        normed, _ = normed_rows(value.astype(BF))
        scaled_ref[rows, :] = (normed * gain_ref[1:2, :]).astype(BF)


def middle_grad_kernel(base_ref, *refs):
    parts, (middle_ref, gain_ref, sum_ref, low_ref) = refs[:-4], refs[-4:]
    for at in range(0, base_ref.shape[0], 32):
        rows = slice(at, at + 32)
        value = parts[0][rows, :].astype(F32)
        for ref in parts[1:]:
            value = value + ref[rows, :].astype(F32)
        normed, factor = normed_rows(middle_ref[rows, :].astype(BF))
        value = value * gain_ref[1:2, :]
        inner = jnp.mean(value * normed, -1, keepdims=True)
        value = base_ref[rows, :].astype(F32) + factor * (value - normed * inner)
        sum_ref[rows, :] = value
        low_ref[rows, :] = value.astype(BF)


def cotangent_at(odd_ref, n):
    return (0, 3 - 2 * odd_ref[0, 0], 2, 1 + 2 * odd_ref[0, 0])[n % 4]


def hidden_kernel(width, odd_ref, *refs):
    (w_ref, hidden_ref, both_ref, x_ref, c_ref, gate_up_ref, down_ref, sems) = refs[10:]
    first = gate_up_ref.shape[1]
    copies = [
        pltpu.make_async_copy(w_ref.at[:, pl.ds(0, first)], gate_up_ref, sems.at[0]),
        pltpu.make_async_copy(w_ref.at[:, pl.ds(first, down_ref.shape[1])], down_ref, sems.at[1]),
    ]
    count = x_ref.shape[0] // 8
    for n in range(8):
        rows = pl.ds(n * count, count)
        copies.append(pltpu.make_async_copy(refs[n], x_ref.at[rows, :], sems.at[2 + n]))
        at = pl.ds(pl.multiple_of(cotangent_at(odd_ref, n) * count, count), count)
        copies.append(
            pltpu.make_async_copy(refs[8 + n // 4].at[at, :], c_ref.at[rows, :], sems.at[10 + n])
        )
    weights_up, weights_down, *pieces = copies
    xs, cots = pieces[::2], pieces[1::2]
    for copy in (*xs[:4], weights_up, *xs[4:], weights_down, *cots):
        copy.start()

    def units(gate, up, grad):
        sigmoid = 1.0 / (1.0 + jnp.exp(-gate))
        gated = gate * sigmoid
        return (
            (gated * up).astype(BF),
            (grad * up * sigmoid * (1.0 + gate * (1.0 - sigmoid))).astype(BF),
            (grad * gated).astype(BF),
        )

    half = 4 * count
    for part in range(2):
        rows = slice(part * half, (part + 1) * half)
        for copy in xs[4 * part : 4 * part + 4]:
            copy.wait()
        if part == 0:
            weights_up.wait()
        x = x_ref[rows, :]
        gate = mm(x, gate_up_ref[:, :width])
        up = mm(x, gate_up_ref[:, width : 2 * width])
        ends = mm(x, gate_up_ref[:, 2 * width :])
        for copy in cots[4 * part : 4 * part + 4]:
            copy.wait()
        if part == 0:
            weights_down.wait()
        c = c_ref[rows, :]
        value, dgate, dup = units(gate, up, mm(c, down_ref[:, :width]))
        hidden_ref[rows, :width] = value
        both_ref[rows, :width] = dgate
        both_ref[rows, width : 2 * width] = dup
        value, dgate, dup = units(ends[:, :64], ends[:, 64:], mm(c, down_ref[:, width:])[:, :64])
        hidden_ref[rows, width:] = jnp.concatenate([value, jnp.zeros_like(value)], 1)
        both_ref[rows, 2 * width :] = jnp.concatenate([dgate, dup], 1)


def sum_of_products(terms, refs):
    total = None
    for left, (low, high), right, (first, last) in terms:
        part = mm_last(refs[left][:, low:high], refs[right][:, first:last])
        total = part if total is None else total + part
    return total


def rows_grad_kernel(terms, count, gain_row, *refs):
    pieces, gain_ref, outs, sum_ref = refs[count : count + 4], refs[count + 4], refs[count + 5 : -1], refs[-1]
    own_ref, across_ref, cores_ref = outs
    size = own_ref.shape[0]
    outs = [own_ref, cores_ref.at[pl.ds(0, size), :], across_ref, cores_ref.at[pl.ds(size, size), :]]
    step = pl.program_id(0)
    tile = sum_ref.shape[1] // pl.num_programs(0)
    columns = pl.ds(pl.multiple_of(step * tile, tile), tile)
    sum_ref[:, columns] = sum_of_products(terms, refs) * gain_ref[gain_row : gain_row + 1, columns]

    @pl.when(step == pl.num_programs(0) - 1)
    def _():
        for n, ref in enumerate(pieces):
            for at in range(0, ref.shape[0], 32):
                normed, factor = normed_rows(ref[at : at + 32, :])
                scaled = sum_ref[n * ref.shape[0] + at : n * ref.shape[0] + at + 32, :]
                inner = jnp.mean(scaled * normed, -1, keepdims=True)
                outs[n][at : at + 32, :] = (factor * (scaled - normed * inner)).astype(BF)


def rows_out_kernel(terms, places, *refs):
    value = sum_of_products(terms, refs).astype(BF)
    outs = refs[len(refs) - len(places) :]
    size = value.shape[0] // sum(len(held) for held in places)
    for out, held in zip(outs, places):
        for n, piece in enumerate(held):
            out[n * size : (n + 1) * size, :] = value[piece * size : (piece + 1) * size]


def write_parts(outs, turned_of, axis, me, right, base):
    for d, out in enumerate(outs):
        index = (me + d) & 3
        if axis == "z":
            turned = turned_of(pl.multiple_of(index * 512, 512), 512)
        else:
            turned = jnp.concatenate(
                [turned_of(pl.multiple_of(z * 512 + index * 128, 128), 128) for z in range(4)], 0
            )
        out[:, base : base + right.shape[1]] = mm(turned, right).astype(BF)


def parts_kernel(axis, columns, count, me_ref, *refs):
    lefts, right_ref, outs = refs[:count], refs[count], refs[count + 1 :]

    def turned_of(at, size):
        return jnp.concatenate([left[:, pl.ds(at, size)] for left in lefts], 0).T

    write_parts(outs, turned_of, axis, me_ref[0, 0], right_ref[:, columns[0] : columns[1]], 0)


def last_parts_kernel(axis, cut, me_ref, left_ref, dq_ref, own_ref, one_ref, two_ref, three_ref,
                      cos_ref, sin_ref, *outs):
    half = HD // 2
    cos, sin = cos_ref[...], sin_ref[...]
    kv = own_ref[...]
    for ref in (one_ref, two_ref, three_ref):
        kv = kv + ref[...].astype(F32)
    kv = kv.T
    a, b = kv[:half], kv[half:HD]
    kv = jnp.concatenate([a * cos + b * sin, b * cos - a * sin, kv[HD:]], 0).T.astype(BF)
    outs[0][...] = kv
    right = jnp.concatenate([dq_ref[:, cut:], kv], 1)

    def turned_of(at, size):
        return left_ref[:, pl.ds(at, size)].T

    write_parts(outs[1:], turned_of, axis, me_ref[0, 0], right, 0)


def settle_kernel(base_ref, *refs):
    out_ref = refs[-1]
    width = base_ref.shape[1]

    def block(at):
        value = base_ref[:, at : at + 128].astype(F32)
        for ref in refs[:-1]:
            value = value + ref[:, at : at + 128].astype(F32)
        return value

    for n in range(width // 256):
        one, two = block(256 * n), block(256 * n + 128)
        low = jnp.concatenate([one[:, :HD], two[:, :HD]], 1)
        high = jnp.concatenate([one[:, HD:], two[:, HD:]], 1)
        out_ref[:, 128 * n : 128 * n + 128] = low.astype(out_ref.dtype)
        out_ref[:, width // 2 + 128 * n : width // 2 + 128 * n + 128] = high.astype(out_ref.dtype)


def fill_bias(bias_ref, me_ref, pos_ref, span, distances):
    step = 64
    quarter = span // 4
    me = me_ref[0, 0]
    at = lax.broadcasted_iota(jnp.int32, (1, span), 1)
    query = (((at // quarter) ^ me) * quarter) + (at & (quarter - 1))
    first = query - pos_ref[...]

    @pl.loop(0, span // step)
    def _(i):
        block = (i * step) // quarter
        start = (block ^ me) * quarter + i * step - block * quarter
        key = start + lax.broadcasted_iota(jnp.int32, (step, span), 0)
        for n, d in enumerate(distances):
            seen = (key - d * span <= query) & (key - d * span >= first)
            bias_ref[pl.ds(pl.multiple_of(n * span + i * step, step), step), :] = jnp.where(
                seen, 0.0, masked_fill
            ).astype(F32)


def attend_kernel(q_ref, *refs):
    blocks = len(refs) - 7
    kv_refs = refs[:blocks]
    me_ref, pos_ref, mix_ref, lse_ref, bias_ref, s_ref, vt_ref = refs[blocks:]
    span = q_ref.shape[1]
    fill_bias(bias_ref, me_ref, pos_ref, span, range(blocks))
    for d in range(blocks):
        vt_ref[:, d * span : (d + 1) * span] = kv_refs[d][...].T[HD:]

    @pl.loop(0, q_ref.shape[0] // 128)
    def _(pair):
        outs = []
        for sub in range(2):
            q = q_ref[pl.ds(pl.multiple_of(pair * 128 + sub * HD, HD), HD), :]
            top = None
            for d in range(blocks):
                rows = slice(d * span, (d + 1) * span)
                s = mm(kv_refs[d][:, :HD], q) + bias_ref[rows, :]
                s_ref[rows, :] = s
                high = jnp.max(s, 0, keepdims=True)
                top = high if top is None else jnp.maximum(top, high)
            total = jnp.zeros_like(top)
            out = jnp.zeros((HD, span), F32)
            for d in range(blocks):
                rows = slice(d * span, (d + 1) * span)
                p = jnp.exp(s_ref[rows, :] - top)
                total = total + jnp.sum(p, 0, keepdims=True)
                out = out + mm(vt_ref[:, rows], p.astype(BF))
            outs.append(out / total)
            lse_ref[pl.ds(pair * 2 + sub, 1), :] = top + jnp.log(total)
        mix_ref[:, pl.ds(pl.multiple_of(pair * 128, 128), 128)] = (
            jnp.concatenate(outs, 0).T.astype(BF)
        )


def attend_back_kernel(distances, first, last, q_ref, *refs):
    blocks = len(distances)
    refs = list(refs)

    def take(count):
        got, refs[:count] = refs[:count], []
        return got

    kv_refs = take(blocks)
    me_ref, pos_ref, lse_ref = take(3)
    if first:
        mix_ref, w_ref, *piece_refs = take(6)
    else:
        gt_ref, delta_ref, part_ref = take(3)
    if last:
        cos_ref, sin_ref = take(2)
        (dq_ref,) = take(1)
    else:
        (sum_ref,) = take(1)
    (dkv_ref,) = take(1)
    if first:
        gt_ref, delta_ref = take(2)
    bias_ref, v_ref, kt_ref, dk_ref, dv_ref = take(5)
    span = q_ref.shape[1]
    half = HD // 2
    heads = q_ref.shape[0] // HD
    fill_bias(bias_ref, me_ref, pos_ref, span, distances)
    for n in range(blocks):
        rows = slice(n * span, (n + 1) * span)
        both = kv_refs[n][...].T
        kt_ref[:, rows] = both[:HD]
        v_ref[rows, :] = both[HD:].T
    dk_ref[...] = jnp.zeros_like(dk_ref)
    dv_ref[...] = jnp.zeros_like(dv_ref)
    if first:
        rows_all = jnp.concatenate([ref[...] for ref in piece_refs], 0)
        for at in range(0, heads * HD, 256):
            grads = mm(rows_all, w_ref[:, heads * HD + at : heads * HD + at + 256]).astype(BF).T
            gt_ref[at : at + 256, :] = grads
        for at in range(0, heads * HD, 128):
            gt = gt_ref[at : at + 128, :]
            mt = mix_ref[:, at : at + 128].T
            prod = gt.astype(F32) * mt.astype(F32)
            for sub in range(2):
                h = at // HD + sub
                delta_ref[h : h + 1, :] = jnp.sum(prod[sub * HD : (sub + 1) * HD], 0, keepdims=True)

    @pl.loop(0, heads // 2)
    def _(pair):
        outs = []
        for sub in range(2):
            rows_h = pl.ds(pl.multiple_of(pair * 128 + sub * HD, HD), HD)
            q, g = q_ref[rows_h, :], gt_ref[rows_h, :]
            lse = lse_ref[pl.ds(pair * 2 + sub, 1), :]
            delta = delta_ref[pl.ds(pair * 2 + sub, 1), :]
            dq = jnp.zeros((HD, span), F32) if first else part_ref[rows_h, :]
            for n in range(blocks):
                rows = slice(n * span, (n + 1) * span)
                s = mm(kv_refs[n][:, :HD], q) + bias_ref[rows, :]
                p = jnp.exp(s - lse)
                ds = (p * (mm(v_ref[rows, :], g) - delta)).astype(BF)
                dv_ref[rows, :] += mm_last(p.astype(BF), g)
                dk_ref[rows, :] += mm_last(ds, q)
                dq = dq + mm(kt_ref[:, rows], ds)
            if last:
                dq = dq * 0.125
                a, b = dq[:half], dq[half:]
                cos, sin = cos_ref[...], sin_ref[...]
                outs += [a * cos + b * sin, b * cos - a * sin]
            else:
                sum_ref[rows_h, :] = dq
        if last:
            dq_ref[:, pl.ds(pl.multiple_of(pair * 128, 128), 128)] = (
                jnp.concatenate(outs, 0).T.astype(BF)
            )

    for n in range(blocks):
        rows = slice(n * span, (n + 1) * span)
        dkv_ref[rows, :] = jnp.concatenate([dk_ref[rows, :], dv_ref[rows, :]], 1).astype(dkv_ref.dtype)


def weight_grads_kernel(odd_ref, *refs):
    one_ref, two_ref, out_ref = refs[10:]
    count = refs[0].shape[0]

    def cotangent(n):
        at = pl.multiple_of(cotangent_at(odd_ref, n) * count, count)
        return refs[8 + n // 4][pl.ds(at, count), :]

    at = 0
    for lefts, ref in (
        ([left[...] for left in refs[:8]], one_ref), ([cotangent(n) for n in range(8)], two_ref)
    ):
        turned = jnp.concatenate(lefts, 0).T
        for c in range(0, ref.shape[1], 256):
            size = min(256, ref.shape[1] - c)
            out_ref[:, at + c : at + c + size] = mm(turned, ref[:, c : c + size]).astype(BF)
        at += ref.shape[1]


def params(mib):
    return pltpu.CompilerParams(vmem_limit_bytes=mib * MIB)


def whole(count):
    return [pl.BlockSpec(memory_space=pltpu.VMEM)] * count


def cost(products, moved):
    return pl.CostEstimate(flops=2 * products, bytes_accessed=moved, transcendentals=0)


def call(kernel, name, shapes, operands, scalars=0, products=0, mib=16):
    return pl.pallas_call(
        kernel,
        out_shape=tuple(jax.ShapeDtypeStruct(*shape) for shape in shapes),
        in_specs=scalar() * scalars + whole(len(operands) - scalars),
        out_specs=tuple(whole(len(shapes))),
        compiler_params=params(mib),
        cost_estimate=cost(products, 4 << 20),
        name=name,
    )(*operands)


def hidden_units(odd, pieces, cots, weights, width):
    count, d = pieces[0].shape
    span = 8 * count
    both, down = 2 * width + 128, width + 128
    return pl.pallas_call(
        functools.partial(hidden_kernel, width),
        out_shape=(jax.ShapeDtypeStruct((span, down), BF), jax.ShapeDtypeStruct((span, both), BF)),
        in_specs=scalar() + [pl.BlockSpec(memory_space=pl.ANY)] * 11,
        out_specs=tuple(whole(2)),
        scratch_shapes=[
            pltpu.VMEM((span, d), BF),
            pltpu.VMEM((span, d), BF),
            pltpu.VMEM((d, both), BF),
            pltpu.VMEM((d, down), BF),
            pltpu.SemaphoreType.DMA((18,)),
        ],
        compiler_params=params(56),
        cost_estimate=cost(3 * span * d * width, 6 * d * width),
        name="hidden_units",
    )(odd, *pieces, *cots, weights)


def feature_rows(weight, tile):
    if not isinstance(weight, tuple):
        return pl.BlockSpec((tile, weight.shape[1]), lambda i: (i, 0))
    return pl.BlockSpec((pl.Element(tile), pl.Element(weight[2])), lambda i: (i * tile, weight[1]))


def array_of(weight):
    return weight[0] if isinstance(weight, tuple) else weight


def fixed(array):
    return pl.BlockSpec(array.shape, lambda i: (0, 0))


def rows_grad(grads, weights, terms, pieces, gains, gain_row):
    span, d = 4 * pieces[0].shape[0], pieces[0].shape[1]
    tile = 512
    n = len(grads)
    terms = [(g, c, n + w, e) for g, c, w, e in terms]
    return pl.pallas_call(
        functools.partial(rows_grad_kernel, terms, n + len(weights), gain_row),
        grid=(d // tile,),
        out_shape=tuple(jax.ShapeDtypeStruct((span // n, d), BF) for n in (4, 4, 2)),
        in_specs=[fixed(g) for g in grads]
        + [feature_rows(w, tile) for w in weights]
        + [fixed(a) for a in (*pieces, gains)],
        out_specs=tuple(pl.BlockSpec((span // n, d), lambda i: (0, 0)) for n in (4, 4, 2)),
        scratch_shapes=[pltpu.VMEM((span, d), F32)],
        compiler_params=params(32),
        cost_estimate=cost(0, 0),
        name="rows_grad",
    )(*grads, *map(array_of, weights), *pieces, gains)


def rows_out(lefts, weights, terms, tile, places, mib):
    span, d = lefts[0].shape[0], array_of(weights[0]).shape[0]
    n = len(lefts)
    terms = [(g, c, n + w, e) for g, c, w, e in terms]
    size = span // sum(len(held) for held in places)
    return pl.pallas_call(
        functools.partial(rows_out_kernel, terms, places),
        grid=(d // tile,),
        out_shape=tuple(jax.ShapeDtypeStruct((len(held) * size, d), BF) for held in places),
        in_specs=[fixed(g) for g in lefts] + [feature_rows(w, tile) for w in weights],
        out_specs=tuple(pl.BlockSpec((len(held) * size, tile), lambda i: (0, i)) for held in places),
        compiler_params=params(mib),
        cost_estimate=cost(sum(span * d * (c[1] - c[0]) for _, c, _, _ in terms), 6 << 20),
        name="rows_out",
    )(*lefts, *map(array_of, weights))


def scalar():
    return [pl.BlockSpec(memory_space=pltpu.SMEM)]


def at_place(axis):
    return place(axis).astype(jnp.int32).reshape(1, 1)


def wide_parts(lefts, right, columns, axis):
    span, d = right.shape[0], lefts[0].shape[1]
    width = columns[1] - columns[0]
    return pl.pallas_call(
        functools.partial(parts_kernel, axis, columns, len(lefts)),
        out_shape=(jax.ShapeDtypeStruct((d // 4, width), BF),) * 4,
        in_specs=scalar() + whole(len(lefts) + 1),
        out_specs=tuple(whole(4)),
        compiler_params=params(20),
        cost_estimate=cost(span * d * width, 8 << 20),
        name="wide_parts",
    )(at_place(axis), *lefts, right)


def last_parts(left, dq, cut, own, arrived, cos, sin, axis):
    span, d = left.shape
    width = dq.shape[1] - cut + 2 * HD
    return pl.pallas_call(
        functools.partial(last_parts_kernel, axis, cut),
        out_shape=(jax.ShapeDtypeStruct((span, 2 * HD), BF),)
        + (jax.ShapeDtypeStruct((d // 4, width), BF),) * 4,
        in_specs=scalar() + whole(8),
        out_specs=tuple(whole(5)),
        compiler_params=params(20),
        cost_estimate=cost(0, 0),
        name="last_parts",
    )(at_place(axis), left, dq, own, *arrived, cos, sin)


def settle(base, parts, kind):
    return pl.pallas_call(
        settle_kernel,
        out_shape=jax.ShapeDtypeStruct(base.shape, kind),
        in_specs=whole(1 + len(parts)),
        out_specs=whole(1)[0],
        compiler_params=params(12),
        cost_estimate=cost(0, 4 << 20),
        name="settle",
    )(base, *parts)


def window_specs():
    return [pl.BlockSpec(memory_space=pltpu.SMEM)] + whole(1)


def attend(q, kvs, window):
    n = len(kvs)
    width, span = q.shape
    heads = width // HD
    return pl.pallas_call(
        attend_kernel,
        out_shape=(
            jax.ShapeDtypeStruct((span, width), BF),
            jax.ShapeDtypeStruct((heads, span), F32),
        ),
        in_specs=whole(n + 1) + window_specs(),
        out_specs=tuple(whole(2)),
        scratch_shapes=[
            pltpu.VMEM((n * span, span), F32),
            pltpu.VMEM((n * span, span), F32),
            pltpu.VMEM((HD, n * span), BF),
        ],
        compiler_params=params(32),
        cost_estimate=cost(30 * 580_000_000, 2 << 20),
        name="attend",
    )(q, *kvs, *window)


def attend_back(distances, q, kvs, window, lse, prepared, mixed=None, out=None, turn=None):
    n = len(kvs)
    width, span = q.shape
    heads = width // HD
    first, last = prepared is None, turn is not None
    operands = [q, *kvs, *window, lse]
    operands += [mixed, *out] if first else list(prepared)
    shapes = []
    if last:
        operands += turn
        shapes.append(jax.ShapeDtypeStruct((span, width), BF))
    else:
        shapes.append(jax.ShapeDtypeStruct((width, span), F32))
    shapes.append(jax.ShapeDtypeStruct((n * span, 2 * HD), F32 if last else BF))
    if first:
        shapes.append(jax.ShapeDtypeStruct((width, span), BF))
        shapes.append(jax.ShapeDtypeStruct((heads, span), F32))
    specs = whole(n + 1) + window_specs() + whole(len(operands) - n - 3)
    return pl.pallas_call(
        functools.partial(attend_back_kernel, distances, first, last),
        out_shape=tuple(shapes),
        in_specs=specs,
        out_specs=tuple(whole(len(shapes))),
        scratch_shapes=[
            pltpu.VMEM((n * span, span), F32),
            pltpu.VMEM((n * span, HD), BF),
            pltpu.VMEM((HD, n * span), BF),
            pltpu.VMEM((n * span, HD), F32),
            pltpu.VMEM((n * span, HD), F32),
        ],
        compiler_params=params(40),
        cost_estimate=cost(1000 * 580_000_000 if first else 0, 1 << 20),
        name="attend_back",
    )(*operands)


def weight_grads(odd, xs, cots, one, two):
    t, d = xs[0].shape
    tile = 256
    rows = pl.BlockSpec((t, tile), lambda i: (0, i))
    width = one.shape[1] + two.shape[1]
    return pl.pallas_call(
        weight_grads_kernel,
        grid=(d // tile,),
        out_shape=jax.ShapeDtypeStruct((d, width), BF),
        in_specs=scalar()
        + [rows] * 8
        + [pl.BlockSpec((4 * t, tile), lambda i: (0, i))] * 2
        + [fixed(one), fixed(two)],
        out_specs=pl.BlockSpec((tile, width), lambda i: (i, 0)),
        compiler_params=params(56),
        cost_estimate=cost(8 * t * d * width, 2 * d * width + 32 * t * d),
        name="weight_grads",
    )(odd, *xs, *cots, one, two)


def per_device(
    inputs,
    positions,
    attn_gain,
    query_weight,
    key_weight,
    value_weight,
    out_weight,
    mlp_gain,
    gate_weight,
    up_weight,
    down_weight,
    cotangent,
):
    width_q = query_weight.shape[1]
    width_k = key_weight.shape[1]
    hidden_width = gate_weight.shape[1]
    span = positions.shape[0]
    quarter = span // 4
    cut = 3 * width_q // 4
    d = inputs.shape[1]
    shard = query_weight.shape[0]
    side = place("yh").astype(jnp.int32).reshape(1, 1)

    units = 128 * (hidden_width // 256)
    both_width, down_width = 2 * units + 128, units + 128
    inputs, cotangent, shard_kv, shard_mlp = call(
        pack_kernel, "pack",
        [(inputs.shape, BF), (inputs.shape, BF), ((shard, 256), BF),
         ((2, shard, both_width + down_width), BF)],
        [inputs, cotangent, attn_gain[None], mlp_gain[None], key_weight, value_weight,
         gate_weight, up_weight, down_weight.T],
        mib=56,
    )
    shard_first = jnp.concatenate([query_weight, out_weight.T], 1)
    other_first, other_kv = swap(shard_first, "yh"), swap(shard_kv, "yh")
    pair_first = join_sides(shard_first, after(other_first, shard_kv))
    first_whole = lax.all_gather(pair_first, ("z", "x"), axis=0, tiled=True)
    pair_kv = join_sides(shard_kv, other_kv)
    along_kv = send_stage(pair_kv, "x")
    rows_in = gather_rows(after(inputs, other_kv))
    kv_whole = flat(stack_stage(send_stage(stack_stage(along_kv, "x", 0), "z"), "z", 0))

    me = (lax.axis_index("yl") * 2 + lax.axis_index("core")).astype(jnp.int32)
    blocked = jnp.arange(4, dtype=jnp.int32) ^ me
    positions = jnp.take(positions.reshape(4, quarter), blocked, axis=0, mode="clip").reshape(1, span)
    freqs = 10000.0 ** (-(jnp.arange(HD // 2, dtype=F32) * 2.0) / HD)
    angles = freqs[:, None] * positions.astype(F32)
    cos, sin = jnp.cos(angles), jnp.sin(angles)
    window = (me.reshape(1, 1), positions)

    kv_block, scaled_in, gains = call(
        keys_values_kernel, "keys_values",
        [((span, 2 * width_k), BF), ((span, d), BF), ((8, d), F32)],
        [*rows_in, kv_whole, cos, sin], products=span * d * 2 * width_k,
    )
    (queries,) = call(
        queries_kernel, "queries",
        [((width_q, span), BF)],
        [scaled_in, after(first_whole, kv_block), cos, sin], products=span * d * width_q,
    )
    blocks = [kv_block] + [shift(kv_block, "x", d) for d in range(1, SEQ_DEVS)]
    cot_yl = swap(after(cotangent, kv_block), "yl")
    cot_near = jnp.concatenate([cotangent, cot_yl], 0)
    cot_far = swap(cot_near, "yh")
    other_mlp = swap(after(pick(shard_mlp, place("yh", 1), 0), kv_block), "yh")
    mlp_pair = join_sides(pick(shard_mlp, place("yh"), 0), after(other_mlp, first_whole, blocks[1:], cot_yl))
    mlp_whole = lax.all_gather(mlp_pair, ("z", "x"), axis=0, tiled=True)
    odd = place("yl").astype(jnp.int32).reshape(1, 1)
    mixed, log_total = attend(queries, blocks, window)

    cotangents = jnp.concatenate([cot_near, after(cot_far, log_total)], 0)
    all_heads = (0, width_q)
    attn_rows = rows_out(
        [after(mixed, cotangents)], [(first_whole, width_q, width_q)], [(0, all_heads, 0, all_heads)],
        1024, [(0,), (2,), (1, 3)], 24,
    )
    cotangents = [cotangents, swap(cotangents, "core")]
    middle, scaled_mid = call(
        middle_kernel, "middle", [(inputs.shape, F32), (inputs.shape, BF)],
        [inputs, *scatter_rows(attn_rows), gains],
    )
    scaled_all = gather_eight(scaled_mid)
    hidden, grad_both = hidden_units(odd, scaled_all, cotangents, mlp_whole, units)
    mid_partial = rows_out(
        [grad_both], [(mlp_whole, 0, both_width)], [(0, (0, both_width), 0, (0, both_width))], 512, [(0, 1, 2, 3), (4, 5, 6, 7)], 56,
    )
    mid_own, mid_others = scatter_eight(*mid_partial)
    mid_arrived = send_back(mid_others)
    mlp_sum = weight_grads(
        odd, [after(scaled_all[0], mid_others), *scaled_all[1:]], cotangents, grad_both, hidden
    )
    mlp_rows = rows_out(
        [after(hidden, mlp_sum)], [(mlp_whole, both_width, down_width)],
        [(0, (0, down_width), 0, (0, down_width))], 512, [(0, 1, 2, 3), (4, 5, 6, 7)], 56,
    )
    grad_middle, grad_middle_low = call(
        middle_grad_kernel, "middle_grad", [(inputs.shape, F32), (inputs.shape, BF)],
        [cotangent, mid_own, *after(mid_arrived, mlp_rows), middle, gains],
    )
    rows_grad_middle = gather_rows(grad_middle_low)
    mlp_sum = lax.psum_scatter(mlp_sum, ("z", "x"), scatter_dimension=0, tiled=True)

    out_parts = wide_parts(rows_grad_middle, mixed, (0, width_q), "z")
    mlp_cores = swap(after(mlp_rows[1], grad_middle_low), "core")
    mlp_own, mlp_beside, mlp_far = call(
        pair_pieces_kernel, "pair_pieces",
        [(inputs.shape, F32), ((2 * quarter, d), BF), (inputs.shape, BF)],
        [odd, mlp_rows[0], mlp_cores], scalars=1,
    )
    query_part, far_grads, grad_turned, delta = attend_back(
        (1, 2, 3), queries, blocks[1:], window, log_total, None, after(mixed, out_parts, mlp_beside),
        [first_whole, *rows_grad_middle],
    )
    mlp_arrived = after(swap(after(mlp_beside, rows_grad_middle), "yl"), query_part)
    mlp_far = (mlp_far.astype(F32) + mlp_arrived[quarter:].astype(F32)).astype(BF)
    arriving = [
        shift(far_grads[(d - 1) * span : d * span], "x", -d) for d in range(1, SEQ_DEVS)
    ]
    out_arrived = [after(shift(out_parts[n], "z", n), query_part) for n in (1, 2, 3)]
    query_raw_grad, own_grads = attend_back(
        (0,), after(queries, mlp_far, out_arrived), blocks[:1], window, log_total, (grad_turned, delta, query_part), turn=[cos, sin]
    )

    out_sum = total(out_parts[0].astype(F32), out_arrived).astype(BF)
    output = settle(
        middle, [mlp_own, mlp_arrived[:quarter], after(swap(mlp_far, "yh"), query_raw_grad)], BF
    )
    a_parts = wide_parts([scaled_in], after(query_raw_grad, arriving), (0, cut), "x")
    a_arrived = [shift(a_parts[n], "x", n) for n in (2, 1, 3)]
    kv_raw_grad, *b_parts = last_parts(
        scaled_in, after(query_raw_grad, a_parts), cut, own_grads, arriving, cos, sin, "z"
    )
    b_arrived = [shift(b_parts[n], "z", n) for n in (2, 1, 3)]
    in_partial = rows_grad(
        [query_raw_grad, kv_raw_grad],
        [(first_whole, 0, width_q), kv_whole],
        [(0, all_heads, 0, all_heads), (1, (0, 2 * width_k), 1, (0, 2 * width_k))],
        rows_in, gains, 0,
    )
    in_own, in_across, in_cores = in_partial
    in_parts = scatter_rows((in_own, in_across, after(in_cores, a_arrived, b_arrived)))
    input_grad = settle(grad_middle, in_parts, F32)

    mlp_send = pick(mlp_sum.reshape(2, shard, -1), place("yh", 1), 0)
    a_sum = wide_sum_next(total(a_parts[0].astype(F32), a_arrived).astype(BF), "z")
    b_sum = total(b_parts[0].astype(F32), b_arrived).astype(BF)
    b_sum = wide_sum_next(jnp.concatenate([b_sum, out_sum], 1), "x", hold=[mlp_send])
    sides = jnp.concatenate([a_sum, b_sum], 1)
    other_sides = swap(pick(sides.reshape(2, shard, -1), place("yh", 1), 0), "yh")
    query_grad, key_grad, value_grad, out_grad = call(
        finish_attn_kernel, "finish_attn",
        [(query_weight.shape, F32), (key_weight.shape, F32), (value_weight.shape, F32),
         (out_weight.shape[::-1], F32)],
        [side, sides, other_sides], scalars=1,
    )
    gate_grad, up_grad, down_grad = call(
        finish_mlp_kernel, "finish_mlp",
        [(gate_weight.shape, F32), (up_weight.shape, F32), (down_weight.shape[::-1], F32)],
        [side, mlp_sum, swap(mlp_send, "yh")], scalars=1,
    )

    ends = width_q - cut
    attn_weights = jnp.concatenate([pair_first[:, :width_q], pair_kv[:, : 2 * width_k]], 1).astype(F32)
    gain_parts = jnp.stack(
        [
            jnp.sum(attn_weights * sides[:, : cut + ends + 2 * width_k].astype(F32), 1),
            jnp.sum(
                mlp_pair[:, :both_width].astype(F32) * mlp_sum[:, :both_width].astype(F32),
                1,
            ),
        ]
    )
    gain_parts = lax.psum(gain_parts, ("yh",) + TP)
    own_gains = pick(gain_parts.reshape(2, 2, shard), place("yh"), 1)
    return (
        output,
        input_grad,
        own_gains[0] / attn_gain.astype(F32),
        query_grad,
        key_grad,
        value_grad,
        out_grad.T,
        own_gains[1] / mlp_gain.astype(F32),
        gate_grad,
        up_grad,
        down_grad.T,
    )


def solution(mesh):
    split = Mesh(mesh.devices.reshape(2, 4, 4, 2, 2), WIDE + TP)
    rows = P(WIDE + TP, None)
    inward = P(WIDE, TP)
    outward = P(TP, WIDE)
    gain = P(WIDE)
    return jax.shard_map(
        per_device,
        mesh=split,
        in_specs=(
            rows, gain, gain, inward, inward, inward, outward, gain, inward, inward, outward, rows,
        ),
        out_specs=(
            rows, rows, gain, inward, inward, inward, outward, gain, inward, inward, outward,
        ),
        check_vma=False,
    )
```

profile of v0, /device:TPU:1, one launch (start us, length us, event | category | flops | bytes accessed | tf_op | source)
XLA Modules:
  0.0 409.9 jit_solution(5058007531257917182)
XLA Ops:
  8.1 3.8 collective-permute-start.10
  11.9 2.8 pack.1
  16.7 3.0 collective-permute-start
  22.1 2.6 collective-permute-start.5
  24.6 1.7 collective-permute-start.6
  27.7 2.0 collective-permute-done.4
  29.7 1.7 collective-permute-start.7
  31.8 4.5 %collective-permute-start.1 = (bf16[128,2048]{1,0:T(8,128)(2,1)S(1)}, bf16[128,2048]{1,0:T(8,128)(2,1)S(1)}, u32[]{:S(2)}, u32[]{:S(2)}) collective-permute-start(bf16[128,2048]{1,0:T(8,128)(2,1)S(1)} %copy-done.7), channel_id=1, source_target_pairs={{0,1},{1,0},{2,3},{3,2},{4,5},{5,4},{6,7},{7,6},{8,9},{9,8},{10,11... | collective-permute-start | bytes 1572872 | tf_op jit(solution)/shard_map/ppermute | solution.py:31
  36.2 4.0 collective-permute-start.9
  41.2 11.6 %collective-permute-done.8 = bf16[4,128,256]{2,1,0:T(8,128)(2,1)S(1)} collective-permute-done((bf16[4,128,256]{2,1,0:T(8,128)(2,1)S(1)}, bf16[4,128,256]{2,1,0:T(8,128)(2,1)S(1)}, u32[]{:S(2)}, u32[]{:S(2)}) %collective-permute-start.8) | collective-permute-done | bytes 262176 | tf_op jit(solution)/shard_map/ppermute | solution.py:31
  58.7 2.7 collective-permute-start.26
  61.4 2.2 collective-permute-start.13
  64.2 4.7 %collective-permute-done.13.refs_3_.refs_2_ = bf16[512,128]{1,0:T(8,128)(2,1)} collective-permute-done((bf16[512,128]{1,0:T(8,128)(2,1)S(1)}, bf16[512,128]{1,0:T(8,128)(2,1)}, u32[]{:S(2)}, u32[]{:S(2)}) %collective-permute-start.13) | collective-permute-done | bytes 131104 | tf_op jit(solution)/shard_map/ppermute | solution.py:31
  68.9 3.9 collective-permute-done.12.refs_2_.refs_1_
  72.8 2.8 collective-permute-done.11.refs_1_.refs_0_
  75.5 2.5 collective-permute-done.26
  78.0 4.0 all-gather.3.cloned.1.call-done.w_ref.refs_1_.refs_7_.refs_2_
  85.7 1.8 pad_maximum_fusion
  87.5 3.4 collective-permute-start.15
  90.9 1.9 constant_dynamic-update-slice_fusion.1
  94.2 17.5 %attend.1 = (bf16[512,512]{1,0:T(8,128)(2,1)S(1)}, f32[8,512]{1,0:T(8,128)S(1)}) custom-call(bf16[512,512]{1,0:T(8,128)(2,1)S(1)} %queries.1.q_ref, bf16[512,128]{1,0:T(8,128)(2,1)S(1)} %get-tuple-element.102.refs_0_, bf16[512,128]{1,0:T(8,128)(2,1)} %collective-permute-done.11.refs_1_.refs_0_, bf16[512,128]{1,0:T(8,128)(2,1)} %collective-permute-done.12.refs_2_.refs_1_, ...), custom_call_target="tpu_custom_call" | custom-call | flops 34800001024 | bytes 2097152 | tf_op jit(solution)/shard_map/attend/pallas_call | solution.py:736
  114.1 1.8 rows_out.3
  115.9 2.1 collective-permute-start.16
  118.0 2.8 collective-permute-done.16
  122.4 11.9 %collective-permute-done.17.refs_2_ = bf16[128,2048]{1,0:T(8,128)(2,1)S(1)} collective-permute-done((bf16[128,2048]{1,0:T(8,128)(2,1)S(1)}, bf16[128,2048]{1,0:T(8,128)(2,1)S(1)}, u32[]{:S(2)}, u32[]{:S(2)}) %collective-permute-start.17) | collective-permute-done | bytes 524320 | tf_op jit(solution)/shard_map/ppermute | solution.py:31
  136.4 2.8 collective-permute-start.20
  140.3 1.9 collective-permute-start.21
  142.2 8.6 %collective-permute-done.20.refs_3_ = bf16[128,2048]{1,0:T(8,128)(2,1)} collective-permute-done((bf16[128,2048]{1,0:T(8,128)(2,1)}, bf16[128,2048]{1,0:T(8,128)(2,1)}, u32[]{:S(2)}, u32[]{:S(2)}) %collective-permute-start.20) | collective-permute-done | bytes 524320 | tf_op jit(solution)/shard_map/ppermute | solution.py:31
  150.8 12.2 %collective-permute-start.24 = (bf16[128,2048]{1,0:T(8,128)(2,1)}, bf16[128,2048]{1,0:T(8,128)(2,1)}, u32[]{:S(2)}, u32[]{:S(2)}) collective-permute-start(bf16[128,2048]{1,0:T(8,128)(2,1)} %collective-permute-done.20.refs_3_), channel_id=1, source_target_pairs={{0,1},{1,0},{2,3},{3,2},{4,5},{5,4},{6,7},{7,6},{8,9},{9,8},{10,11... | collective-permute-start | bytes 1572872 | tf_op jit(solution)/shard_map/ppermute | solution.py:31
  162.9 3.2 collective-permute-done.18.refs_1_
  167.0 1.9 collective-permute-done.22.refs_5_
  168.9 20.1 %hidden_units.1 = (bf16[1024,768]{1,0:T(8,128)(2,1)}, bf16[1024,1408]{1,0:T(8,128)(2,1)}) custom-call(s32[1,1]{1,0:T(1,128)} %bitcast.18.odd_ref, bf16[128,2048]{1,0:T(8,128)(2,1)} %get-tuple-element.126.refs_0_, bf16[128,2048]{1,0:T(8,128)(2,1)} %collective-permute-done.18.refs_1_, bf16[128,2048]{1,0:T(8,128)(2,1)} %collective-permute-done.19.refs_2_, ...), custom_call_target="tpu_custom_call" | custom-call | flops 8053063680 | bytes 7864320 | tf_op jit(solution)/shard_map/hidden_units/pallas_call | solution.py:610
  189.0 10.5 %rows_out.4 = (bf16[512,2048]{1,0:T(8,128)(2,1)}, bf16[512,2048]{1,0:T(8,128)(2,1)}) custom-call(bf16[1024,1408]{1,0:T(8,128)(2,1)} %get-tuple-element.120.refs_0_.refs_10_, bf16[2048,2176]{1,0:T(8,128)(2,1)} %all-gather.5.cloned.1.call-done.refs_10_.refs_1_), custom_call_target="tpu_custom_call" | custom-call | flops 5905580032 | bytes 6291456 | tf_op jit(solution)/shard_map/rows_out/pallas_call | solution.py:667
  200.0 4.0 collective-permute-done.27.two_ref
  209.5 16.2 %weight_grads.1 = bf16[2048,2176]{1,0:T(8,128)(2,1)} custom-call(s32[1,1]{1,0:T(1,128)} %bitcast.18.odd_ref, bf16[128,2048]{1,0:T(8,128)(2,1)} %get-tuple-element.126.refs_0_, bf16[128,2048]{1,0:T(8,128)(2,1)} %collective-permute-done.18.refs_1_, bf16[128,2048]{1,0:T(8,128)(2,1)} %collective-permute-done.19.refs_2_, ...), custom_call_target="tpu_custom_call" | custom-call | flops 9126805504 | bytes 17301504 | tf_op jit(solution)/shard_map/weight_grads/pallas_call | solution.py:796
  225.8 7.2 %rows_out.5 = (bf16[512,2048]{1,0:T(8,128)(2,1)}, bf16[512,2048]{1,0:T(8,128)(2,1)}) custom-call(bf16[1024,768]{1,0:T(8,128)(2,1)} %get-tuple-element.127.refs_11_.refs_0_, bf16[2048,2176]{1,0:T(8,128)(2,1)} %all-gather.5.cloned.1.call-done.refs_10_.refs_1_), custom_call_target="tpu_custom_call" | custom-call | flops 3221225472 | bytes 6291456 | tf_op jit(solution)/shard_map/rows_out/pallas_call | solution.py:667
  233.0 2.8 collective-permute-done.29.refs_2_
  235.8 2.9 middle_grad.1
  240.4 13.5 %collective-permute-done.33.refs_2_.refs_10_ = bf16[128,2048]{1,0:T(8,128)(2,1)S(1)} collective-permute-done((bf16[128,2048]{1,0:T(8,128)(2,1)}, bf16[128,2048]{1,0:T(8,128)(2,1)S(1)}, u32[]{:S(2)}, u32[]{:S(2)}) %collective-permute-start.33) | collective-permute-done | bytes 524320 | tf_op jit(solution)/shard_map/ppermute | solution.py:31
  254.8 1.6 collective-permute-done.34.refs_3_.refs_11_
  258.5 3.6 wide_parts.2
  263.3 2.6 collective-permute-start.38
  267.0 3.2 pair_pieces.1
  271.4 20.5 %attend_back.2 = (f32[512,512]{1,0:T(8,128)S(1)}, bf16[1536,128]{1,0:T(8,128)(2,1)S(1)}, bf16[512,512]{1,0:T(8,128)(2,1)S(1)}, f32[8,512]{1,0:T(8,128)S(1)}) custom-call(bf16[512,512]{1,0:T(8,128)(2,1)S(1)} %copy-done.15, bf16[512,128]{1,0:T(8,128)(2,1)} %collective-permute-done.11.refs_1_.refs_0_, bf16[512,128]{1,0:T(8,128)(2,1)} %collective-permute-done.12.refs_2_.refs_1_, ...), custom_call_target="tpu_custom_call" | custom-call | flops 1160000045056 | bytes 1048576 | tf_op jit(solution)/shard_map/attend_back/pallas_call | solution.py:773
  291.9 8.0 %collective-permute-done.39 = bf16[512,512]{1,0:T(8,128)(2,1)} collective-permute-done((bf16[512,512]{1,0:T(8,128)(2,1)}, bf16[512,512]{1,0:T(8,128)(2,1)}, u32[]{:S(2)}, u32[]{:S(2)}) %collective-permute-start.39) | collective-permute-done | bytes 524320 | tf_op jit(solution)/shard_map/ppermute | solution.py:31
  299.9 2.9 collective-permute-done.38
  302.8 1.8 collective-permute-start.42
  305.5 2.0 collective-permute-start.40
  307.5 2.0 add_convert_fusion.2
  309.5 6.7 %attend_back.3 = (bf16[512,512]{1,0:T(8,128)(2,1)S(1)}, f32[512,128]{1,0:T(8,128)S(1)}) custom-call(bf16[512,512]{1,0:T(8,128)(2,1)S(1)} %copy-done.15, bf16[512,128]{1,0:T(8,128)(2,1)S(1)} %get-tuple-element.102.refs_0_, s32[1,1]{1,0:T(1,128)} %bitcast.16.refs_4_.refs_3_.refs_1_, s32[1,512]{1,0:T(1,128)S(1)} %bitcast.82, ...), custom_call_target="tpu_custom_call" | custom-call | bytes 1048576 | tf_op jit(solution)/shard_map/attend_back/pallas_call | solution.py:773
  322.1 2.8 collective-permute-start.43
  324.9 1.6 collective-permute-start.45
  326.5 9.0 %collective-permute-done.46 = bf16[512,256]{1,0:T(8,128)(2,1)S(1)} collective-permute-done((bf16[512,256]{1,0:T(8,128)(2,1)S(1)}, bf16[512,256]{1,0:T(8,128)(2,1)S(1)}, u32[]{:S(2)}, u32[]{:S(2)}) %collective-permute-start.46) | collective-permute-done | bytes 262176 | tf_op jit(solution)/shard_map/ppermute | solution.py:31
  335.9 5.0 %rows_grad.1 = (bf16[128,2048]{1,0:T(8,128)(2,1)S(1)}, bf16[128,2048]{1,0:T(8,128)(2,1)S(1)}, bf16[256,2048]{1,0:T(8,128)(2,1)}) custom-call(bf16[512,512]{1,0:T(8,128)(2,1)S(1)} %get-tuple-element.162.refs_1_.dq_ref.refs_0_, bf16[512,128]{1,0:T(8,128)(2,1)S(1)} %get-tuple-element.164.refs_1_, bf16[2048,1024]{1,0:T(8,128)(2,1)S(1)} %copy-done.3, ...), custom_call_target="tpu_custom_call" | custom-call | tf_op jit(solution)/shard_map/rows_grad/pallas_call | solution.py:647
  340.9 1.9 collective-permute-done.47
  342.9 6.6 %collective-permute-done.43 = bf16[512,384]{1,0:T(8,128)(2,1)S(1)} collective-permute-done((bf16[512,384]{1,0:T(8,128)(2,1)S(1)}, bf16[512,384]{1,0:T(8,128)(2,1)S(1)}, u32[]{:S(2)}, u32[]{:S(2)}) %collective-permute-start.43) | collective-permute-done | bytes 393248 | tf_op jit(solution)/shard_map/ppermute | solution.py:31
  351.9 1.7 add_convert_fusion
  354.7 2.2 collective-permute-start.36
  361.5 2.0 collective-permute-start.52
  365.4 3.4 collective-permute-start.54
  370.2 2.5 collective-permute-start.56
  376.4 3.4 collective-permute-done.50.refs_2_
  382.3 2.6 collective-permute-start.58
  387.1 13.6 %psum.7 = f32[2,2,64]{2,1,0:T(2,128)S(1)} all-reduce(f32[2,2,64]{2,1,0:T(2,128)S(1)} %reshape.102), channel_id=1, replica_groups=mesh['yh'=2,'z'=4,'x'=4,'yl'=2,'core'=2] {'yh','yl','core'}, use_global_device_ids=true, to_apply=%region_3.4 | all-reduce | flops 256 | bytes 2048 | tf_op jit(solution)/shard_map/psum | solution.py:984
  (268 shorter events, 70.4 us)
Async XLA Ops:
  7.2 74.8 %all-gather.3.cloned.1.call-start = ((), (), s32[]{:S(2)}) async-start(), calls=%async_computation.1 | async-start | bytes 4456448 | tf_op jit(solution)/shard_map/all_gather | solution.py:848
  8.1 6.8 %collective-permute-start.10 = (bf16[64,1024]{1,0:T(8,128)(2,1)S(1)}, bf16[64,1024]{1,0:T(8,128)(2,1)S(1)}, u32[]{:S(2)}, u32[]{:S(2)}) collective-permute-start(bf16[64,1024]{1,0:T(8,128)(2,1)S(1)} %pad_maximum_fusion.5), channel_id=1, source_target_pairs={{0,64},{64,0},{1,65},{65,1},{2,66},{66,2},{3,67},{67,3},{4,68},{68... | collective-permute-start | bytes 393224 | tf_op jit(solution)/shard_map/ppermute | solution.py:31
  16.7 152.2 %all-gather.5.cloned.1.call-start = ((), (), s32[]{:S(2)}) async-start(), calls=%async_computation.2 | async-start | bytes 9469952 | tf_op jit(solution)/shard_map/all_gather | solution.py:878
  16.7 4.6 %collective-permute-start = (bf16[64,256]{1,0:T(8,128)(2,1)}, bf16[64,256]{1,0:T(8,128)(2,1)S(1)}, u32[]{:S(2)}, u32[]{:S(2)}) collective-permute-start(bf16[64,256]{1,0:T(8,128)(2,1)} %get-tuple-element.98), channel_id=1, source_target_pairs={{0,64},{64,0},{1,65},{65,1},{2,66},{66,2},{3,67},{67,3},{4,68},{68... | collective-permute-start | bytes 98312 | tf_op jit(solution)/shard_map/ppermute | solution.py:31
  22.1 7.6 %collective-permute-start.5 = (bf16[128,256]{1,0:T(8,128)(2,1)S(1)}, bf16[128,256]{1,0:T(8,128)(2,1)S(1)}, u32[]{:S(2)}, u32[]{:S(2)}) collective-permute-start(bf16[128,256]{1,0:T(8,128)(2,1)S(1)} %pad_maximum_fusion.6), channel_id=1, source_target_pairs={{0,12},{4,0},{8,4},{12,8},{1,13},{5,1},{9,5},{13,9},{2,14},{6,2},{... | collective-permute-start | bytes 196616 | tf_op jit(solution)/shard_map/ppermute | solution.py:31
  24.6 5.0 %collective-permute-start.4 = (bf16[128,256]{1,0:T(8,128)(2,1)S(1)}, bf16[128,256]{1,0:T(8,128)(2,1)S(1)}, u32[]{:S(2)}, u32[]{:S(2)}) collective-permute-start(bf16[128,256]{1,0:T(8,128)(2,1)S(1)} %pad_maximum_fusion.6), channel_id=1, source_target_pairs={{0,4},{4,8},{8,12},{12,0},{1,5},{5,9},{9,13},{13,1},{2,6},{6,10},{... | collective-permute-start | bytes 196616 | tf_op jit(solution)/shard_map/ppermute | solution.py:31
  24.6 5.1 %collective-permute-start.6 = (bf16[128,256]{1,0:T(8,128)(2,1)S(1)}, bf16[128,256]{1,0:T(8,128)(2,1)S(1)}, u32[]{:S(2)}, u32[]{:S(2)}) collective-permute-start(bf16[128,256]{1,0:T(8,128)(2,1)S(1)} %pad_maximum_fusion.6), channel_id=1, source_target_pairs={{0,8},{4,12},{8,0},{12,4},{1,9},{5,13},{9,1},{13,5},{2,10},{6,14},... | collective-permute-start | bytes 196616 | tf_op jit(solution)/shard_map/ppermute | solution.py:31
  26.4 14.0 %collective-permute-start.2 = (bf16[128,2048]{1,0:T(8,128)(2,1)}, bf16[128,2048]{1,0:T(8,128)(2,1)S(1)}, u32[]{:S(2)}, u32[]{:S(2)}) collective-permute-start(bf16[128,2048]{1,0:T(8,128)(2,1)} %get-tuple-element.99.refs_0_.base_ref.refs_4_), channel_id=1, source_target_pairs={{0,2},{2,0},{1,3},{3,1},{4,6},{6,4},{5,7},{7,5},{8,10},{10,8},{9,1... | collective-permute-start | bytes 1572872 | tf_op jit(solution)/shard_map/ppermute | solution.py:31
  29.7 11.4 %collective-permute-start.7 = (bf16[4,128,256]{2,1,0:T(8,128)(2,1)S(1)}, bf16[4,128,256]{2,1,0:T(8,128)(2,1)S(1)}, u32[]{:S(2)}, u32[]{:S(2)}) collective-permute-start(bf16[4,128,256]{2,1,0:T(8,128)(2,1)S(1)} %bitcast_dynamic-update-slice_fusion.4), channel_id=1, source_target_pairs={{0,16},{16,32},{32,48},{48,0},{1,17},{17,33},{33,49},{49,1},{2,18}... | collective-permute-start | bytes 786440 | tf_op jit(solution)/shard_map/ppermute | solution.py:31
  31.8 21.1 %collective-permute-start.1 = (bf16[128,2048]{1,0:T(8,128)(2,1)S(1)}, bf16[128,2048]{1,0:T(8,128)(2,1)S(1)}, u32[]{:S(2)}, u32[]{:S(2)}) collective-permute-start(bf16[128,2048]{1,0:T(8,128)(2,1)S(1)} %copy-done.7), channel_id=1, source_target_pairs={{0,1},{1,0},{2,3},{3,2},{4,5},{5,4},{6,7},{7,6},{8,9},{9,8},{10,11... | collective-permute-start | bytes 1572872 | tf_op jit(solution)/shard_map/ppermute | solution.py:31
  36.2 16.6 %collective-permute-start.9 = (bf16[4,128,256]{2,1,0:T(8,128)(2,1)S(1)}, bf16[4,128,256]{2,1,0:T(8,128)(2,1)S(1)}, u32[]{:S(2)}, u32[]{:S(2)}) collective-permute-start(bf16[4,128,256]{2,1,0:T(8,128)(2,1)S(1)} %bitcast_dynamic-update-slice_fusion.4), channel_id=1, source_target_pairs={{0,32},{16,48},{32,0},{48,16},{1,33},{17,49},{33,1},{49,17},{2,34}... | collective-permute-start | bytes 786440 | tf_op jit(solution)/shard_map/ppermute | solution.py:31
  40.3 12.5 %collective-permute-start.8 = (bf16[4,128,256]{2,1,0:T(8,128)(2,1)S(1)}, bf16[4,128,256]{2,1,0:T(8,128)(2,1)S(1)}, u32[]{:S(2)}, u32[]{:S(2)}) collective-permute-start(bf16[4,128,256]{2,1,0:T(8,128)(2,1)S(1)} %bitcast_dynamic-update-slice_fusion.4), channel_id=1, source_target_pairs={{0,48},{16,0},{32,16},{48,32},{1,49},{17,1},{33,17},{49,33},{2,50}... | collective-permute-start | bytes 786440 | tf_op jit(solution)/shard_map/ppermute | solution.py:31
  40.4 12.4 %collective-permute-start.3 = (bf16[128,2048]{1,0:T(8,128)(2,1)S(1)}, bf16[128,2048]{1,0:T(8,128)(2,1)S(1)}, u32[]{:S(2)}, u32[]{:S(2)}) collective-permute-start(bf16[128,2048]{1,0:T(8,128)(2,1)S(1)} %collective-permute-done.2.refs_2_.refs_6_), channel_id=1, source_target_pairs={{0,1},{1,0},{2,3},{3,2},{4,5},{5,4},{6,7},{7,6},{8,9},{9,8},{10,11... | collective-permute-start | bytes 1572872 | tf_op jit(solution)/shard_map/ppermute | solution.py:31
  56.8 21.2 %collective-permute-start.14 = (bf16[128,2048]{1,0:T(8,128)(2,1)S(1)}, bf16[128,2048]{1,0:T(8,128)(2,1)}, u32[]{:S(2)}, u32[]{:S(2)}) collective-permute-start(bf16[128,2048]{1,0:T(8,128)(2,1)S(1)} %copy-done.6), channel_id=1, source_target_pairs={{0,2},{2,0},{1,3},{3,1},{4,6},{6,4},{5,7},{7,5},{8,10},{10,8},{9,1... | collective-permute-start | bytes 1572872 | tf_op jit(solution)/shard_map/ppermute | solution.py:31
  58.7 19.3 %collective-permute-start.26 = (bf16[64,2176]{1,0:T(8,128)(2,1)}, bf16[64,2176]{1,0:T(8,128)(2,1)}, u32[]{:S(2)}, u32[]{:S(2)}) collective-permute-start(bf16[64,2176]{1,0:T(8,128)(2,1)} %dynamic-slice_bitcast_fusion.1), channel_id=1, source_target_pairs={{0,64},{64,0},{1,65},{65,1},{2,66},{66,2},{3,67},{67,3},{4,68},{68... | collective-permute-start | bytes 835592 | tf_op jit(solution)/shard_map/ppermute | solution.py:31
  61.4 7.5 %collective-permute-start.13 = (bf16[512,128]{1,0:T(8,128)(2,1)S(1)}, bf16[512,128]{1,0:T(8,128)(2,1)}, u32[]{:S(2)}, u32[]{:S(2)}) collective-permute-start(bf16[512,128]{1,0:T(8,128)(2,1)S(1)} %get-tuple-element.102.refs_0_), channel_id=1, source_target_pairs={{0,12},{4,0},{8,4},{12,8},{1,13},{5,1},{9,5},{13,9},{2,14},{6,2},{... | collective-permute-start | bytes 393224 | tf_op jit(solution)/shard_map/ppermute | solution.py:31
  63.6 9.2 %collective-permute-start.12 = (bf16[512,128]{1,0:T(8,128)(2,1)S(1)}, bf16[512,128]{1,0:T(8,128)(2,1)}, u32[]{:S(2)}, u32[]{:S(2)}) collective-permute-start(bf16[512,128]{1,0:T(8,128)(2,1)S(1)} %get-tuple-element.102.refs_0_), channel_id=1, source_target_pairs={{0,8},{4,12},{8,0},{12,4},{1,9},{5,13},{9,1},{13,5},{2,10},{6,14},... | collective-permute-start | bytes 393224 | tf_op jit(solution)/shard_map/ppermute | solution.py:31
  63.6 11.9 %collective-permute-start.11 = (bf16[512,128]{1,0:T(8,128)(2,1)S(1)}, bf16[512,128]{1,0:T(8,128)(2,1)}, u32[]{:S(2)}, u32[]{:S(2)}) collective-permute-start(bf16[512,128]{1,0:T(8,128)(2,1)S(1)} %get-tuple-element.102.refs_0_), channel_id=1, source_target_pairs={{0,4},{4,8},{8,12},{12,0},{1,5},{5,9},{9,13},{13,1},{2,6},{6,10},{... | collective-permute-start | bytes 393224 | tf_op jit(solution)/shard_map/ppermute | solution.py:31
  84.8 296.4 %reduce-scatter.2.cloned.1.call-start = ((), (), s32[]{:S(2)}) async-start(), calls=%async_computation.3 | async-start | bytes 9469952 | tf_op jit(solution)/shard_map/reduce_scatter | solution.py:912
  87.5 25.5 %collective-permute-start.15 = (bf16[256,2048]{1,0:T(8,128)(2,1)S(1)}, bf16[256,2048]{1,0:T(8,128)(2,1)S(1)}, u32[]{:S(2)}, u32[]{:S(2)}) collective-permute-start(bf16[256,2048]{1,0:T(8,128)(2,1)S(1)} %pad_maximum_fusion), channel_id=1, source_target_pairs={{0,64},{64,0},{1,65},{65,1},{2,66},{66,2},{3,67},{67,3},{4,68},{68... | collective-permute-start | bytes 3145736 | tf_op jit(solution)/shard_map/ppermute | solution.py:31
  115.9 4.9 %collective-permute-start.16 = (bf16[256,2048]{1,0:T(8,128)(2,1)S(1)}, bf16[256,2048]{1,0:T(8,128)(2,1)S(1)}, u32[]{:S(2)}, u32[]{:S(2)}) collective-permute-start(bf16[256,2048]{1,0:T(8,128)(2,1)S(1)} %get-tuple-element.111), channel_id=1, source_target_pairs={{0,1},{1,0},{2,3},{3,2},{4,5},{5,4},{6,7},{7,6},{8,9},{9,8},{10,11... | collective-permute-start | bytes 3145736 | tf_op jit(solution)/shard_map/ppermute | solution.py:31
  117.9 49.1 %collective-permute-start.25 = (bf16[512,2048]{1,0:T(8,128)(2,1)}, bf16[512,2048]{1,0:T(8,128)(2,1)}, u32[]{:S(2)}, u32[]{:S(2)}) collective-permute-start(bf16[512,2048]{1,0:T(8,128)(2,1)} %constant_dynamic-update-slice_fusion.refs_8_), channel_id=1, source_target_pairs={{0,1},{1,0},{2,3},{3,2},{4,5},{5,4},{6,7},{7,6},{8,9},{9,8},{10,11... | collective-permute-start | bytes 6291464 | tf_op jit(solution)/shard_map/ppermute | solution.py:31
  120.9 13.3 %collective-permute-start.17 = (bf16[128,2048]{1,0:T(8,128)(2,1)S(1)}, bf16[128,2048]{1,0:T(8,128)(2,1)S(1)}, u32[]{:S(2)}, u32[]{:S(2)}) collective-permute-start(bf16[128,2048]{1,0:T(8,128)(2,1)S(1)} %add_convert_fusion.3), channel_id=1, source_target_pairs={{0,2},{2,0},{1,3},{3,1},{4,6},{6,4},{5,7},{7,5},{8,10},{10,8},{9,1... | collective-permute-start | bytes 1572872 | tf_op jit(solution)/shard_map/ppermute | solution.py:31
  136.4 14.3 %collective-permute-start.20 = (bf16[128,2048]{1,0:T(8,128)(2,1)}, bf16[128,2048]{1,0:T(8,128)(2,1)}, u32[]{:S(2)}, u32[]{:S(2)}) collective-permute-start(bf16[128,2048]{1,0:T(8,128)(2,1)} %get-tuple-element.126.refs_0_), channel_id=1, source_target_pairs={{0,66},{2,0},{64,2},{66,64},{1,67},{3,1},{65,3},{67,65},{4,70},{6,... | collective-permute-start | bytes 1572872 | tf_op jit(solution)/shard_map/ppermute | solution.py:31
  139.2 23.7 %collective-permute-start.19 = (bf16[128,2048]{1,0:T(8,128)(2,1)}, bf16[128,2048]{1,0:T(8,128)(2,1)}, u32[]{:S(2)}, u32[]{:S(2)}) collective-permute-start(bf16[128,2048]{1,0:T(8,128)(2,1)} %get-tuple-element.126.refs_0_), channel_id=1, source_target_pairs={{0,64},{2,66},{64,0},{66,2},{1,65},{3,67},{65,1},{67,3},{4,68},{6,... | collective-permute-start | bytes 1572872 | tf_op jit(solution)/shard_map/ppermute | solution.py:31
  139.5 26.6 %collective-permute-start.18 = (bf16[128,2048]{1,0:T(8,128)(2,1)}, bf16[128,2048]{1,0:T(8,128)(2,1)}, u32[]{:S(2)}, u32[]{:S(2)}) collective-permute-start(bf16[128,2048]{1,0:T(8,128)(2,1)} %get-tuple-element.126.refs_0_), channel_id=1, source_target_pairs={{0,2},{2,64},{64,66},{66,0},{1,3},{3,65},{65,67},{67,1},{4,6},{6,6... | collective-permute-start | bytes 1572872 | tf_op jit(solution)/shard_map/ppermute | solution.py:31
  140.3 26.7 %collective-permute-start.21 = (bf16[128,2048]{1,0:T(8,128)(2,1)}, bf16[128,2048]{1,0:T(8,128)(2,1)}, u32[]{:S(2)}, u32[]{:S(2)}) collective-permute-start(bf16[128,2048]{1,0:T(8,128)(2,1)} %get-tuple-element.126.refs_0_), channel_id=1, source_target_pairs={{0,1},{1,0},{2,3},{3,2},{4,5},{5,4},{6,7},{7,6},{8,9},{9,8},{10,11... | collective-permute-start | bytes 1572872 | tf_op jit(solution)/shard_map/ppermute | solution.py:31
  150.8 16.2 %collective-permute-start.24 = (bf16[128,2048]{1,0:T(8,128)(2,1)}, bf16[128,2048]{1,0:T(8,128)(2,1)}, u32[]{:S(2)}, u32[]{:S(2)}) collective-permute-start(bf16[128,2048]{1,0:T(8,128)(2,1)} %collective-permute-done.20.refs_3_), channel_id=1, source_target_pairs={{0,1},{1,0},{2,3},{3,2},{4,5},{5,4},{6,7},{7,6},{8,9},{9,8},{10,11... | collective-permute-start | bytes 1572872 | tf_op jit(solution)/shard_map/ppermute | solution.py:31
  162.9 4.1 %collective-permute-start.23 = (bf16[128,2048]{1,0:T(8,128)(2,1)}, bf16[128,2048]{1,0:T(8,128)(2,1)}, u32[]{:S(2)}, u32[]{:S(2)}) collective-permute-start(bf16[128,2048]{1,0:T(8,128)(2,1)} %collective-permute-done.19.refs_2_), channel_id=1, source_target_pairs={{0,1},{1,0},{2,3},{3,2},{4,5},{5,4},{6,7},{7,6},{8,9},{9,8},{10,11... | collective-permute-start | bytes 1572872 | tf_op jit(solution)/shard_map/ppermute | solution.py:31
  166.1 2.8 collective-permute-start.22
  199.5 4.5 %collective-permute-start.27 = (bf16[512,2048]{1,0:T(8,128)(2,1)}, bf16[512,2048]{1,0:T(8,128)(2,1)S(1)}, u32[]{:S(2)}, u32[]{:S(2)}) collective-permute-start(bf16[512,2048]{1,0:T(8,128)(2,1)} %get-tuple-element.122), channel_id=1, source_target_pairs={{0,1},{1,0},{2,3},{3,2},{4,5},{5,4},{6,7},{7,6},{8,9},{9,8},{10,11... | collective-permute-start | bytes 6291464 | tf_op jit(solution)/shard_map/ppermute | solution.py:31
  208.1 24.9 %collective-permute-start.28 = (bf16[128,2048]{1,0:T(8,128)(2,1)}, bf16[128,2048]{1,0:T(8,128)(2,1)}, u32[]{:S(2)}, u32[]{:S(2)}) collective-permute-start(bf16[128,2048]{1,0:T(8,128)(2,1)} %get-tuple-element.123), channel_id=1, source_target_pairs={{0,66},{2,0},{64,2},{66,64},{1,67},{3,1},{65,3},{67,65},{4,70},{6,... | collective-permute-start | bytes 1572872 | tf_op jit(solution)/shard_map/ppermute | solution.py:31
  208.9 24.1 %collective-permute-start.30 = (bf16[128,2048]{1,0:T(8,128)(2,1)}, bf16[128,2048]{1,0:T(8,128)(2,1)}, u32[]{:S(2)}, u32[]{:S(2)}) collective-permute-start(bf16[128,2048]{1,0:T(8,128)(2,1)} %get-tuple-element.124), channel_id=1, source_target_pairs={{0,64},{2,66},{64,0},{66,2},{1,65},{3,67},{65,1},{67,3},{4,68},{6,... | collective-permute-start | bytes 1572872 | tf_op jit(solution)/shard_map/ppermute | solution.py:31
  208.9 26.9 %collective-permute-start.29 = (bf16[128,2048]{1,0:T(8,128)(2,1)}, bf16[128,2048]{1,0:T(8,128)(2,1)}, u32[]{:S(2)}, u32[]{:S(2)}) collective-permute-start(bf16[128,2048]{1,0:T(8,128)(2,1)} %get-tuple-element.125), channel_id=1, source_target_pairs={{0,2},{2,64},{64,66},{66,0},{1,3},{3,65},{65,67},{67,1},{4,6},{6,6... | collective-permute-start | bytes 1572872 | tf_op jit(solution)/shard_map/ppermute | solution.py:31
  239.7 27.3 %collective-permute-start.31 = (bf16[512,2048]{1,0:T(8,128)(2,1)}, bf16[512,2048]{1,0:T(8,128)(2,1)}, u32[]{:S(2)}, u32[]{:S(2)}) collective-permute-start(bf16[512,2048]{1,0:T(8,128)(2,1)} %get-tuple-element.135), channel_id=1, source_target_pairs={{0,1},{1,0},{2,3},{3,2},{4,5},{5,4},{6,7},{7,6},{8,9},{9,8},{10,11... | collective-permute-start | bytes 6291464 | tf_op jit(solution)/shard_map/ppermute | solution.py:31
  240.2 13.8 %collective-permute-start.33 = (bf16[128,2048]{1,0:T(8,128)(2,1)}, bf16[128,2048]{1,0:T(8,128)(2,1)S(1)}, u32[]{:S(2)}, u32[]{:S(2)}) collective-permute-start(bf16[128,2048]{1,0:T(8,128)(2,1)} %get-tuple-element.134.refs_0_.refs_8_), channel_id=1, source_target_pairs={{0,2},{2,0},{1,3},{3,1},{4,6},{6,4},{5,7},{7,5},{8,10},{10,8},{9,1... | collective-permute-start | bytes 1572872 | tf_op jit(solution)/shard_map/ppermute | solution.py:31
  240.2 14.6 %collective-permute-start.32 = (bf16[128,2048]{1,0:T(8,128)(2,1)}, bf16[128,2048]{1,0:T(8,128)(2,1)}, u32[]{:S(2)}, u32[]{:S(2)}) collective-permute-start(bf16[128,2048]{1,0:T(8,128)(2,1)} %get-tuple-element.134.refs_0_.refs_8_), channel_id=1, source_target_pairs={{0,1},{1,0},{2,3},{3,2},{4,5},{5,4},{6,7},{7,6},{8,9},{9,8},{10,11... | collective-permute-start | bytes 1572872 | tf_op jit(solution)/shard_map/ppermute | solution.py:31
  253.9 2.5 collective-permute-start.34
  262.1 40.6 %collective-permute-start.37 = (bf16[512,512]{1,0:T(8,128)(2,1)}, bf16[512,512]{1,0:T(8,128)(2,1)}, u32[]{:S(2)}, u32[]{:S(2)}) collective-permute-start(bf16[512,512]{1,0:T(8,128)(2,1)} %get-tuple-element.140), channel_id=1, source_target_pairs={{0,16},{16,32},{32,48},{48,0},{1,17},{17,33},{33,49},{49,1},{2,18}... | collective-permute-start | bytes 1572872 | tf_op jit(solution)/shard_map/ppermute | solution.py:31
  263.3 39.5 %collective-permute-start.38 = (bf16[512,512]{1,0:T(8,128)(2,1)}, bf16[512,512]{1,0:T(8,128)(2,1)}, u32[]{:S(2)}, u32[]{:S(2)}) collective-permute-start(bf16[512,512]{1,0:T(8,128)(2,1)} %get-tuple-element.141), channel_id=1, source_target_pairs={{0,32},{16,48},{32,0},{48,16},{1,33},{17,49},{33,1},{49,17},{2,34}... | collective-permute-start | bytes 1572872 | tf_op jit(solution)/shard_map/ppermute | solution.py:31
  265.9 34.0 %collective-permute-start.39 = (bf16[512,512]{1,0:T(8,128)(2,1)}, bf16[512,512]{1,0:T(8,128)(2,1)}, u32[]{:S(2)}, u32[]{:S(2)}) collective-permute-start(bf16[512,512]{1,0:T(8,128)(2,1)} %get-tuple-element.142), channel_id=1, source_target_pairs={{0,48},{16,0},{32,16},{48,32},{1,49},{17,1},{33,17},{49,33},{2,50}... | collective-permute-start | bytes 1572872 | tf_op jit(solution)/shard_map/ppermute | solution.py:31
  271.2 36.3 %collective-permute-start.35 = (bf16[256,2048]{1,0:T(8,128)(2,1)}, bf16[256,2048]{1,0:T(8,128)(2,1)}, u32[]{:S(2)}, u32[]{:S(2)}) collective-permute-start(bf16[256,2048]{1,0:T(8,128)(2,1)} %get-tuple-element.138), channel_id=1, source_target_pairs={{0,2},{2,0},{1,3},{3,1},{4,6},{6,4},{5,7},{7,5},{8,10},{10,8},{9,1... | collective-permute-start | bytes 3145736 | tf_op jit(solution)/shard_map/ppermute | solution.py:31
  302.8 13.5 %collective-permute-start.42 = (bf16[512,128]{1,0:T(8,128)(2,1)S(1)}, bf16[512,128]{1,0:T(8,128)(2,1)S(1)}, u32[]{:S(2)}, u32[]{:S(2)}) collective-permute-start(bf16[512,128]{1,0:T(8,128)(2,1)S(1)} %get-tuple-element.191), channel_id=1, source_target_pairs={{0,4},{4,8},{8,12},{12,0},{1,5},{5,9},{9,13},{13,1},{2,6},{6,10},{... | collective-permute-start | bytes 393224 | tf_op jit(solution)/shard_map/ppermute | solution.py:31
  304.6 12.2 %collective-permute-start.41 = (bf16[512,128]{1,0:T(8,128)(2,1)S(1)}, bf16[512,128]{1,0:T(8,128)(2,1)S(1)}, u32[]{:S(2)}, u32[]{:S(2)}) collective-permute-start(bf16[512,128]{1,0:T(8,128)(2,1)S(1)} %get-tuple-element.192), channel_id=1, source_target_pairs={{0,8},{4,12},{8,0},{12,4},{1,9},{5,13},{9,1},{13,5},{2,10},{6,14},... | collective-permute-start | bytes 393224 | tf_op jit(solution)/shard_map/ppermute | solution.py:31
  305.5 11.7 %collective-permute-start.40 = (bf16[512,128]{1,0:T(8,128)(2,1)S(1)}, bf16[512,128]{1,0:T(8,128)(2,1)S(1)}, u32[]{:S(2)}, u32[]{:S(2)}) collective-permute-start(bf16[512,128]{1,0:T(8,128)(2,1)S(1)} %get-tuple-element.193), channel_id=1, source_target_pairs={{0,12},{4,0},{8,4},{12,8},{1,13},{5,1},{9,5},{13,9},{2,14},{6,2},{... | collective-permute-start | bytes 393224 | tf_op jit(solution)/shard_map/ppermute | solution.py:31
  321.0 14.5 %collective-permute-start.46 = (bf16[512,256]{1,0:T(8,128)(2,1)S(1)}, bf16[512,256]{1,0:T(8,128)(2,1)S(1)}, u32[]{:S(2)}, u32[]{:S(2)}) collective-permute-start(bf16[512,256]{1,0:T(8,128)(2,1)S(1)} %get-tuple-element.167), channel_id=1, source_target_pairs={{0,32},{16,48},{32,0},{48,16},{1,33},{17,49},{33,1},{49,17},{2,34}... | collective-permute-start | bytes 786440 | tf_op jit(solution)/shard_map/ppermute | solution.py:31
  322.1 20.8 %collective-permute-start.44 = (bf16[512,384]{1,0:T(8,128)(2,1)S(1)}, bf16[512,384]{1,0:T(8,128)(2,1)S(1)}, u32[]{:S(2)}, u32[]{:S(2)}) collective-permute-start(bf16[512,384]{1,0:T(8,128)(2,1)S(1)} %get-tuple-element.159), channel_id=1, source_target_pairs={{0,4},{4,8},{8,12},{12,0},{1,5},{5,9},{9,13},{13,1},{2,6},{6,10},{... | collective-permute-start | bytes 1179656 | tf_op jit(solution)/shard_map/ppermute | solution.py:31
  322.1 27.3 %collective-permute-start.43 = (bf16[512,384]{1,0:T(8,128)(2,1)S(1)}, bf16[512,384]{1,0:T(8,128)(2,1)S(1)}, u32[]{:S(2)}, u32[]{:S(2)}) collective-permute-start(bf16[512,384]{1,0:T(8,128)(2,1)S(1)} %get-tuple-element.160), channel_id=1, source_target_pairs={{0,8},{4,12},{8,0},{12,4},{1,9},{5,13},{9,1},{13,5},{2,10},{6,14},... | collective-permute-start | bytes 1179656 | tf_op jit(solution)/shard_map/ppermute | solution.py:31
  324.9 24.5 %collective-permute-start.45 = (bf16[512,384]{1,0:T(8,128)(2,1)S(1)}, bf16[512,384]{1,0:T(8,128)(2,1)S(1)}, u32[]{:S(2)}, u32[]{:S(2)}) collective-permute-start(bf16[512,384]{1,0:T(8,128)(2,1)S(1)} %get-tuple-element.161), channel_id=1, source_target_pairs={{0,12},{4,0},{8,4},{12,8},{1,13},{5,1},{9,5},{13,9},{2,14},{6,2},{... | collective-permute-start | bytes 1179656 | tf_op jit(solution)/shard_map/ppermute | solution.py:31
  326.5 16.3 %collective-permute-start.47 = (bf16[512,256]{1,0:T(8,128)(2,1)S(1)}, bf16[512,256]{1,0:T(8,128)(2,1)S(1)}, u32[]{:S(2)}, u32[]{:S(2)}) collective-permute-start(bf16[512,256]{1,0:T(8,128)(2,1)S(1)} %get-tuple-element.168), channel_id=1, source_target_pairs={{0,16},{16,32},{32,48},{48,0},{1,17},{17,33},{33,49},{49,1},{2,18}... | collective-permute-start | bytes 786440 | tf_op jit(solution)/shard_map/ppermute | solution.py:31
  335.6 7.3 %collective-permute-start.48 = (bf16[512,256]{1,0:T(8,128)(2,1)S(1)}, bf16[512,256]{1,0:T(8,128)(2,1)S(1)}, u32[]{:S(2)}, u32[]{:S(2)}) collective-permute-start(bf16[512,256]{1,0:T(8,128)(2,1)S(1)} %get-tuple-element.169), channel_id=1, source_target_pairs={{0,48},{16,0},{32,16},{48,32},{1,49},{17,1},{33,17},{49,33},{2,50}... | collective-permute-start | bytes 786440 | tf_op jit(solution)/shard_map/ppermute | solution.py:31
  350.3 8.0 %collective-permute-start.49 = (bf16[256,2048]{1,0:T(8,128)(2,1)}, bf16[256,2048]{1,0:T(8,128)(2,1)}, u32[]{:S(2)}, u32[]{:S(2)}) collective-permute-start(bf16[256,2048]{1,0:T(8,128)(2,1)} %get-tuple-element.170), channel_id=1, source_target_pairs={{0,1},{1,0},{2,3},{3,2},{4,5},{5,4},{6,7},{7,6},{8,9},{9,8},{10,11... | collective-permute-start | bytes 3145736 | tf_op jit(solution)/shard_map/ppermute | solution.py:31
  354.7 19.3 %collective-permute-start.36 = (bf16[128,2048]{1,0:T(8,128)(2,1)S(1)}, bf16[128,2048]{1,0:T(8,128)(2,1)S(1)}, u32[]{:S(2)}, u32[]{:S(2)}) collective-permute-start(bf16[128,2048]{1,0:T(8,128)(2,1)S(1)} %copy-done.50), channel_id=1, source_target_pairs={{0,64},{64,0},{1,65},{65,1},{2,66},{66,2},{3,67},{67,3},{4,68},{68... | collective-permute-start | bytes 1572872 | tf_op jit(solution)/shard_map/ppermute | solution.py:31
  359.6 20.1 %collective-permute-start.50 = (bf16[128,2048]{1,0:T(8,128)(2,1)S(1)}, bf16[128,2048]{1,0:T(8,128)(2,1)S(1)}, u32[]{:S(2)}, u32[]{:S(2)}) collective-permute-start(bf16[128,2048]{1,0:T(8,128)(2,1)S(1)} %add_convert_fusion.1), channel_id=1, source_target_pairs={{0,2},{2,0},{1,3},{3,1},{4,6},{6,4},{5,7},{7,5},{8,10},{10,8},{9,1... | collective-permute-start | bytes 1572872 | tf_op jit(solution)/shard_map/ppermute | solution.py:31
  360.0 5.4 %collective-permute-start.51 = (bf16[128,384]{1,0:T(8,128)(2,1)S(1)}, bf16[128,384]{1,0:T(8,128)(2,1)S(1)}, u32[]{:S(2)}, u32[]{:S(2)}) collective-permute-start(bf16[128,384]{1,0:T(8,128)(2,1)S(1)} %get-tuple-element.188), channel_id=1, source_target_pairs={{0,16},{16,32},{32,48},{48,0},{1,17},{17,33},{33,49},{49,1},{2,18}... | collective-permute-start | bytes 294920 | tf_op jit(solution)/shard_map/ppermute | solution.py:31
  360.1 10.1 %collective-permute-start.53 = (bf16[128,384]{1,0:T(8,128)(2,1)S(1)}, bf16[128,384]{1,0:T(8,128)(2,1)S(1)}, u32[]{:S(2)}, u32[]{:S(2)}) collective-permute-start(bf16[128,384]{1,0:T(8,128)(2,1)S(1)} %get-tuple-element.189), channel_id=1, source_target_pairs={{0,32},{16,48},{32,0},{48,16},{1,33},{17,49},{33,1},{49,17},{2,34}... | collective-permute-start | bytes 294920 | tf_op jit(solution)/shard_map/ppermute | solution.py:31
  361.5 11.1 %collective-permute-start.52 = (bf16[128,384]{1,0:T(8,128)(2,1)S(1)}, bf16[128,384]{1,0:T(8,128)(2,1)S(1)}, u32[]{:S(2)}, u32[]{:S(2)}) collective-permute-start(bf16[128,384]{1,0:T(8,128)(2,1)S(1)} %get-tuple-element.190), channel_id=1, source_target_pairs={{0,48},{16,0},{32,16},{48,32},{1,49},{17,1},{33,17},{49,33},{2,50}... | collective-permute-start | bytes 294920 | tf_op jit(solution)/shard_map/ppermute | solution.py:31
  365.4 19.5 %collective-permute-start.54 = (bf16[128,768]{1,0:T(8,128)(2,1)}, bf16[128,768]{1,0:T(8,128)(2,1)}, u32[]{:S(2)}, u32[]{:S(2)}) collective-permute-start(bf16[128,768]{1,0:T(8,128)(2,1)} %get-tuple-element.185), channel_id=1, source_target_pairs={{0,4},{4,8},{8,12},{12,0},{1,5},{5,9},{9,13},{13,1},{2,6},{6,10},{... | collective-permute-start | bytes 589832 | tf_op jit(solution)/shard_map/ppermute | solution.py:31
  370.2 14.7 %collective-permute-start.56 = (bf16[128,768]{1,0:T(8,128)(2,1)S(1)}, bf16[128,768]{1,0:T(8,128)(2,1)}, u32[]{:S(2)}, u32[]{:S(2)}) collective-permute-start(bf16[128,768]{1,0:T(8,128)(2,1)S(1)} %get-tuple-element.186), channel_id=1, source_target_pairs={{0,8},{4,12},{8,0},{12,4},{1,9},{5,13},{9,1},{13,5},{2,10},{6,14},... | collective-permute-start | bytes 589832 | tf_op jit(solution)/shard_map/ppermute | solution.py:31
  372.7 12.2 %collective-permute-start.55 = (bf16[128,768]{1,0:T(8,128)(2,1)S(1)}, bf16[128,768]{1,0:T(8,128)(2,1)}, u32[]{:S(2)}, u32[]{:S(2)}) collective-permute-start(bf16[128,768]{1,0:T(8,128)(2,1)S(1)} %get-tuple-element.187), channel_id=1, source_target_pairs={{0,12},{4,0},{8,4},{12,8},{1,13},{5,1},{9,5},{13,9},{2,14},{6,2},{... | collective-permute-start | bytes 589832 | tf_op jit(solution)/shard_map/ppermute | solution.py:31
  381.1 19.5 %copy-start.63 = (bf16[64]{0:T(256)(128)(2,1)S(1)}, bf16[64]{0:T(256)(128)(2,1)}, u32[]{:S(2)}) copy-start(bf16[64]{0:T(256)(128)(2,1)} %param.19) | copy-start | bytes 388
  381.2 21.8 %copy-start.1 = (s32[512]{0:T(512)S(1)}, s32[512]{0:T(512)}, u32[]{:S(2)}) copy-start(s32[512]{0:T(512)} %param.13) | copy-start | bytes 6148
  382.3 19.6 %collective-permute-start.58 = (bf16[64,2176]{1,0:T(8,128)(2,1)S(1)}, bf16[64,2176]{1,0:T(8,128)(2,1)S(1)}, u32[]{:S(2)}, u32[]{:S(2)}) collective-permute-start(bf16[64,2176]{1,0:T(8,128)(2,1)S(1)} %dynamic-slice_bitcast_fusion), channel_id=1, source_target_pairs={{0,64},{64,0},{1,65},{65,1},{2,66},{66,2},{3,67},{67,3},{4,68},{68... | collective-permute-start | bytes 835592 | tf_op jit(solution)/shard_map/ppermute | solution.py:31
  386.6 14.6 %collective-permute-start.57 = (bf16[64,1152]{1,0:T(8,128)(2,1)S(1)}, bf16[64,1152]{1,0:T(8,128)(2,1)S(1)}, u32[]{:S(2)}, u32[]{:S(2)}) collective-permute-start(bf16[64,1152]{1,0:T(8,128)(2,1)S(1)} %dynamic-slice_bitcast_fusion.5), channel_id=1, source_target_pairs={{0,64},{64,0},{1,65},{65,1},{2,66},{66,2},{3,67},{67,3},{4,68},{68... | collective-permute-start | bytes 442376 | tf_op jit(solution)/shard_map/ppermute | solution.py:31
  (62 other events, 497.8 us)
Sparse Core Ops, SparseCore 0:
  16.8 65.1 all-gather.2
  84.9 73.3 all-gather.4
  254.9 122.2 reduce-scatter.1
where the time goes:
time: 418 us; the launch traced here: 410 us
  Pallas kernels  130 us (31%)
  waiting for transfers between devices  119 us (28%)
  starting transfers between devices  92.4 us (22%)
  local copies, waits for them, and re-layouts  22.9 us (5%)
  other arithmetic  16.3 us (4%)
  between operations  15.2 us (4%)
  blocking collectives  13.6 us (3%)
    ppermute x59, waiting for transfers between devices, shift(): lax.ppermute(block, axis, [(i, (i + distance) % n) for i in range(n)])  115 us
    ppermute x59, starting transfers between devices, shift(): lax.ppermute(block, axis, [(i, (i + distance) % n) for i in range(n)])  92.3 us
    pallas_call x2, Pallas kernels, attend_back(): pl.pallas_call(functools.partial(attend_back_kernel, distances, first, la...  27.2 us
    pallas_call x1, Pallas kernels, hidden_units(): pl.pallas_call(functools.partial(hidden_kernel, width), out_shape=(jax.Sh...  20.1 us
    pallas_call x3, Pallas kernels, rows_out(): pl.pallas_call(functools.partial(rows_out_kernel, terms, places), grid=(d...  19.5 us
    pallas_call x1, Pallas kernels, attend(): pl.pallas_call(attend_kernel, out_shape=(jax.ShapeDtypeStruct((span, widt...  17.5 us
    pallas_call x9, Pallas kernels, call(): pl.pallas_call(kernel, out_shape=tuple((jax.ShapeDtypeStruct(*shape) for...  16.2 us
    pallas_call x1, Pallas kernels, weight_grads(): pl.pallas_call(weight_grads_kernel, grid=(d // tile,), out_shape=jax.Shap...  16.2 us
  transfers between devices with their start and end apart: 62, of which 29 were waited for; matrix products, arithmetic and copies ran while one was open for 5% of the time, Pallas kernels for 23%

commit v1 on v0

--- a/solution.py
+++ b/solution.py
@@ -783,7 +783,7 @@
             pltpu.VMEM((n * span, HD), F32),
         ],
         compiler_params=params(40),
-        cost_estimate=cost(1000 * 580_000_000 if first else 0, 1 << 20),
+        cost_estimate=cost(110 * 580_000_000 if first else 0, 1 << 20),
         name="attend_back",
     )(*operands)
 
@@ -874,15 +874,16 @@
     cot_near = jnp.concatenate([cotangent, cot_yl], 0)
     cot_far = swap(cot_near, "yh")
     other_mlp = swap(after(pick(shard_mlp, place("yh", 1), 0), kv_block), "yh")
-    mlp_pair = join_sides(pick(shard_mlp, place("yh"), 0), after(other_mlp, first_whole, blocks[1:], cot_yl))
+    mlp_pair = join_sides(pick(shard_mlp, place("yh"), 0), after(other_mlp, first_whole, blocks[1:], cot_near))
     mlp_whole = lax.all_gather(mlp_pair, ("z", "x"), axis=0, tiled=True)
     odd = place("yl").astype(jnp.int32).reshape(1, 1)
     mixed, log_total = attend(queries, blocks, window)
 
-    cotangents = jnp.concatenate([cot_near, after(cot_far, log_total)], 0)
+    cot_far = after(cot_far, log_total)
+    cotangents = jnp.concatenate([after(cot_near, log_total), cot_far], 0)
     all_heads = (0, width_q)
     attn_rows = rows_out(
-        [after(mixed, cotangents)], [(first_whole, width_q, width_q)], [(0, all_heads, 0, all_heads)],
+        [after(mixed, cot_far)], [(first_whole, width_q, width_q)], [(0, all_heads, 0, all_heads)],
         1024, [(0,), (2,), (1, 3)], 24,
     )
     cotangents = [cotangents, swap(cotangents, "core")]
@@ -927,16 +928,16 @@
     arriving = [
         shift(far_grads[(d - 1) * span : d * span], "x", -d) for d in range(1, SEQ_DEVS)
     ]
-    out_arrived = [after(shift(out_parts[n], "z", n), query_part) for n in (1, 2, 3)]
+    out_arrived = [shift(out_parts[n], "z", n) for n in (2, 1, 3)]
     query_raw_grad, own_grads = attend_back(
-        (0,), after(queries, mlp_far, out_arrived), blocks[:1], window, log_total, (grad_turned, delta, query_part), turn=[cos, sin]
-    )
-
-    out_sum = total(out_parts[0].astype(F32), out_arrived).astype(BF)
+        (0,), after(queries, mlp_far), blocks[:1], window, log_total, (grad_turned, delta, query_part), turn=[cos, sin]
+    )
+
+    out_sum = total(out_parts[0].astype(F32), after(out_arrived, query_raw_grad)).astype(BF)
     output = settle(
         middle, [mlp_own, mlp_arrived[:quarter], after(swap(mlp_far, "yh"), query_raw_grad)], BF
     )
-    a_parts = wide_parts([scaled_in], after(query_raw_grad, arriving), (0, cut), "x")
+    a_parts = wide_parts([scaled_in], after(query_raw_grad, arriving, out_arrived), (0, cut), "x")
     a_arrived = [shift(a_parts[n], "x", n) for n in (2, 1, 3)]
     kv_raw_grad, *b_parts = last_parts(
         scaled_in, after(query_raw_grad, a_parts), cut, own_grads, arriving, cos, sin, "z"

time: 418 us -> 401 us (0.959)
  waiting for transfers between devices: 119 us -> 107 us
  local copies, waits for them, and re-layouts: 22.9 us -> 30.9 us
  starting transfers between devices: 92.4 us -> 86.2 us
    ppermute x59, waiting for transfers between devices: 115 us -> 103 us  [shift(): lax.ppermute(block, axis, [(i, (i + distance) % n) for i in range(n)])]
    ppermute x59, starting transfers between devices: 92.3 us -> 86 us  [shift(): lax.ppermute(block, axis, [(i, (i + distance) % n) for i in range(n)])]
    unnamed x130 -> x162, local copies, waits for them, and re-layouts: 16.1 us -> 22.2 us
  transfers between devices with their start and end apart: 62 -> 62, of which waited for: 29 -> 25; matrix products, arithmetic and copies ran while one was open for 5% -> 5% of each run, Pallas kernels for 23% -> 24%
where the time goes in v1:
time: 401 us; the launch traced here: 394 us
  Pallas kernels  128 us (32%)
  waiting for transfers between devices  107 us (27%)
  starting transfers between devices  86.2 us (21%)
  local copies, waits for them, and re-layouts  30.9 us (8%)
  between operations  15.3 us (4%)
  blocking collectives  13.4 us (3%)
  other arithmetic  13.1 us (3%)
    ppermute x59, waiting for transfers between devices, shift(): lax.ppermute(block, axis, [(i, (i + distance) % n) for i in range(n)])  103 us
    ppermute x59, starting transfers between devices, shift(): lax.ppermute(block, axis, [(i, (i + distance) % n) for i in range(n)])  86 us
    pallas_call x2, Pallas kernels, attend_back(): pl.pallas_call(functools.partial(attend_back_kernel, distances, first, la...  27 us
    unnamed x162, local copies, waits for them, and re-layouts  22.2 us
    pallas_call x1, Pallas kernels, hidden_units(): pl.pallas_call(functools.partial(hidden_kernel, width), out_shape=(jax.Sh...  20.1 us
    pallas_call x3, Pallas kernels, rows_out(): pl.pallas_call(functools.partial(rows_out_kernel, terms, places), grid=(d...  19.5 us
    pallas_call x1, Pallas kernels, attend(): pl.pallas_call(attend_kernel, out_shape=(jax.ShapeDtypeStruct((span, widt...  16.3 us
    pallas_call x1, Pallas kernels, weight_grads(): pl.pallas_call(weight_grads_kernel, grid=(d // tile,), out_shape=jax.Shap...  16.2 us
  transfers between devices with their start and end apart: 62, of which 25 were waited for; matrix products, arithmetic and copies ran while one was open for 5% of the time, Pallas kernels for 24%

profile of v1, /device:TPU:1, one launch (start us, length us, event | category | flops | bytes accessed | tf_op | source)
XLA Modules:
  0.0 393.6 jit_solution(15717524206979044062)
XLA Ops:
  8.1 3.8 collective-permute-start.10
  11.9 2.9 pack.1
  17.3 3.0 collective-permute-start
  22.7 2.6 collective-permute-start.5
  25.3 1.7 collective-permute-start.6
  28.3 2.0 collective-permute-done.4
  30.4 1.7 collective-permute-start.7
  32.4 4.4 %collective-permute-start.1 = (bf16[128,2048]{1,0:T(8,128)(2,1)S(1)}, bf16[128,2048]{1,0:T(8,128)(2,1)S(1)}, u32[]{:S(2)}, u32[]{:S(2)}) collective-permute-start(bf16[128,2048]{1,0:T(8,128)(2,1)S(1)} %copy-done.7), channel_id=1, source_target_pairs={{0,1},{1,0},{2,3},{3,2},{4,5},{5,4},{6,7},{7,6},{8,9},{9,8},{10,11... | collective-permute-start | bytes 1572872 | tf_op jit(solution)/shard_map/ppermute | solution.py:31
  36.8 4.0 %collective-permute-start.9 = (bf16[4,128,256]{2,1,0:T(8,128)(2,1)S(1)}, bf16[4,128,256]{2,1,0:T(8,128)(2,1)S(1)}, u32[]{:S(2)}, u32[]{:S(2)}) collective-permute-start(bf16[4,128,256]{2,1,0:T(8,128)(2,1)S(1)} %bitcast_dynamic-update-slice_fusion.4), channel_id=1, source_target_pairs={{0,32},{16,48},{32,0},{48,16},{1,33},{17,49},{33,1},{49,17},{2,34}... | collective-permute-start | bytes 786440 | tf_op jit(solution)/shard_map/ppermute | solution.py:31
  41.8 11.6 %collective-permute-done.8 = bf16[4,128,256]{2,1,0:T(8,128)(2,1)S(1)} collective-permute-done((bf16[4,128,256]{2,1,0:T(8,128)(2,1)S(1)}, bf16[4,128,256]{2,1,0:T(8,128)(2,1)S(1)}, u32[]{:S(2)}, u32[]{:S(2)}) %collective-permute-start.8) | collective-permute-done | bytes 262176 | tf_op jit(solution)/shard_map/ppermute | solution.py:31
  59.3 2.7 collective-permute-start.26
  62.8 2.2 collective-permute-start.13
  65.6 4.7 %collective-permute-done.14 = bf16[128,2048]{1,0:T(8,128)(2,1)} collective-permute-done((bf16[128,2048]{1,0:T(8,128)(2,1)S(1)}, bf16[128,2048]{1,0:T(8,128)(2,1)}, u32[]{:S(2)}, u32[]{:S(2)}) %collective-permute-start.14) | collective-permute-done | bytes 524320 | tf_op jit(solution)/shard_map/ppermute | solution.py:31
  70.3 1.9 constant_dynamic-update-slice_fusion
  74.3 2.1 collective-permute-done.11.refs_1_.refs_0_
  77.1 1.5 collective-permute-done.26
  78.6 4.3 %all-gather.3.cloned.1.call-done.w_ref.refs_1_.refs_7_.refs_2_ = bf16[2048,1024]{1,0:T(8,128)(2,1)} async-done(((bf16[128,1024]{1,0:T(8,128)(2,1)}), bf16[2048,1024]{1,0:T(8,128)(2,1)}) %all-gather.3.cloned.1.call-update) | async-done | bytes 4194320 | tf_op jit(solution)/shard_map/all_gather | solution.py:848
  85.6 2.8 collective-permute-start.15
  88.4 2.2 copy-done.2
  90.6 1.5 queries.1.q_ref
  92.1 16.3 %attend.1 = (bf16[512,512]{1,0:T(8,128)(2,1)S(1)}, f32[8,512]{1,0:T(8,128)S(1)}) custom-call(bf16[512,512]{1,0:T(8,128)(2,1)S(1)} %queries.1.q_ref, bf16[512,128]{1,0:T(8,128)(2,1)S(1)} %get-tuple-element.103.refs_0_, bf16[512,128]{1,0:T(8,128)(2,1)S(1)} %copy-done.47, bf16[512,128]{1,0:T(8,128)(2,1)S(1)} %copy-done.44, bf16[512,128]{1,0:T(8,128)(2,1)S(1)} %copy-done.41, ...), custom_call_target="tpu_custom_call" | custom-call | flops 34800001024 | bytes 2097152 | tf_op jit(solution)/shard_map/attend/pallas_call | solution.py:736
  108.5 2.9 collective-permute-done.15
  111.4 1.8 rows_out.3
  113.2 1.9 collective-permute-start.16
  118.9 11.9 %collective-permute-done.17.refs_2_ = bf16[128,2048]{1,0:T(8,128)(2,1)S(1)} collective-permute-done((bf16[128,2048]{1,0:T(8,128)(2,1)S(1)}, bf16[128,2048]{1,0:T(8,128)(2,1)S(1)}, u32[]{:S(2)}, u32[]{:S(2)}) %collective-permute-start.17) | collective-permute-done | bytes 524320 | tf_op jit(solution)/shard_map/ppermute | solution.py:31
  132.9 2.1 collective-permute-start.20
  136.3 2.0 collective-permute-start.21
  138.3 7.5 %collective-permute-done.20.refs_3_ = bf16[128,2048]{1,0:T(8,128)(2,1)} collective-permute-done((bf16[128,2048]{1,0:T(8,128)(2,1)}, bf16[128,2048]{1,0:T(8,128)(2,1)}, u32[]{:S(2)}, u32[]{:S(2)}) %collective-permute-start.20) | collective-permute-done | bytes 524320 | tf_op jit(solution)/shard_map/ppermute | solution.py:31
  145.9 12.9 %collective-permute-start.24 = (bf16[128,2048]{1,0:T(8,128)(2,1)}, bf16[128,2048]{1,0:T(8,128)(2,1)}, u32[]{:S(2)}, u32[]{:S(2)}) collective-permute-start(bf16[128,2048]{1,0:T(8,128)(2,1)} %collective-permute-done.20.refs_3_), channel_id=1, source_target_pairs={{0,1},{1,0},{2,3},{3,2},{4,5},{5,4},{6,7},{7,6},{8,9},{9,8},{10,11... | collective-permute-start | bytes 1572872 | tf_op jit(solution)/shard_map/ppermute | solution.py:31
  158.8 3.2 collective-permute-done.18.refs_1_
  162.9 1.9 collective-permute-done.22.refs_5_
  164.7 20.1 %hidden_units.1 = (bf16[1024,768]{1,0:T(8,128)(2,1)}, bf16[1024,1408]{1,0:T(8,128)(2,1)}) custom-call(s32[1,1]{1,0:T(1,128)} %bitcast.18.odd_ref, bf16[128,2048]{1,0:T(8,128)(2,1)} %get-tuple-element.128.refs_0_, bf16[128,2048]{1,0:T(8,128)(2,1)} %collective-permute-done.18.refs_1_, bf16[128,2048]{1,0:T(8,128)(2,1)} %collective-permute-done.19.refs_2_, ...), custom_call_target="tpu_custom_call" | custom-call | flops 8053063680 | bytes 7864320 | tf_op jit(solution)/shard_map/hidden_units/pallas_call | solution.py:610
  184.9 10.5 %rows_out.4 = (bf16[512,2048]{1,0:T(8,128)(2,1)}, bf16[512,2048]{1,0:T(8,128)(2,1)}) custom-call(bf16[1024,1408]{1,0:T(8,128)(2,1)} %get-tuple-element.122.refs_0_.refs_10_, bf16[2048,2176]{1,0:T(8,128)(2,1)} %all-gather.5.cloned.1.call-done.refs_10_.refs_1_), custom_call_target="tpu_custom_call" | custom-call | flops 5905580032 | bytes 6291456 | tf_op jit(solution)/shard_map/rows_out/pallas_call | solution.py:667
  196.0 4.0 %collective-permute-done.27.two_ref = bf16[512,2048]{1,0:T(8,128)(2,1)S(1)} collective-permute-done((bf16[512,2048]{1,0:T(8,128)(2,1)}, bf16[512,2048]{1,0:T(8,128)(2,1)S(1)}, u32[]{:S(2)}, u32[]{:S(2)}) %collective-permute-start.27) | collective-permute-done | bytes 2097184 | tf_op jit(solution)/shard_map/ppermute | solution.py:31
  200.0 1.6 copy-done.13
  201.5 1.4 add_pieces.1
  205.7 16.2 %weight_grads.1 = bf16[2048,2176]{1,0:T(8,128)(2,1)} custom-call(s32[1,1]{1,0:T(1,128)} %bitcast.18.odd_ref, bf16[128,2048]{1,0:T(8,128)(2,1)} %get-tuple-element.128.refs_0_, bf16[128,2048]{1,0:T(8,128)(2,1)} %collective-permute-done.18.refs_1_, bf16[128,2048]{1,0:T(8,128)(2,1)} %collective-permute-done.19.refs_2_, ...), custom_call_target="tpu_custom_call" | custom-call | flops 9126805504 | bytes 17301504 | tf_op jit(solution)/shard_map/weight_grads/pallas_call | solution.py:796
  222.0 7.2 %rows_out.5 = (bf16[512,2048]{1,0:T(8,128)(2,1)}, bf16[512,2048]{1,0:T(8,128)(2,1)}) custom-call(bf16[1024,768]{1,0:T(8,128)(2,1)} %get-tuple-element.129.refs_11_.refs_0_, bf16[2048,2176]{1,0:T(8,128)(2,1)} %all-gather.5.cloned.1.call-done.refs_10_.refs_1_), custom_call_target="tpu_custom_call" | custom-call | flops 3221225472 | bytes 6291456 | tf_op jit(solution)/shard_map/rows_out/pallas_call | solution.py:667
  229.2 2.5 collective-permute-done.29.refs_2_
  231.7 3.1 middle_grad.1
  236.3 13.8 %collective-permute-done.33.refs_2_.refs_10_ = bf16[128,2048]{1,0:T(8,128)(2,1)S(1)} collective-permute-done((bf16[128,2048]{1,0:T(8,128)(2,1)}, bf16[128,2048]{1,0:T(8,128)(2,1)S(1)}, u32[]{:S(2)}, u32[]{:S(2)}) %collective-permute-start.33) | collective-permute-done | bytes 524320 | tf_op jit(solution)/shard_map/ppermute | solution.py:31
  254.6 2.8 wide_parts.2
  257.4 1.9 collective-permute-start.41
  259.4 2.6 collective-permute-start.40
  263.0 2.5 pair_pieces.1
  267.7 20.3 %attend_back.2 = (f32[512,512]{1,0:T(8,128)S(1)}, bf16[1536,128]{1,0:T(8,128)(2,1)S(1)}, bf16[512,512]{1,0:T(8,128)(2,1)S(1)}, f32[8,512]{1,0:T(8,128)S(1)}) custom-call(bf16[512,512]{1,0:T(8,128)(2,1)S(1)} %copy-done.16, bf16[512,128]{1,0:T(8,128)(2,1)S(1)} %copy-done.48, bf16[512,128]{1,0:T(8,128)(2,1)S(1)} %copy-done.45, bf16[512,128]{1,0:T(8,128)(2,1)S(1)} %copy-done.42, ...), custom_call_target="tpu_custom_call" | custom-call | flops 127600001024 | bytes 1048576 | tf_op jit(solution)/shard_map/attend_back/pallas_call | solution.py:773
  288.1 2.5 collective-permute-done.35
  293.6 6.7 %attend_back.3 = (bf16[512,512]{1,0:T(8,128)(2,1)S(1)}, f32[512,128]{1,0:T(8,128)S(1)}) custom-call(bf16[512,512]{1,0:T(8,128)(2,1)S(1)} %copy-done.16, bf16[512,128]{1,0:T(8,128)(2,1)S(1)} %get-tuple-element.103.refs_0_, s32[1,1]{1,0:T(1,128)} %bitcast.16.refs_4_.refs_3_.refs_1_, s32[1,512]{1,0:T(1,128)S(1)} %bitcast.82, ...), custom_call_target="tpu_custom_call" | custom-call | bytes 1048576 | tf_op jit(solution)/shard_map/attend_back/pallas_call | solution.py:773
  304.4 1.5 collective-permute-start.44
  305.9 2.4 collective-permute-start.43
  309.2 2.0 collective-permute-done.46
  312.1 5.0 %rows_grad.1 = (bf16[128,2048]{1,0:T(8,128)(2,1)S(1)}, bf16[128,2048]{1,0:T(8,128)(2,1)S(1)}, bf16[256,2048]{1,0:T(8,128)(2,1)}) custom-call(bf16[512,512]{1,0:T(8,128)(2,1)S(1)} %get-tuple-element.161.refs_1_.dq_ref.refs_0_, bf16[512,128]{1,0:T(8,128)(2,1)S(1)} %get-tuple-element.163.refs_1_, bf16[2048,1024]{1,0:T(8,128)(2,1)S(1)} %copy-done.4, ...), custom_call_target="tpu_custom_call" | custom-call | tf_op jit(solution)/shard_map/rows_grad/pallas_call | solution.py:647
  317.1 2.4 collective-permute-done.47
  319.5 2.4 collective-permute-done.48
  321.9 11.1 %collective-permute-done.43 = bf16[512,384]{1,0:T(8,128)(2,1)S(1)} collective-permute-done((bf16[512,384]{1,0:T(8,128)(2,1)S(1)}, bf16[512,384]{1,0:T(8,128)(2,1)S(1)}, u32[]{:S(2)}, u32[]{:S(2)}) %collective-permute-start.43) | collective-permute-done | bytes 393248 | tf_op jit(solution)/shard_map/ppermute | solution.py:31
  333.9 2.8 collective-permute-start.49
  337.9 1.8 collective-permute-start.36
  339.7 1.5 add_convert_fusion
  345.2 2.9 collective-permute-start.53
  350.0 2.5 collective-permute-done.53
  352.5 1.5 collective-permute-start.56
  356.4 7.2 %collective-permute-done.50.refs_2_ = bf16[128,2048]{1,0:T(8,128)(2,1)S(1)} collective-permute-done((bf16[128,2048]{1,0:T(8,128)(2,1)S(1)}, bf16[128,2048]{1,0:T(8,128)(2,1)S(1)}, u32[]{:S(2)}, u32[]{:S(2)}) %collective-permute-start.50) | collective-permute-done | bytes 524320 | tf_op jit(solution)/shard_map/ppermute | solution.py:31
  366.1 2.8 collective-permute-start.58
  370.9 13.4 %psum.7 = f32[2,2,64]{2,1,0:T(2,128)S(1)} all-reduce(f32[2,2,64]{2,1,0:T(2,128)S(1)} %reshape.102), channel_id=1, replica_groups=mesh['yh'=2,'z'=4,'x'=4,'yl'=2,'core'=2] {'yh','yl','core'}, use_global_device_ids=true, to_apply=%region_3.4 | all-reduce | flops 256 | bytes 2048 | tf_op jit(solution)/shard_map/psum | solution.py:985
  (300 shorter events, 67.1 us)
Async XLA Ops:
  7.2 75.6 %all-gather.3.cloned.1.call-start = ((), (), s32[]{:S(2)}) async-start(), calls=%async_computation.1 | async-start | bytes 4456448 | tf_op jit(solution)/shard_map/all_gather | solution.py:848
  8.1 6.8 %collective-permute-start.10 = (bf16[64,1024]{1,0:T(8,128)(2,1)S(1)}, bf16[64,1024]{1,0:T(8,128)(2,1)S(1)}, u32[]{:S(2)}, u32[]{:S(2)}) collective-permute-start(bf16[64,1024]{1,0:T(8,128)(2,1)S(1)} %pad_maximum_fusion.4), channel_id=1, source_target_pairs={{0,64},{64,0},{1,65},{65,1},{2,66},{66,2},{3,67},{67,3},{4,68},{68... | collective-permute-start | bytes 393224 | tf_op jit(solution)/shard_map/ppermute | solution.py:31
  17.3 147.5 %all-gather.5.cloned.1.call-start = ((), (), s32[]{:S(2)}) async-start(), calls=%async_computation.2 | async-start | bytes 9469952 | tf_op jit(solution)/shard_map/all_gather | solution.py:878
  17.3 4.6 %collective-permute-start = (bf16[64,256]{1,0:T(8,128)(2,1)}, bf16[64,256]{1,0:T(8,128)(2,1)S(1)}, u32[]{:S(2)}, u32[]{:S(2)}) collective-permute-start(bf16[64,256]{1,0:T(8,128)(2,1)} %get-tuple-element.99), channel_id=1, source_target_pairs={{0,64},{64,0},{1,65},{65,1},{2,66},{66,2},{3,67},{67,3},{4,68},{68... | collective-permute-start | bytes 98312 | tf_op jit(solution)/shard_map/ppermute | solution.py:31
  22.7 7.6 %collective-permute-start.5 = (bf16[128,256]{1,0:T(8,128)(2,1)S(1)}, bf16[128,256]{1,0:T(8,128)(2,1)S(1)}, u32[]{:S(2)}, u32[]{:S(2)}) collective-permute-start(bf16[128,256]{1,0:T(8,128)(2,1)S(1)} %pad_maximum_fusion.5), channel_id=1, source_target_pairs={{0,12},{4,0},{8,4},{12,8},{1,13},{5,1},{9,5},{13,9},{2,14},{6,2},{... | collective-permute-start | bytes 196616 | tf_op jit(solution)/shard_map/ppermute | solution.py:31
  25.3 5.0 %collective-permute-start.4 = (bf16[128,256]{1,0:T(8,128)(2,1)S(1)}, bf16[128,256]{1,0:T(8,128)(2,1)S(1)}, u32[]{:S(2)}, u32[]{:S(2)}) collective-permute-start(bf16[128,256]{1,0:T(8,128)(2,1)S(1)} %pad_maximum_fusion.5), channel_id=1, source_target_pairs={{0,4},{4,8},{8,12},{12,0},{1,5},{5,9},{9,13},{13,1},{2,6},{6,10},{... | collective-permute-start | bytes 196616 | tf_op jit(solution)/shard_map/ppermute | solution.py:31
  25.3 5.1 %collective-permute-start.6 = (bf16[128,256]{1,0:T(8,128)(2,1)S(1)}, bf16[128,256]{1,0:T(8,128)(2,1)S(1)}, u32[]{:S(2)}, u32[]{:S(2)}) collective-permute-start(bf16[128,256]{1,0:T(8,128)(2,1)S(1)} %pad_maximum_fusion.5), channel_id=1, source_target_pairs={{0,8},{4,12},{8,0},{12,4},{1,9},{5,13},{9,1},{13,5},{2,10},{6,14},... | collective-permute-start | bytes 196616 | tf_op jit(solution)/shard_map/ppermute | solution.py:31
  27.0 14.0 %collective-permute-start.2 = (bf16[128,2048]{1,0:T(8,128)(2,1)}, bf16[128,2048]{1,0:T(8,128)(2,1)S(1)}, u32[]{:S(2)}, u32[]{:S(2)}) collective-permute-start(bf16[128,2048]{1,0:T(8,128)(2,1)} %get-tuple-element.100.refs_0_.base_ref.refs_4_), channel_id=1, source_target_pairs={{0,2},{2,0},{1,3},{3,1},{4,6},{6,4},{5,7},{7,5},{8,10},{10,8},{9,1... | collective-permute-start | bytes 1572872 | tf_op jit(solution)/shard_map/ppermute | solution.py:31
  30.4 11.4 %collective-permute-start.7 = (bf16[4,128,256]{2,1,0:T(8,128)(2,1)S(1)}, bf16[4,128,256]{2,1,0:T(8,128)(2,1)S(1)}, u32[]{:S(2)}, u32[]{:S(2)}) collective-permute-start(bf16[4,128,256]{2,1,0:T(8,128)(2,1)S(1)} %bitcast_dynamic-update-slice_fusion.4), channel_id=1, source_target_pairs={{0,16},{16,32},{32,48},{48,0},{1,17},{17,33},{33,49},{49,1},{2,18}... | collective-permute-start | bytes 786440 | tf_op jit(solution)/shard_map/ppermute | solution.py:31
  32.4 21.0 %collective-permute-start.1 = (bf16[128,2048]{1,0:T(8,128)(2,1)S(1)}, bf16[128,2048]{1,0:T(8,128)(2,1)S(1)}, u32[]{:S(2)}, u32[]{:S(2)}) collective-permute-start(bf16[128,2048]{1,0:T(8,128)(2,1)S(1)} %copy-done.7), channel_id=1, source_target_pairs={{0,1},{1,0},{2,3},{3,2},{4,5},{5,4},{6,7},{7,6},{8,9},{9,8},{10,11... | collective-permute-start | bytes 1572872 | tf_op jit(solution)/shard_map/ppermute | solution.py:31
  36.8 16.6 %collective-permute-start.9 = (bf16[4,128,256]{2,1,0:T(8,128)(2,1)S(1)}, bf16[4,128,256]{2,1,0:T(8,128)(2,1)S(1)}, u32[]{:S(2)}, u32[]{:S(2)}) collective-permute-start(bf16[4,128,256]{2,1,0:T(8,128)(2,1)S(1)} %bitcast_dynamic-update-slice_fusion.4), channel_id=1, source_target_pairs={{0,32},{16,48},{32,0},{48,16},{1,33},{17,49},{33,1},{49,17},{2,34}... | collective-permute-start | bytes 786440 | tf_op jit(solution)/shard_map/ppermute | solution.py:31
  40.8 12.5 %collective-permute-start.8 = (bf16[4,128,256]{2,1,0:T(8,128)(2,1)S(1)}, bf16[4,128,256]{2,1,0:T(8,128)(2,1)S(1)}, u32[]{:S(2)}, u32[]{:S(2)}) collective-permute-start(bf16[4,128,256]{2,1,0:T(8,128)(2,1)S(1)} %bitcast_dynamic-update-slice_fusion.4), channel_id=1, source_target_pairs={{0,48},{16,0},{32,16},{48,32},{1,49},{17,1},{33,17},{49,33},{2,50}... | collective-permute-start | bytes 786440 | tf_op jit(solution)/shard_map/ppermute | solution.py:31
  41.0 12.4 %collective-permute-start.3 = (bf16[128,2048]{1,0:T(8,128)(2,1)S(1)}, bf16[128,2048]{1,0:T(8,128)(2,1)S(1)}, u32[]{:S(2)}, u32[]{:S(2)}) collective-permute-start(bf16[128,2048]{1,0:T(8,128)(2,1)S(1)} %collective-permute-done.2.refs_2_.refs_6_), channel_id=1, source_target_pairs={{0,1},{1,0},{2,3},{3,2},{4,5},{5,4},{6,7},{7,6},{8,9},{9,8},{10,11... | collective-permute-start | bytes 1572872 | tf_op jit(solution)/shard_map/ppermute | solution.py:31
  57.3 12.9 %collective-permute-start.14 = (bf16[128,2048]{1,0:T(8,128)(2,1)S(1)}, bf16[128,2048]{1,0:T(8,128)(2,1)}, u32[]{:S(2)}, u32[]{:S(2)}) collective-permute-start(bf16[128,2048]{1,0:T(8,128)(2,1)S(1)} %copy-done.14), channel_id=1, source_target_pairs={{0,2},{2,0},{1,3},{3,1},{4,6},{6,4},{5,7},{7,5},{8,10},{10,8},{9,1... | collective-permute-start | bytes 1572872 | tf_op jit(solution)/shard_map/ppermute | solution.py:31
  59.3 19.3 %collective-permute-start.26 = (bf16[64,2176]{1,0:T(8,128)(2,1)}, bf16[64,2176]{1,0:T(8,128)(2,1)}, u32[]{:S(2)}, u32[]{:S(2)}) collective-permute-start(bf16[64,2176]{1,0:T(8,128)(2,1)} %dynamic-slice_bitcast_fusion.1), channel_id=1, source_target_pairs={{0,64},{64,0},{1,65},{65,1},{2,66},{66,2},{3,67},{67,3},{4,68},{68... | collective-permute-start | bytes 835592 | tf_op jit(solution)/shard_map/ppermute | solution.py:31
  62.8 9.4 %collective-permute-start.13 = (bf16[512,128]{1,0:T(8,128)(2,1)S(1)}, bf16[512,128]{1,0:T(8,128)(2,1)S(1)}, u32[]{:S(2)}, u32[]{:S(2)}) collective-permute-start(bf16[512,128]{1,0:T(8,128)(2,1)S(1)} %get-tuple-element.103.refs_0_), channel_id=1, source_target_pairs={{0,12},{4,0},{8,4},{12,8},{1,13},{5,1},{9,5},{13,9},{2,14},{6,2},{... | collective-permute-start | bytes 393224 | tf_op jit(solution)/shard_map/ppermute | solution.py:31
  65.0 8.7 %collective-permute-start.12 = (bf16[512,128]{1,0:T(8,128)(2,1)S(1)}, bf16[512,128]{1,0:T(8,128)(2,1)S(1)}, u32[]{:S(2)}, u32[]{:S(2)}) collective-permute-start(bf16[512,128]{1,0:T(8,128)(2,1)S(1)} %get-tuple-element.103.refs_0_), channel_id=1, source_target_pairs={{0,8},{4,12},{8,0},{12,4},{1,9},{5,13},{9,1},{13,5},{2,10},{6,14},... | collective-permute-start | bytes 393224 | tf_op jit(solution)/shard_map/ppermute | solution.py:31
  65.0 11.4 %collective-permute-start.11 = (bf16[512,128]{1,0:T(8,128)(2,1)S(1)}, bf16[512,128]{1,0:T(8,128)(2,1)S(1)}, u32[]{:S(2)}, u32[]{:S(2)}) collective-permute-start(bf16[512,128]{1,0:T(8,128)(2,1)S(1)} %get-tuple-element.103.refs_0_), channel_id=1, source_target_pairs={{0,4},{4,8},{8,12},{12,0},{1,5},{5,9},{9,13},{13,1},{2,6},{6,10},{... | collective-permute-start | bytes 393224 | tf_op jit(solution)/shard_map/ppermute | solution.py:31
  85.6 279.4 %reduce-scatter.2.cloned.1.call-start = ((), (), s32[]{:S(2)}) async-start(), calls=%async_computation.3 | async-start | bytes 9469952 | tf_op jit(solution)/shard_map/reduce_scatter | solution.py:913
  85.6 25.8 %collective-permute-start.15 = (bf16[256,2048]{1,0:T(8,128)(2,1)}, bf16[256,2048]{1,0:T(8,128)(2,1)S(1)}, u32[]{:S(2)}, u32[]{:S(2)}) collective-permute-start(bf16[256,2048]{1,0:T(8,128)(2,1)} %constant_dynamic-update-slice_fusion), channel_id=1, source_target_pairs={{0,64},{64,0},{1,65},{65,1},{2,66},{66,2},{3,67},{67,3},{4,68},{68... | collective-permute-start | bytes 3145736 | tf_op jit(solution)/shard_map/ppermute | solution.py:31
  113.2 4.2 %collective-permute-start.16 = (bf16[256,2048]{1,0:T(8,128)(2,1)S(1)}, bf16[256,2048]{1,0:T(8,128)(2,1)S(1)}, u32[]{:S(2)}, u32[]{:S(2)}) collective-permute-start(bf16[256,2048]{1,0:T(8,128)(2,1)S(1)} %get-tuple-element.112), channel_id=1, source_target_pairs={{0,1},{1,0},{2,3},{3,2},{4,5},{5,4},{6,7},{7,6},{8,9},{9,8},{10,11... | collective-permute-start | bytes 3145736 | tf_op jit(solution)/shard_map/ppermute | solution.py:31
  117.3 45.5 %collective-permute-start.25 = (bf16[512,2048]{1,0:T(8,128)(2,1)}, bf16[512,2048]{1,0:T(8,128)(2,1)}, u32[]{:S(2)}, u32[]{:S(2)}) collective-permute-start(bf16[512,2048]{1,0:T(8,128)(2,1)} %constant_dynamic-update-slice_fusion.2.refs_8_), channel_id=1, source_target_pairs={{0,1},{1,0},{2,3},{3,2},{4,5},{5,4},{6,7},{7,6},{8,9},{9,8},{10,11... | collective-permute-start | bytes 6291464 | tf_op jit(solution)/shard_map/ppermute | solution.py:31
  117.5 13.2 %collective-permute-start.17 = (bf16[128,2048]{1,0:T(8,128)(2,1)S(1)}, bf16[128,2048]{1,0:T(8,128)(2,1)S(1)}, u32[]{:S(2)}, u32[]{:S(2)}) collective-permute-start(bf16[128,2048]{1,0:T(8,128)(2,1)S(1)} %add_convert_fusion.3), channel_id=1, source_target_pairs={{0,2},{2,0},{1,3},{3,1},{4,6},{6,4},{5,7},{7,5},{8,10},{10,8},{9,1... | collective-permute-start | bytes 1572872 | tf_op jit(solution)/shard_map/ppermute | solution.py:31
  132.9 12.9 %collective-permute-start.20 = (bf16[128,2048]{1,0:T(8,128)(2,1)}, bf16[128,2048]{1,0:T(8,128)(2,1)}, u32[]{:S(2)}, u32[]{:S(2)}) collective-permute-start(bf16[128,2048]{1,0:T(8,128)(2,1)} %get-tuple-element.128.refs_0_), channel_id=1, source_target_pairs={{0,66},{2,0},{64,2},{66,64},{1,67},{3,1},{65,3},{67,65},{4,70},{6,... | collective-permute-start | bytes 1572872 | tf_op jit(solution)/shard_map/ppermute | solution.py:31
  135.1 23.7 %collective-permute-start.19 = (bf16[128,2048]{1,0:T(8,128)(2,1)}, bf16[128,2048]{1,0:T(8,128)(2,1)}, u32[]{:S(2)}, u32[]{:S(2)}) collective-permute-start(bf16[128,2048]{1,0:T(8,128)(2,1)} %get-tuple-element.128.refs_0_), channel_id=1, source_target_pairs={{0,64},{2,66},{64,0},{66,2},{1,65},{3,67},{65,1},{67,3},{4,68},{6,... | collective-permute-start | bytes 1572872 | tf_op jit(solution)/shard_map/ppermute | solution.py:31
  135.9 26.0 %collective-permute-start.18 = (bf16[128,2048]{1,0:T(8,128)(2,1)}, bf16[128,2048]{1,0:T(8,128)(2,1)}, u32[]{:S(2)}, u32[]{:S(2)}) collective-permute-start(bf16[128,2048]{1,0:T(8,128)(2,1)} %get-tuple-element.128.refs_0_), channel_id=1, source_target_pairs={{0,2},{2,64},{64,66},{66,0},{1,3},{3,65},{65,67},{67,1},{4,6},{6,6... | collective-permute-start | bytes 1572872 | tf_op jit(solution)/shard_map/ppermute | solution.py:31
  136.3 26.6 %collective-permute-start.21 = (bf16[128,2048]{1,0:T(8,128)(2,1)}, bf16[128,2048]{1,0:T(8,128)(2,1)}, u32[]{:S(2)}, u32[]{:S(2)}) collective-permute-start(bf16[128,2048]{1,0:T(8,128)(2,1)} %get-tuple-element.128.refs_0_), channel_id=1, source_target_pairs={{0,1},{1,0},{2,3},{3,2},{4,5},{5,4},{6,7},{7,6},{8,9},{9,8},{10,11... | collective-permute-start | bytes 1572872 | tf_op jit(solution)/shard_map/ppermute | solution.py:31
  145.9 17.0 %collective-permute-start.24 = (bf16[128,2048]{1,0:T(8,128)(2,1)}, bf16[128,2048]{1,0:T(8,128)(2,1)}, u32[]{:S(2)}, u32[]{:S(2)}) collective-permute-start(bf16[128,2048]{1,0:T(8,128)(2,1)} %collective-permute-done.20.refs_3_), channel_id=1, source_target_pairs={{0,1},{1,0},{2,3},{3,2},{4,5},{5,4},{6,7},{7,6},{8,9},{9,8},{10,11... | collective-permute-start | bytes 1572872 | tf_op jit(solution)/shard_map/ppermute | solution.py:31
  158.8 4.1 %collective-permute-start.23 = (bf16[128,2048]{1,0:T(8,128)(2,1)}, bf16[128,2048]{1,0:T(8,128)(2,1)}, u32[]{:S(2)}, u32[]{:S(2)}) collective-permute-start(bf16[128,2048]{1,0:T(8,128)(2,1)} %collective-permute-done.19.refs_2_), channel_id=1, source_target_pairs={{0,1},{1,0},{2,3},{3,2},{4,5},{5,4},{6,7},{7,6},{8,9},{9,8},{10,11... | collective-permute-start | bytes 1572872 | tf_op jit(solution)/shard_map/ppermute | solution.py:31
  162.0 2.8 collective-permute-start.22
  195.4 4.5 %collective-permute-start.27 = (bf16[512,2048]{1,0:T(8,128)(2,1)}, bf16[512,2048]{1,0:T(8,128)(2,1)S(1)}, u32[]{:S(2)}, u32[]{:S(2)}) collective-permute-start(bf16[512,2048]{1,0:T(8,128)(2,1)} %get-tuple-element.124), channel_id=1, source_target_pairs={{0,1},{1,0},{2,3},{3,2},{4,5},{5,4},{6,7},{7,6},{8,9},{9,8},{10,11... | collective-permute-start | bytes 6291464 | tf_op jit(solution)/shard_map/ppermute | solution.py:31
  203.9 25.2 %collective-permute-start.28 = (bf16[128,2048]{1,0:T(8,128)(2,1)}, bf16[128,2048]{1,0:T(8,128)(2,1)}, u32[]{:S(2)}, u32[]{:S(2)}) collective-permute-start(bf16[128,2048]{1,0:T(8,128)(2,1)} %get-tuple-element.125), channel_id=1, source_target_pairs={{0,66},{2,0},{64,2},{66,64},{1,67},{3,1},{65,3},{67,65},{4,70},{6,... | collective-permute-start | bytes 1572872 | tf_op jit(solution)/shard_map/ppermute | solution.py:31
  204.8 24.4 %collective-permute-start.30 = (bf16[128,2048]{1,0:T(8,128)(2,1)}, bf16[128,2048]{1,0:T(8,128)(2,1)}, u32[]{:S(2)}, u32[]{:S(2)}) collective-permute-start(bf16[128,2048]{1,0:T(8,128)(2,1)} %get-tuple-element.126), channel_id=1, source_target_pairs={{0,64},{2,66},{64,0},{66,2},{1,65},{3,67},{65,1},{67,3},{4,68},{6,... | collective-permute-start | bytes 1572872 | tf_op jit(solution)/shard_map/ppermute | solution.py:31
  205.1 26.5 %collective-permute-start.29 = (bf16[128,2048]{1,0:T(8,128)(2,1)}, bf16[128,2048]{1,0:T(8,128)(2,1)}, u32[]{:S(2)}, u32[]{:S(2)}) collective-permute-start(bf16[128,2048]{1,0:T(8,128)(2,1)} %get-tuple-element.127), channel_id=1, source_target_pairs={{0,2},{2,64},{64,66},{66,0},{1,3},{3,65},{65,67},{67,1},{4,6},{6,6... | collective-permute-start | bytes 1572872 | tf_op jit(solution)/shard_map/ppermute | solution.py:31
  235.8 27.2 %collective-permute-start.31 = (bf16[512,2048]{1,0:T(8,128)(2,1)}, bf16[512,2048]{1,0:T(8,128)(2,1)}, u32[]{:S(2)}, u32[]{:S(2)}) collective-permute-start(bf16[512,2048]{1,0:T(8,128)(2,1)} %get-tuple-element.137), channel_id=1, source_target_pairs={{0,1},{1,0},{2,3},{3,2},{4,5},{5,4},{6,7},{7,6},{8,9},{9,8},{10,11... | collective-permute-start | bytes 6291464 | tf_op jit(solution)/shard_map/ppermute | solution.py:31
  236.3 13.9 %collective-permute-start.33 = (bf16[128,2048]{1,0:T(8,128)(2,1)}, bf16[128,2048]{1,0:T(8,128)(2,1)S(1)}, u32[]{:S(2)}, u32[]{:S(2)}) collective-permute-start(bf16[128,2048]{1,0:T(8,128)(2,1)} %get-tuple-element.136.refs_0_.refs_8_), channel_id=1, source_target_pairs={{0,2},{2,0},{1,3},{3,1},{4,6},{6,4},{5,7},{7,5},{8,10},{10,8},{9,1... | collective-permute-start | bytes 1572872 | tf_op jit(solution)/shard_map/ppermute | solution.py:31
  236.3 15.4 %collective-permute-start.32 = (bf16[128,2048]{1,0:T(8,128)(2,1)}, bf16[128,2048]{1,0:T(8,128)(2,1)}, u32[]{:S(2)}, u32[]{:S(2)}) collective-permute-start(bf16[128,2048]{1,0:T(8,128)(2,1)} %get-tuple-element.136.refs_0_.refs_8_), channel_id=1, source_target_pairs={{0,1},{1,0},{2,3},{3,2},{4,5},{5,4},{6,7},{7,6},{8,9},{9,8},{10,11... | collective-permute-start | bytes 1572872 | tf_op jit(solution)/shard_map/ppermute | solution.py:31
  250.2 2.3 collective-permute-start.34
  257.4 34.0 %collective-permute-start.41 = (bf16[512,512]{1,0:T(8,128)(2,1)S(1)}, bf16[512,512]{1,0:T(8,128)(2,1)S(1)}, u32[]{:S(2)}, u32[]{:S(2)}) collective-permute-start(bf16[512,512]{1,0:T(8,128)(2,1)S(1)} %get-tuple-element.142), channel_id=1, source_target_pairs={{0,16},{16,32},{32,48},{48,0},{1,17},{17,33},{33,49},{49,1},{2,18}... | collective-permute-start | bytes 1572872 | tf_op jit(solution)/shard_map/ppermute | solution.py:31
  259.4 40.9 %collective-permute-start.40 = (bf16[512,512]{1,0:T(8,128)(2,1)S(1)}, bf16[512,512]{1,0:T(8,128)(2,1)S(1)}, u32[]{:S(2)}, u32[]{:S(2)}) collective-permute-start(bf16[512,512]{1,0:T(8,128)(2,1)S(1)} %get-tuple-element.143), channel_id=1, source_target_pairs={{0,32},{16,48},{32,0},{48,16},{1,33},{17,49},{33,1},{49,17},{2,34}... | collective-permute-start | bytes 1572872 | tf_op jit(solution)/shard_map/ppermute | solution.py:31
  262.0 38.3 %collective-permute-start.42 = (bf16[512,512]{1,0:T(8,128)(2,1)S(1)}, bf16[512,512]{1,0:T(8,128)(2,1)S(1)}, u32[]{:S(2)}, u32[]{:S(2)}) collective-permute-start(bf16[512,512]{1,0:T(8,128)(2,1)S(1)} %get-tuple-element.144), channel_id=1, source_target_pairs={{0,48},{16,0},{32,16},{48,32},{1,49},{17,1},{33,17},{49,33},{2,50}... | collective-permute-start | bytes 1572872 | tf_op jit(solution)/shard_map/ppermute | solution.py:31
  266.5 24.1 %collective-permute-start.35 = (bf16[256,2048]{1,0:T(8,128)(2,1)S(1)}, bf16[256,2048]{1,0:T(8,128)(2,1)S(1)}, u32[]{:S(2)}, u32[]{:S(2)}) collective-permute-start(bf16[256,2048]{1,0:T(8,128)(2,1)S(1)} %get-tuple-element.140), channel_id=1, source_target_pairs={{0,2},{2,0},{1,3},{3,1},{4,6},{6,4},{5,7},{7,5},{8,10},{10,8},{9,1... | collective-permute-start | bytes 3145736 | tf_op jit(solution)/shard_map/ppermute | solution.py:31
  288.0 12.3 %collective-permute-start.39 = (bf16[512,128]{1,0:T(8,128)(2,1)S(1)}, bf16[512,128]{1,0:T(8,128)(2,1)S(1)}, u32[]{:S(2)}, u32[]{:S(2)}) collective-permute-start(bf16[512,128]{1,0:T(8,128)(2,1)S(1)} %get-tuple-element.193), channel_id=1, source_target_pairs={{0,4},{4,8},{8,12},{12,0},{1,5},{5,9},{9,13},{13,1},{2,6},{6,10},{... | collective-permute-start | bytes 393224 | tf_op jit(solution)/shard_map/ppermute | solution.py:31
  290.6 9.7 %collective-permute-start.38 = (bf16[512,128]{1,0:T(8,128)(2,1)S(1)}, bf16[512,128]{1,0:T(8,128)(2,1)S(1)}, u32[]{:S(2)}, u32[]{:S(2)}) collective-permute-start(bf16[512,128]{1,0:T(8,128)(2,1)S(1)} %get-tuple-element.194), channel_id=1, source_target_pairs={{0,8},{4,12},{8,0},{12,4},{1,9},{5,13},{9,1},{13,5},{2,10},{6,14},... | collective-permute-start | bytes 393224 | tf_op jit(solution)/shard_map/ppermute | solution.py:31
  291.4 9.0 %collective-permute-start.37 = (bf16[512,128]{1,0:T(8,128)(2,1)S(1)}, bf16[512,128]{1,0:T(8,128)(2,1)S(1)}, u32[]{:S(2)}, u32[]{:S(2)}) collective-permute-start(bf16[512,128]{1,0:T(8,128)(2,1)S(1)} %get-tuple-element.195), channel_id=1, source_target_pairs={{0,12},{4,0},{8,4},{12,8},{1,13},{5,1},{9,5},{13,9},{2,14},{6,2},{... | collective-permute-start | bytes 393224 | tf_op jit(solution)/shard_map/ppermute | solution.py:31
  304.2 7.1 %collective-permute-start.46 = (bf16[512,256]{1,0:T(8,128)(2,1)S(1)}, bf16[512,256]{1,0:T(8,128)(2,1)S(1)}, u32[]{:S(2)}, u32[]{:S(2)}) collective-permute-start(bf16[512,256]{1,0:T(8,128)(2,1)S(1)} %get-tuple-element.166), channel_id=1, source_target_pairs={{0,32},{16,48},{32,0},{48,16},{1,33},{17,49},{33,1},{49,17},{2,34}... | collective-permute-start | bytes 786440 | tf_op jit(solution)/shard_map/ppermute | solution.py:31
  304.4 17.5 %collective-permute-start.44 = (bf16[512,384]{1,0:T(8,128)(2,1)S(1)}, bf16[512,384]{1,0:T(8,128)(2,1)S(1)}, u32[]{:S(2)}, u32[]{:S(2)}) collective-permute-start(bf16[512,384]{1,0:T(8,128)(2,1)S(1)} %get-tuple-element.158), channel_id=1, source_target_pairs={{0,4},{4,8},{8,12},{12,0},{1,5},{5,9},{9,13},{13,1},{2,6},{6,10},{... | collective-permute-start | bytes 1179656 | tf_op jit(solution)/shard_map/ppermute | solution.py:31
  305.9 27.1 %collective-permute-start.43 = (bf16[512,384]{1,0:T(8,128)(2,1)S(1)}, bf16[512,384]{1,0:T(8,128)(2,1)S(1)}, u32[]{:S(2)}, u32[]{:S(2)}) collective-permute-start(bf16[512,384]{1,0:T(8,128)(2,1)S(1)} %get-tuple-element.159), channel_id=1, source_target_pairs={{0,8},{4,12},{8,0},{12,4},{1,9},{5,13},{9,1},{13,5},{2,10},{6,14},... | collective-permute-start | bytes 1179656 | tf_op jit(solution)/shard_map/ppermute | solution.py:31
  308.3 24.7 %collective-permute-start.45 = (bf16[512,384]{1,0:T(8,128)(2,1)S(1)}, bf16[512,384]{1,0:T(8,128)(2,1)S(1)}, u32[]{:S(2)}, u32[]{:S(2)}) collective-permute-start(bf16[512,384]{1,0:T(8,128)(2,1)S(1)} %get-tuple-element.160), channel_id=1, source_target_pairs={{0,12},{4,0},{8,4},{12,8},{1,13},{5,1},{9,5},{13,9},{2,14},{6,2},{... | collective-permute-start | bytes 1179656 | tf_op jit(solution)/shard_map/ppermute | solution.py:31
  308.6 10.9 %collective-permute-start.47 = (bf16[512,256]{1,0:T(8,128)(2,1)S(1)}, bf16[512,256]{1,0:T(8,128)(2,1)S(1)}, u32[]{:S(2)}, u32[]{:S(2)}) collective-permute-start(bf16[512,256]{1,0:T(8,128)(2,1)S(1)} %get-tuple-element.167), channel_id=1, source_target_pairs={{0,16},{16,32},{32,48},{48,0},{1,17},{17,33},{33,49},{49,1},{2,18}... | collective-permute-start | bytes 786440 | tf_op jit(solution)/shard_map/ppermute | solution.py:31
  311.3 10.6 %collective-permute-start.48 = (bf16[512,256]{1,0:T(8,128)(2,1)S(1)}, bf16[512,256]{1,0:T(8,128)(2,1)S(1)}, u32[]{:S(2)}, u32[]{:S(2)}) collective-permute-start(bf16[512,256]{1,0:T(8,128)(2,1)S(1)} %get-tuple-element.168), channel_id=1, source_target_pairs={{0,48},{16,0},{32,16},{48,32},{1,49},{17,1},{33,17},{49,33},{2,50}... | collective-permute-start | bytes 786440 | tf_op jit(solution)/shard_map/ppermute | solution.py:31
  312.0 24.7 %copy-start.55 = (bf16[64,1024]{1,0:T(8,128)(2,1)S(1)}, bf16[64,1024]{1,0:T(8,128)(2,1)}, u32[]{:S(2)}) copy-start(bf16[64,1024]{1,0:T(8,128)(2,1)} %copy-done.54) | copy-start | bytes 393220
  312.1 27.6 %copy-start.61 = (bf16[512,512]{1,0:T(8,128)(2,1)S(1)}, bf16[512,512]{1,0:T(8,128)(2,1)}, u32[]{:S(2)}) copy-start(bf16[512,512]{1,0:T(8,128)(2,1)} %copy-done.60) | copy-start | bytes 1572868
  333.9 8.7 %collective-permute-start.49 = (bf16[256,2048]{1,0:T(8,128)(2,1)}, bf16[256,2048]{1,0:T(8,128)(2,1)}, u32[]{:S(2)}, u32[]{:S(2)}) collective-permute-start(bf16[256,2048]{1,0:T(8,128)(2,1)} %get-tuple-element.169), channel_id=1, source_target_pairs={{0,1},{1,0},{2,3},{3,2},{4,5},{5,4},{6,7},{7,6},{8,9},{9,8},{10,11... | collective-permute-start | bytes 3145736 | tf_op jit(solution)/shard_map/ppermute | solution.py:31
  337.9 16.2 %collective-permute-start.36 = (bf16[128,2048]{1,0:T(8,128)(2,1)}, bf16[128,2048]{1,0:T(8,128)(2,1)S(1)}, u32[]{:S(2)}, u32[]{:S(2)}) collective-permute-start(bf16[128,2048]{1,0:T(8,128)(2,1)} %add_convert_fusion.2), channel_id=1, source_target_pairs={{0,64},{64,0},{1,65},{65,1},{2,66},{66,2},{3,67},{67,3},{4,68},{68... | collective-permute-start | bytes 1572872 | tf_op jit(solution)/shard_map/ppermute | solution.py:31
  343.9 19.7 %collective-permute-start.50 = (bf16[128,2048]{1,0:T(8,128)(2,1)S(1)}, bf16[128,2048]{1,0:T(8,128)(2,1)S(1)}, u32[]{:S(2)}, u32[]{:S(2)}) collective-permute-start(bf16[128,2048]{1,0:T(8,128)(2,1)S(1)} %add_convert_fusion.1), channel_id=1, source_target_pairs={{0,2},{2,0},{1,3},{3,1},{4,6},{6,4},{5,7},{7,5},{8,10},{10,8},{9,1... | collective-permute-start | bytes 1572872 | tf_op jit(solution)/shard_map/ppermute | solution.py:31
  344.5 5.5 %collective-permute-start.51 = (bf16[128,384]{1,0:T(8,128)(2,1)S(1)}, bf16[128,384]{1,0:T(8,128)(2,1)S(1)}, u32[]{:S(2)}, u32[]{:S(2)}) collective-permute-start(bf16[128,384]{1,0:T(8,128)(2,1)S(1)} %get-tuple-element.190), channel_id=1, source_target_pairs={{0,16},{16,32},{32,48},{48,0},{1,17},{17,33},{33,49},{49,1},{2,18}... | collective-permute-start | bytes 294920 | tf_op jit(solution)/shard_map/ppermute | solution.py:31
  345.2 7.3 %collective-permute-start.53 = (bf16[128,384]{1,0:T(8,128)(2,1)S(1)}, bf16[128,384]{1,0:T(8,128)(2,1)S(1)}, u32[]{:S(2)}, u32[]{:S(2)}) collective-permute-start(bf16[128,384]{1,0:T(8,128)(2,1)S(1)} %get-tuple-element.191), channel_id=1, source_target_pairs={{0,32},{16,48},{32,0},{48,16},{1,33},{17,49},{33,1},{49,17},{2,34}... | collective-permute-start | bytes 294920 | tf_op jit(solution)/shard_map/ppermute | solution.py:31
  348.1 5.9 %collective-permute-start.52 = (bf16[128,384]{1,0:T(8,128)(2,1)S(1)}, bf16[128,384]{1,0:T(8,128)(2,1)S(1)}, u32[]{:S(2)}, u32[]{:S(2)}) collective-permute-start(bf16[128,384]{1,0:T(8,128)(2,1)S(1)} %get-tuple-element.192), channel_id=1, source_target_pairs={{0,48},{16,0},{32,16},{48,32},{1,49},{17,1},{33,17},{49,33},{2,50}... | collective-permute-start | bytes 294920 | tf_op jit(solution)/shard_map/ppermute | solution.py:31
  350.0 18.9 %collective-permute-start.54 = (bf16[128,768]{1,0:T(8,128)(2,1)}, bf16[128,768]{1,0:T(8,128)(2,1)}, u32[]{:S(2)}, u32[]{:S(2)}) collective-permute-start(bf16[128,768]{1,0:T(8,128)(2,1)} %get-tuple-element.187), channel_id=1, source_target_pairs={{0,4},{4,8},{8,12},{12,0},{1,5},{5,9},{9,13},{13,1},{2,6},{6,10},{... | collective-permute-start | bytes 589832 | tf_op jit(solution)/shard_map/ppermute | solution.py:31
  352.5 16.4 %collective-permute-start.56 = (bf16[128,768]{1,0:T(8,128)(2,1)S(1)}, bf16[128,768]{1,0:T(8,128)(2,1)}, u32[]{:S(2)}, u32[]{:S(2)}) collective-permute-start(bf16[128,768]{1,0:T(8,128)(2,1)S(1)} %get-tuple-element.188), channel_id=1, source_target_pairs={{0,8},{4,12},{8,0},{12,4},{1,9},{5,13},{9,1},{13,5},{2,10},{6,14},... | collective-permute-start | bytes 589832 | tf_op jit(solution)/shard_map/ppermute | solution.py:31
  354.0 14.9 %collective-permute-start.55 = (bf16[128,768]{1,0:T(8,128)(2,1)S(1)}, bf16[128,768]{1,0:T(8,128)(2,1)}, u32[]{:S(2)}, u32[]{:S(2)}) collective-permute-start(bf16[128,768]{1,0:T(8,128)(2,1)S(1)} %get-tuple-element.189), channel_id=1, source_target_pairs={{0,12},{4,0},{8,4},{12,8},{1,13},{5,1},{9,5},{13,9},{2,14},{6,2},{... | collective-permute-start | bytes 589832 | tf_op jit(solution)/shard_map/ppermute | solution.py:31
  366.1 19.5 %collective-permute-start.58 = (bf16[64,2176]{1,0:T(8,128)(2,1)S(1)}, bf16[64,2176]{1,0:T(8,128)(2,1)S(1)}, u32[]{:S(2)}, u32[]{:S(2)}) collective-permute-start(bf16[64,2176]{1,0:T(8,128)(2,1)S(1)} %dynamic-slice_bitcast_fusion), channel_id=1, source_target_pairs={{0,64},{64,0},{1,65},{65,1},{2,66},{66,2},{3,67},{67,3},{4,68},{68... | collective-permute-start | bytes 835592 | tf_op jit(solution)/shard_map/ppermute | solution.py:31
  370.6 14.2 %collective-permute-start.57 = (bf16[64,1152]{1,0:T(8,128)(2,1)S(1)}, bf16[64,1152]{1,0:T(8,128)(2,1)S(1)}, u32[]{:S(2)}, u32[]{:S(2)}) collective-permute-start(bf16[64,1152]{1,0:T(8,128)(2,1)S(1)} %dynamic-slice_bitcast_fusion.5), channel_id=1, source_target_pairs={{0,64},{64,0},{1,65},{65,1},{2,66},{66,2},{3,67},{67,3},{4,68},{68... | collective-permute-start | bytes 442376 | tf_op jit(solution)/shard_map/ppermute | solution.py:31
  (78 other events, 576.3 us)
Sparse Core Ops, SparseCore 0:
  17.4 65.3 all-gather.2
  85.7 73.1 all-gather.4
  222.1 112.9 reduce-scatter.1

commit v2 on v1

--- a/solution.py
+++ b/solution.py
@@ -659,8 +659,8 @@
     )(*grads, *map(array_of, weights), *pieces, gains)
 
 
-def rows_out(lefts, weights, terms, tile, places, mib):
-    span, d = lefts[0].shape[0], array_of(weights[0]).shape[0]
+def rows_out(lefts, weights, terms, tile, places, mib, part=(0, 1)):
+    span, d = lefts[0].shape[0] // part[1], array_of(weights[0]).shape[0]
     n = len(lefts)
     terms = [(g, c, n + w, e) for g, c, w, e in terms]
     size = span // sum(len(held) for held in places)
@@ -668,7 +668,8 @@
         functools.partial(rows_out_kernel, terms, places),
         grid=(d // tile,),
         out_shape=tuple(jax.ShapeDtypeStruct((len(held) * size, d), BF) for held in places),
-        in_specs=[fixed(g) for g in lefts] + [feature_rows(w, tile) for w in weights],
+        in_specs=[pl.BlockSpec((span, g.shape[1]), lambda i: (part[0], 0)) for g in lefts]
+        + [feature_rows(w, tile) for w in weights],
         out_specs=tuple(pl.BlockSpec((len(held) * size, tile), lambda i: (0, i)) for held in places),
         compiler_params=params(mib),
         cost_estimate=cost(sum(span * d * (c[1] - c[0]) for _, c, _, _ in terms), 6 << 20),
@@ -747,7 +748,7 @@
             pltpu.VMEM((HD, n * span), BF),
         ],
         compiler_params=params(32),
-        cost_estimate=cost(30 * 580_000_000, 2 << 20),
+        cost_estimate=cost(5 * 580_000_000, 1 << 20),
         name="attend",
     )(q, *kvs, *window)
 
@@ -844,7 +845,7 @@
     )
     shard_first = jnp.concatenate([query_weight, out_weight.T], 1)
     other_first, other_kv = swap(shard_first, "yh"), swap(shard_kv, "yh")
-    pair_first = join_sides(shard_first, after(other_first, shard_kv))
+    pair_first = join_sides(shard_first, other_first)
     first_whole = lax.all_gather(pair_first, ("z", "x"), axis=0, tiled=True)
     pair_kv = join_sides(shard_kv, other_kv)
     along_kv = send_stage(pair_kv, "x")
@@ -893,10 +894,15 @@
     )
     scaled_all = gather_eight(scaled_mid)
     hidden, grad_both = hidden_units(odd, scaled_all, cotangents, mlp_whole, units)
-    mid_partial = rows_out(
-        [grad_both], [(mlp_whole, 0, both_width)], [(0, (0, both_width), 0, (0, both_width))], 512, [(0, 1, 2, 3), (4, 5, 6, 7)], 56,
-    )
-    mid_own, mid_others = scatter_eight(*mid_partial)
+    for_both = [(0, (0, both_width), 0, (0, both_width))]
+    quarters = [(0, 1, 2, 3)]
+    (mid_there,) = rows_out(
+        [grad_both], [(mlp_whole, 0, both_width)], for_both, 512, quarters, 56, (1, 2)
+    )
+    (mid_here,) = rows_out(
+        [after(grad_both, mid_there)], [(mlp_whole, 0, both_width)], for_both, 512, quarters, 56, (0, 2)
+    )
+    mid_own, mid_others = scatter_eight(mid_here, mid_there)
     mid_arrived = send_back(mid_others)
     mlp_sum = weight_grads(
         odd, [after(scaled_all[0], mid_others), *scaled_all[1:]], cotangents, grad_both, hidden
@@ -909,16 +915,19 @@
         middle_grad_kernel, "middle_grad", [(inputs.shape, F32), (inputs.shape, BF)],
         [cotangent, mid_own, *after(mid_arrived, mlp_rows), middle, gains],
     )
-    rows_grad_middle = gather_rows(grad_middle_low)
+    grad_across = swap(grad_middle_low, "yl")
     mlp_sum = lax.psum_scatter(mlp_sum, ("z", "x"), scatter_dimension=0, tiled=True)
 
-    out_parts = wide_parts(rows_grad_middle, mixed, (0, width_q), "z")
     mlp_cores = swap(after(mlp_rows[1], grad_middle_low), "core")
     mlp_own, mlp_beside, mlp_far = call(
         pair_pieces_kernel, "pair_pieces",
         [(inputs.shape, F32), ((2 * quarter, d), BF), (inputs.shape, BF)],
         [odd, mlp_rows[0], mlp_cores], scalars=1,
     )
+    rows_grad_middle = [
+        grad_middle_low, swap(grad_middle_low, "core"), grad_across, swap(grad_across, "core")
+    ]
+    out_parts = wide_parts(rows_grad_middle, mixed, (0, width_q), "z")
     query_part, far_grads, grad_turned, delta = attend_back(
         (1, 2, 3), queries, blocks[1:], window, log_total, None, after(mixed, out_parts, mlp_beside),
         [first_whole, *rows_grad_middle],

time: 401 us -> 402 us (level)
  waiting for transfers between devices: 107 us -> 102 us
    ppermute x59, waiting for transfers between devices: 103 us -> 98.2 us  [shift(): lax.ppermute(block, axis, [(i, (i + distance) % n) for i in range(n)])]
    pallas_call x3 -> x4, Pallas kernels: 19.5 us -> 23.8 us  [rows_out(): pl.pallas_call(functools.partial(rows_out_kernel, terms, places), grid=(d...]
  transfers between devices with their start and end apart: 62 -> 62, of which waited for: 25 -> 25; matrix products, arithmetic and copies ran while one was open for 5% -> 5% of each run, Pallas kernels for 24% -> 26%
where the time goes in v2:
time: 402 us; the launch traced here: 395 us
  Pallas kernels  132 us (33%)
  waiting for transfers between devices  102 us (25%)
  starting transfers between devices  88.4 us (22%)
  local copies, waits for them, and re-layouts  29.7 us (7%)
  between operations  15.3 us (4%)
  other arithmetic  13.9 us (3%)
  blocking collectives  13.2 us (3%)
    ppermute x59, waiting for transfers between devices, shift(): lax.ppermute(block, axis, [(i, (i + distance) % n) for i in range(n)])  98.2 us
    ppermute x59, starting transfers between devices, shift(): lax.ppermute(block, axis, [(i, (i + distance) % n) for i in range(n)])  88.3 us
    pallas_call x2, Pallas kernels, attend_back(): pl.pallas_call(functools.partial(attend_back_kernel, distances, first, la...  27.2 us
    pallas_call x4, Pallas kernels, rows_out(): pl.pallas_call(functools.partial(rows_out_kernel, terms, places), grid=(d...  23.8 us
    unnamed x162, local copies, waits for them, and re-layouts  21.1 us
    pallas_call x1, Pallas kernels, hidden_units(): pl.pallas_call(functools.partial(hidden_kernel, width), out_shape=(jax.Sh...  20.1 us
    pallas_call x1, Pallas kernels, attend(): pl.pallas_call(attend_kernel, out_shape=(jax.ShapeDtypeStruct((span, widt...  16.3 us
    pallas_call x1, Pallas kernels, weight_grads(): pl.pallas_call(weight_grads_kernel, grid=(d // tile,), out_shape=jax.Shap...  16.2 us
  transfers between devices with their start and end apart: 62, of which 25 were waited for; matrix products, arithmetic and copies ran while one was open for 5% of the time, Pallas kernels for 26%

profile of v2, /device:TPU:1, one launch (start us, length us, event | category | flops | bytes accessed | tf_op | source)
XLA Modules:
  0.0 394.9 jit_solution(16689512430629025544)
XLA Ops:
  8.1 3.8 collective-permute-start.10
  11.9 2.9 collective-permute-done.10
  16.7 2.9 pack.1
  19.6 2.9 collective-permute-start
  24.9 2.6 collective-permute-start.5
  27.4 1.7 collective-permute-start.6
  30.5 2.0 collective-permute-done.4
  32.5 1.7 collective-permute-start.7
  34.6 5.1 %collective-permute-start.1 = (bf16[128,2048]{1,0:T(8,128)(2,1)}, bf16[128,2048]{1,0:T(8,128)(2,1)S(1)}, u32[]{:S(2)}, u32[]{:S(2)}) collective-permute-start(bf16[128,2048]{1,0:T(8,128)(2,1)} %get-tuple-element.98.refs_0_.base_ref.refs_4_), channel_id=1, source_target_pairs={{0,1},{1,0},{2,3},{3,2},{4,5},{5,4},{6,7},{7,6},{8,9},{9,8},{10,11... | collective-permute-start | bytes 1572872 | tf_op jit(solution)/shard_map/ppermute | solution.py:31
  39.7 2.9 collective-permute-start.9
  44.4 9.6 %collective-permute-done.8 = bf16[4,128,256]{2,1,0:T(8,128)(2,1)S(1)} collective-permute-done((bf16[4,128,256]{2,1,0:T(8,128)(2,1)S(1)}, bf16[4,128,256]{2,1,0:T(8,128)(2,1)S(1)}, u32[]{:S(2)}, u32[]{:S(2)}) %collective-permute-start.8) | collective-permute-done | bytes 262176 | tf_op jit(solution)/shard_map/ppermute | solution.py:31
  60.1 2.9 collective-permute-start.26
  63.8 2.8 collective-permute-start.13
  67.2 3.7 collective-permute-done.14
  70.9 1.9 constant_dynamic-update-slice_fusion
  73.5 1.7 collective-permute-done.12.refs_2_.refs_1_
  75.8 2.0 collective-permute-done.11.refs_1_.refs_0_
  79.4 3.7 all-gather.3.cloned.1.call-done.w_ref.refs_1_.refs_7_.refs_2_
  85.9 2.7 collective-permute-start.15
  88.7 2.2 copy-done.2
  90.8 1.5 queries.1.q_ref
  92.4 16.3 %attend.1 = (bf16[512,512]{1,0:T(8,128)(2,1)S(1)}, f32[8,512]{1,0:T(8,128)S(1)}) custom-call(bf16[512,512]{1,0:T(8,128)(2,1)S(1)} %queries.1.q_ref, bf16[512,128]{1,0:T(8,128)(2,1)S(1)} %get-tuple-element.100.refs_0_, bf16[512,128]{1,0:T(8,128)(2,1)S(1)} %copy-done.47, bf16[512,128]{1,0:T(8,128)(2,1)S(1)} %copy-done.44, bf16[512,128]{1,0:T(8,128)(2,1)S(1)} %copy-done.41, ...), custom_call_target="tpu_custom_call" | custom-call | flops 5800000000 | bytes 1048576 | tf_op jit(solution)/shard_map/attend/pallas_call | solution.py:737
  108.7 3.0 collective-permute-done.15
  111.7 1.8 rows_out.4
  113.5 1.9 collective-permute-start.16
  119.1 11.9 %collective-permute-done.17.refs_2_ = bf16[128,2048]{1,0:T(8,128)(2,1)S(1)} collective-permute-done((bf16[128,2048]{1,0:T(8,128)(2,1)S(1)}, bf16[128,2048]{1,0:T(8,128)(2,1)S(1)}, u32[]{:S(2)}, u32[]{:S(2)}) %collective-permute-start.17) | collective-permute-done | bytes 524320 | tf_op jit(solution)/shard_map/ppermute | solution.py:31
  133.2 2.4 collective-permute-start.20
  136.6 2.0 collective-permute-start.21
  138.6 8.1 %collective-permute-done.20.refs_3_ = bf16[128,2048]{1,0:T(8,128)(2,1)} collective-permute-done((bf16[128,2048]{1,0:T(8,128)(2,1)}, bf16[128,2048]{1,0:T(8,128)(2,1)}, u32[]{:S(2)}, u32[]{:S(2)}) %collective-permute-start.20) | collective-permute-done | bytes 524320 | tf_op jit(solution)/shard_map/ppermute | solution.py:31
  146.6 12.7 %collective-permute-start.24 = (bf16[128,2048]{1,0:T(8,128)(2,1)}, bf16[128,2048]{1,0:T(8,128)(2,1)}, u32[]{:S(2)}, u32[]{:S(2)}) collective-permute-start(bf16[128,2048]{1,0:T(8,128)(2,1)} %collective-permute-done.20.refs_3_), channel_id=1, source_target_pairs={{0,1},{1,0},{2,3},{3,2},{4,5},{5,4},{6,7},{7,6},{8,9},{9,8},{10,11... | collective-permute-start | bytes 1572872 | tf_op jit(solution)/shard_map/ppermute | solution.py:31
  159.3 3.2 collective-permute-done.18.refs_1_
  163.4 1.9 collective-permute-done.22.refs_5_
  165.3 20.1 %hidden_units.1 = (bf16[1024,768]{1,0:T(8,128)(2,1)}, bf16[1024,1408]{1,0:T(8,128)(2,1)}) custom-call(s32[1,1]{1,0:T(1,128)} %bitcast.18.odd_ref, bf16[128,2048]{1,0:T(8,128)(2,1)} %get-tuple-element.124.refs_0_, bf16[128,2048]{1,0:T(8,128)(2,1)} %collective-permute-done.18.refs_1_, bf16[128,2048]{1,0:T(8,128)(2,1)} %collective-permute-done.19.refs_2_, ...), custom_call_target="tpu_custom_call" | custom-call | flops 8053063680 | bytes 7864320 | tf_op jit(solution)/shard_map/hidden_units/pallas_call | solution.py:610
  185.4 7.4 %rows_out.5 = bf16[512,2048]{1,0:T(8,128)(2,1)} custom-call(bf16[1024,1408]{1,0:T(8,128)(2,1)} %get-tuple-element.120.refs_0_.refs_10_, bf16[2048,2176]{1,0:T(8,128)(2,1)} %all-gather.5.cloned.1.call-done.refs_10_.refs_1_), custom_call_target="tpu_custom_call" | custom-call | flops 2952790016 | bytes 6291456 | tf_op jit(solution)/shard_map/rows_out/pallas_call | solution.py:667
  193.3 7.4 %rows_out.6.one_ref = bf16[512,2048]{1,0:T(8,128)(2,1)} custom-call(bf16[1024,1408]{1,0:T(8,128)(2,1)} %get-tuple-element.120.refs_0_.refs_10_, bf16[2048,2176]{1,0:T(8,128)(2,1)} %all-gather.5.cloned.1.call-done.refs_10_.refs_1_), custom_call_target="tpu_custom_call" | custom-call | flops 2952790016 | bytes 6291456 | tf_op jit(solution)/shard_map/rows_out/pallas_call | solution.py:667
  200.7 1.6 copy-done.7
  202.3 1.4 add_pieces.1
  206.2 16.2 %weight_grads.1 = bf16[2048,2176]{1,0:T(8,128)(2,1)} custom-call(s32[1,1]{1,0:T(1,128)} %bitcast.18.odd_ref, bf16[128,2048]{1,0:T(8,128)(2,1)} %get-tuple-element.124.refs_0_, bf16[128,2048]{1,0:T(8,128)(2,1)} %collective-permute-done.18.refs_1_, bf16[128,2048]{1,0:T(8,128)(2,1)} %collective-permute-done.19.refs_2_, ...), custom_call_target="tpu_custom_call" | custom-call | flops 9126805504 | bytes 17301504 | tf_op jit(solution)/shard_map/weight_grads/pallas_call | solution.py:797
  222.5 7.2 %rows_out.7 = (bf16[512,2048]{1,0:T(8,128)(2,1)}, bf16[512,2048]{1,0:T(8,128)(2,1)}) custom-call(bf16[1024,768]{1,0:T(8,128)(2,1)} %get-tuple-element.125.refs_11_.refs_0_, bf16[2048,2176]{1,0:T(8,128)(2,1)} %all-gather.5.cloned.1.call-done.refs_10_.refs_1_), custom_call_target="tpu_custom_call" | custom-call | flops 3221225472 | bytes 6291456 | tf_op jit(solution)/shard_map/rows_out/pallas_call | solution.py:667
  229.7 2.7 collective-permute-done.29.refs_2_
  232.4 3.2 middle_grad.1
  237.1 13.8 %collective-permute-done.33.refs_2_.refs_10_ = bf16[128,2048]{1,0:T(8,128)(2,1)S(1)} collective-permute-done((bf16[128,2048]{1,0:T(8,128)(2,1)}, bf16[128,2048]{1,0:T(8,128)(2,1)S(1)}, u32[]{:S(2)}, u32[]{:S(2)}) %collective-permute-start.33) | collective-permute-done | bytes 524320 | tf_op jit(solution)/shard_map/ppermute | solution.py:31
  255.4 2.9 wide_parts.2
  258.3 1.5 collective-permute-start.41
  259.9 2.6 collective-permute-start.40
  263.5 2.4 pair_pieces.1
  268.1 20.5 %attend_back.2 = (f32[512,512]{1,0:T(8,128)S(1)}, bf16[1536,128]{1,0:T(8,128)(2,1)S(1)}, bf16[512,512]{1,0:T(8,128)(2,1)S(1)}, f32[8,512]{1,0:T(8,128)S(1)}) custom-call(bf16[512,512]{1,0:T(8,128)(2,1)S(1)} %copy-done.16, bf16[512,128]{1,0:T(8,128)(2,1)S(1)} %copy-done.48, bf16[512,128]{1,0:T(8,128)(2,1)S(1)} %copy-done.45, bf16[512,128]{1,0:T(8,128)(2,1)S(1)} %copy-done.42, ...), custom_call_target="tpu_custom_call" | custom-call | flops 127600001024 | bytes 1048576 | tf_op jit(solution)/shard_map/attend_back/pallas_call | solution.py:774
  288.8 2.3 collective-permute-done.35
  294.0 6.7 %attend_back.3 = (bf16[512,512]{1,0:T(8,128)(2,1)S(1)}, f32[512,128]{1,0:T(8,128)S(1)}) custom-call(bf16[512,512]{1,0:T(8,128)(2,1)S(1)} %copy-done.16, bf16[512,128]{1,0:T(8,128)(2,1)S(1)} %get-tuple-element.100.refs_0_, s32[1,1]{1,0:T(1,128)} %bitcast.16.refs_4_.refs_3_.refs_1_, s32[1,512]{1,0:T(1,128)S(1)} %bitcast.82, ...), custom_call_target="tpu_custom_call" | custom-call | bytes 1048576 | tf_op jit(solution)/shard_map/attend_back/pallas_call | solution.py:774
  304.9 1.5 collective-permute-start.44
  306.4 2.2 collective-permute-start.43
  310.0 1.7 collective-permute-done.46
  312.3 5.0 %rows_grad.1 = (bf16[128,2048]{1,0:T(8,128)(2,1)S(1)}, bf16[128,2048]{1,0:T(8,128)(2,1)S(1)}, bf16[256,2048]{1,0:T(8,128)(2,1)}) custom-call(bf16[512,512]{1,0:T(8,128)(2,1)S(1)} %get-tuple-element.157.refs_1_.dq_ref.refs_0_, bf16[512,128]{1,0:T(8,128)(2,1)S(1)} %get-tuple-element.159.refs_1_, bf16[2048,1024]{1,0:T(8,128)(2,1)S(1)} %copy-done.4, ...), custom_call_target="tpu_custom_call" | custom-call | tf_op jit(solution)/shard_map/rows_grad/pallas_call | solution.py:647
  317.3 2.8 collective-permute-done.47
  320.0 2.4 collective-permute-done.48
  322.4 10.4 %collective-permute-done.43 = bf16[512,384]{1,0:T(8,128)(2,1)S(1)} collective-permute-done((bf16[512,384]{1,0:T(8,128)(2,1)S(1)}, bf16[512,384]{1,0:T(8,128)(2,1)S(1)}, u32[]{:S(2)}, u32[]{:S(2)}) %collective-permute-start.43) | collective-permute-done | bytes 393248 | tf_op jit(solution)/shard_map/ppermute | solution.py:31
  334.1 2.9 collective-permute-start.49
  338.8 2.0 collective-permute-start.36
  340.8 1.5 add_convert_fusion
  346.1 3.2 collective-permute-start.53
  351.3 2.5 collective-permute-done.53
  358.5 6.4 %collective-permute-done.50.refs_2_ = bf16[128,2048]{1,0:T(8,128)(2,1)S(1)} collective-permute-done((bf16[128,2048]{1,0:T(8,128)(2,1)S(1)}, bf16[128,2048]{1,0:T(8,128)(2,1)S(1)}, u32[]{:S(2)}, u32[]{:S(2)}) %collective-permute-start.50) | collective-permute-done | bytes 524320 | tf_op jit(solution)/shard_map/ppermute | solution.py:31
  367.4 3.2 collective-permute-start.58
  372.3 13.2 %psum.7 = f32[2,2,64]{2,1,0:T(2,128)S(1)} all-reduce(f32[2,2,64]{2,1,0:T(2,128)S(1)} %reshape.102), channel_id=1, replica_groups=mesh['yh'=2,'z'=4,'x'=4,'yl'=2,'core'=2] {'yh','yl','core'}, use_global_device_ids=true, to_apply=%region_3.4 | all-reduce | flops 256 | bytes 2048 | tf_op jit(solution)/shard_map/psum | solution.py:994
  (301 shorter events, 70.6 us)
Async XLA Ops:
  7.2 75.9 %all-gather.3.cloned.1.call-start = ((), (), s32[]{:S(2)}) async-start(), calls=%async_computation.1 | async-start | bytes 4456448 | tf_op jit(solution)/shard_map/all_gather | solution.py:849
  8.1 6.8 %collective-permute-start.10 = (bf16[64,1024]{1,0:T(8,128)(2,1)S(1)}, bf16[64,1024]{1,0:T(8,128)(2,1)S(1)}, u32[]{:S(2)}, u32[]{:S(2)}) collective-permute-start(bf16[64,1024]{1,0:T(8,128)(2,1)S(1)} %pad_maximum_fusion.4), channel_id=1, source_target_pairs={{0,64},{64,0},{1,65},{65,1},{2,66},{66,2},{3,67},{67,3},{4,68},{68... | collective-permute-start | bytes 393224 | tf_op jit(solution)/shard_map/ppermute | solution.py:31
  16.6 148.6 %all-gather.5.cloned.1.call-start = ((), (), s32[]{:S(2)}) async-start(), calls=%async_computation.2 | async-start | bytes 9469952 | tf_op jit(solution)/shard_map/all_gather | solution.py:879
  19.6 4.5 %collective-permute-start = (bf16[64,256]{1,0:T(8,128)(2,1)}, bf16[64,256]{1,0:T(8,128)(2,1)S(1)}, u32[]{:S(2)}, u32[]{:S(2)}) collective-permute-start(bf16[64,256]{1,0:T(8,128)(2,1)} %get-tuple-element.97), channel_id=1, source_target_pairs={{0,64},{64,0},{1,65},{65,1},{2,66},{66,2},{3,67},{67,3},{4,68},{68... | collective-permute-start | bytes 98312 | tf_op jit(solution)/shard_map/ppermute | solution.py:31
  24.8 29.3 %copy-start.8 = (bf16[128,2048]{1,0:T(8,128)(2,1)S(1)}, bf16[128,2048]{1,0:T(8,128)(2,1)}, u32[]{:S(2)}) copy-start(bf16[128,2048]{1,0:T(8,128)(2,1)} %get-tuple-element.98.refs_0_.base_ref.refs_4_) | copy-start | bytes 1572868
  24.9 7.6 %collective-permute-start.5 = (bf16[128,256]{1,0:T(8,128)(2,1)S(1)}, bf16[128,256]{1,0:T(8,128)(2,1)S(1)}, u32[]{:S(2)}, u32[]{:S(2)}) collective-permute-start(bf16[128,256]{1,0:T(8,128)(2,1)S(1)} %pad_maximum_fusion.5), channel_id=1, source_target_pairs={{0,12},{4,0},{8,4},{12,8},{1,13},{5,1},{9,5},{13,9},{2,14},{6,2},{... | collective-permute-start | bytes 196616 | tf_op jit(solution)/shard_map/ppermute | solution.py:31
  27.4 5.0 %collective-permute-start.4 = (bf16[128,256]{1,0:T(8,128)(2,1)S(1)}, bf16[128,256]{1,0:T(8,128)(2,1)S(1)}, u32[]{:S(2)}, u32[]{:S(2)}) collective-permute-start(bf16[128,256]{1,0:T(8,128)(2,1)S(1)} %pad_maximum_fusion.5), channel_id=1, source_target_pairs={{0,4},{4,8},{8,12},{12,0},{1,5},{5,9},{9,13},{13,1},{2,6},{6,10},{... | collective-permute-start | bytes 196616 | tf_op jit(solution)/shard_map/ppermute | solution.py:31
  27.4 5.1 %collective-permute-start.6 = (bf16[128,256]{1,0:T(8,128)(2,1)S(1)}, bf16[128,256]{1,0:T(8,128)(2,1)S(1)}, u32[]{:S(2)}, u32[]{:S(2)}) collective-permute-start(bf16[128,256]{1,0:T(8,128)(2,1)S(1)} %pad_maximum_fusion.5), channel_id=1, source_target_pairs={{0,8},{4,12},{8,0},{12,4},{1,9},{5,13},{9,1},{13,5},{2,10},{6,14},... | collective-permute-start | bytes 196616 | tf_op jit(solution)/shard_map/ppermute | solution.py:31
  29.2 14.5 %collective-permute-start.2 = (bf16[128,2048]{1,0:T(8,128)(2,1)}, bf16[128,2048]{1,0:T(8,128)(2,1)S(1)}, u32[]{:S(2)}, u32[]{:S(2)}) collective-permute-start(bf16[128,2048]{1,0:T(8,128)(2,1)} %get-tuple-element.98.refs_0_.base_ref.refs_4_), channel_id=1, source_target_pairs={{0,2},{2,0},{1,3},{3,1},{4,6},{6,4},{5,7},{7,5},{8,10},{10,8},{9,1... | collective-permute-start | bytes 1572872 | tf_op jit(solution)/shard_map/ppermute | solution.py:31
  32.5 11.9 %collective-permute-start.7 = (bf16[4,128,256]{2,1,0:T(8,128)(2,1)S(1)}, bf16[4,128,256]{2,1,0:T(8,128)(2,1)S(1)}, u32[]{:S(2)}, u32[]{:S(2)}) collective-permute-start(bf16[4,128,256]{2,1,0:T(8,128)(2,1)S(1)} %bitcast_dynamic-update-slice_fusion.4), channel_id=1, source_target_pairs={{0,16},{16,32},{32,48},{48,0},{1,17},{17,33},{33,49},{49,1},{2,18}... | collective-permute-start | bytes 786440 | tf_op jit(solution)/shard_map/ppermute | solution.py:31
  34.6 19.5 %collective-permute-start.1 = (bf16[128,2048]{1,0:T(8,128)(2,1)}, bf16[128,2048]{1,0:T(8,128)(2,1)S(1)}, u32[]{:S(2)}, u32[]{:S(2)}) collective-permute-start(bf16[128,2048]{1,0:T(8,128)(2,1)} %get-tuple-element.98.refs_0_.base_ref.refs_4_), channel_id=1, source_target_pairs={{0,1},{1,0},{2,3},{3,2},{4,5},{5,4},{6,7},{7,6},{8,9},{9,8},{10,11... | collective-permute-start | bytes 1572872 | tf_op jit(solution)/shard_map/ppermute | solution.py:31
  39.7 14.4 %collective-permute-start.9 = (bf16[4,128,256]{2,1,0:T(8,128)(2,1)S(1)}, bf16[4,128,256]{2,1,0:T(8,128)(2,1)S(1)}, u32[]{:S(2)}, u32[]{:S(2)}) collective-permute-start(bf16[4,128,256]{2,1,0:T(8,128)(2,1)S(1)} %bitcast_dynamic-update-slice_fusion.4), channel_id=1, source_target_pairs={{0,32},{16,48},{32,0},{48,16},{1,33},{17,49},{33,1},{49,17},{2,34}... | collective-permute-start | bytes 786440 | tf_op jit(solution)/shard_map/ppermute | solution.py:31
  42.5 11.5 %collective-permute-start.8 = (bf16[4,128,256]{2,1,0:T(8,128)(2,1)S(1)}, bf16[4,128,256]{2,1,0:T(8,128)(2,1)S(1)}, u32[]{:S(2)}, u32[]{:S(2)}) collective-permute-start(bf16[4,128,256]{2,1,0:T(8,128)(2,1)S(1)} %bitcast_dynamic-update-slice_fusion.4), channel_id=1, source_target_pairs={{0,48},{16,0},{32,16},{48,32},{1,49},{17,1},{33,17},{49,33},{2,50}... | collective-permute-start | bytes 786440 | tf_op jit(solution)/shard_map/ppermute | solution.py:31
  43.7 10.4 %collective-permute-start.3 = (bf16[128,2048]{1,0:T(8,128)(2,1)S(1)}, bf16[128,2048]{1,0:T(8,128)(2,1)S(1)}, u32[]{:S(2)}, u32[]{:S(2)}) collective-permute-start(bf16[128,2048]{1,0:T(8,128)(2,1)S(1)} %collective-permute-done.2.refs_2_.refs_6_), channel_id=1, source_target_pairs={{0,1},{1,0},{2,3},{3,2},{4,5},{5,4},{6,7},{7,6},{8,9},{9,8},{10,11... | collective-permute-start | bytes 1572872 | tf_op jit(solution)/shard_map/ppermute | solution.py:31
  58.0 12.9 %collective-permute-start.14 = (bf16[128,2048]{1,0:T(8,128)(2,1)S(1)}, bf16[128,2048]{1,0:T(8,128)(2,1)}, u32[]{:S(2)}, u32[]{:S(2)}) collective-permute-start(bf16[128,2048]{1,0:T(8,128)(2,1)S(1)} %copy-done.14), channel_id=1, source_target_pairs={{0,2},{2,0},{1,3},{3,1},{4,6},{6,4},{5,7},{7,5},{8,10},{10,8},{9,1... | collective-permute-start | bytes 1572872 | tf_op jit(solution)/shard_map/ppermute | solution.py:31
  60.1 19.3 %collective-permute-start.26 = (bf16[64,2176]{1,0:T(8,128)(2,1)}, bf16[64,2176]{1,0:T(8,128)(2,1)}, u32[]{:S(2)}, u32[]{:S(2)}) collective-permute-start(bf16[64,2176]{1,0:T(8,128)(2,1)} %dynamic-slice_bitcast_fusion.1), channel_id=1, source_target_pairs={{0,64},{64,0},{1,65},{65,1},{2,66},{66,2},{3,67},{67,3},{4,68},{68... | collective-permute-start | bytes 835592 | tf_op jit(solution)/shard_map/ppermute | solution.py:31
  63.8 9.0 %collective-permute-start.13 = (bf16[512,128]{1,0:T(8,128)(2,1)S(1)}, bf16[512,128]{1,0:T(8,128)(2,1)S(1)}, u32[]{:S(2)}, u32[]{:S(2)}) collective-permute-start(bf16[512,128]{1,0:T(8,128)(2,1)S(1)} %get-tuple-element.100.refs_0_), channel_id=1, source_target_pairs={{0,12},{4,0},{8,4},{12,8},{1,13},{5,1},{9,5},{13,9},{2,14},{6,2},{... | collective-permute-start | bytes 393224 | tf_op jit(solution)/shard_map/ppermute | solution.py:31
  66.6 8.6 %collective-permute-start.12 = (bf16[512,128]{1,0:T(8,128)(2,1)S(1)}, bf16[512,128]{1,0:T(8,128)(2,1)S(1)}, u32[]{:S(2)}, u32[]{:S(2)}) collective-permute-start(bf16[512,128]{1,0:T(8,128)(2,1)S(1)} %get-tuple-element.100.refs_0_), channel_id=1, source_target_pairs={{0,8},{4,12},{8,0},{12,4},{1,9},{5,13},{9,1},{13,5},{2,10},{6,14},... | collective-permute-start | bytes 393224 | tf_op jit(solution)/shard_map/ppermute | solution.py:31
  66.6 11.3 %collective-permute-start.11 = (bf16[512,128]{1,0:T(8,128)(2,1)S(1)}, bf16[512,128]{1,0:T(8,128)(2,1)S(1)}, u32[]{:S(2)}, u32[]{:S(2)}) collective-permute-start(bf16[512,128]{1,0:T(8,128)(2,1)S(1)} %get-tuple-element.100.refs_0_), channel_id=1, source_target_pairs={{0,4},{4,8},{8,12},{12,0},{1,5},{5,9},{9,13},{13,1},{2,6},{6,10},{... | collective-permute-start | bytes 393224 | tf_op jit(solution)/shard_map/ppermute | solution.py:31
  85.9 280.4 %reduce-scatter.2.cloned.1.call-start = ((), (), s32[]{:S(2)}) async-start(), calls=%async_computation.3 | async-start | bytes 9469952 | tf_op jit(solution)/shard_map/reduce_scatter | solution.py:919
  85.9 25.8 %collective-permute-start.15 = (bf16[256,2048]{1,0:T(8,128)(2,1)}, bf16[256,2048]{1,0:T(8,128)(2,1)S(1)}, u32[]{:S(2)}, u32[]{:S(2)}) collective-permute-start(bf16[256,2048]{1,0:T(8,128)(2,1)} %constant_dynamic-update-slice_fusion), channel_id=1, source_target_pairs={{0,64},{64,0},{1,65},{65,1},{2,66},{66,2},{3,67},{67,3},{4,68},{68... | collective-permute-start | bytes 3145736 | tf_op jit(solution)/shard_map/ppermute | solution.py:31
  113.5 4.2 %collective-permute-start.16 = (bf16[256,2048]{1,0:T(8,128)(2,1)S(1)}, bf16[256,2048]{1,0:T(8,128)(2,1)S(1)}, u32[]{:S(2)}, u32[]{:S(2)}) collective-permute-start(bf16[256,2048]{1,0:T(8,128)(2,1)S(1)} %get-tuple-element.109), channel_id=1, source_target_pairs={{0,1},{1,0},{2,3},{3,2},{4,5},{5,4},{6,7},{7,6},{8,9},{9,8},{10,11... | collective-permute-start | bytes 3145736 | tf_op jit(solution)/shard_map/ppermute | solution.py:31
  117.6 45.8 %collective-permute-start.25 = (bf16[512,2048]{1,0:T(8,128)(2,1)}, bf16[512,2048]{1,0:T(8,128)(2,1)}, u32[]{:S(2)}, u32[]{:S(2)}) collective-permute-start(bf16[512,2048]{1,0:T(8,128)(2,1)} %constant_dynamic-update-slice_fusion.2.refs_8_), channel_id=1, source_target_pairs={{0,1},{1,0},{2,3},{3,2},{4,5},{5,4},{6,7},{7,6},{8,9},{9,8},{10,11... | collective-permute-start | bytes 6291464 | tf_op jit(solution)/shard_map/ppermute | solution.py:31
  117.8 13.2 %collective-permute-start.17 = (bf16[128,2048]{1,0:T(8,128)(2,1)S(1)}, bf16[128,2048]{1,0:T(8,128)(2,1)S(1)}, u32[]{:S(2)}, u32[]{:S(2)}) collective-permute-start(bf16[128,2048]{1,0:T(8,128)(2,1)S(1)} %add_convert_fusion.3), channel_id=1, source_target_pairs={{0,2},{2,0},{1,3},{3,1},{4,6},{6,4},{5,7},{7,5},{8,10},{10,8},{9,1... | collective-permute-start | bytes 1572872 | tf_op jit(solution)/shard_map/ppermute | solution.py:31
  133.2 13.4 %collective-permute-start.20 = (bf16[128,2048]{1,0:T(8,128)(2,1)}, bf16[128,2048]{1,0:T(8,128)(2,1)}, u32[]{:S(2)}, u32[]{:S(2)}) collective-permute-start(bf16[128,2048]{1,0:T(8,128)(2,1)} %get-tuple-element.124.refs_0_), channel_id=1, source_target_pairs={{0,66},{2,0},{64,2},{66,64},{1,67},{3,1},{65,3},{67,65},{4,70},{6,... | collective-permute-start | bytes 1572872 | tf_op jit(solution)/shard_map/ppermute | solution.py:31
  135.6 23.7 %collective-permute-start.19 = (bf16[128,2048]{1,0:T(8,128)(2,1)}, bf16[128,2048]{1,0:T(8,128)(2,1)}, u32[]{:S(2)}, u32[]{:S(2)}) collective-permute-start(bf16[128,2048]{1,0:T(8,128)(2,1)} %get-tuple-element.124.refs_0_), channel_id=1, source_target_pairs={{0,64},{2,66},{64,0},{66,2},{1,65},{3,67},{65,1},{67,3},{4,68},{6,... | collective-permute-start | bytes 1572872 | tf_op jit(solution)/shard_map/ppermute | solution.py:31
  136.2 26.3 %collective-permute-start.18 = (bf16[128,2048]{1,0:T(8,128)(2,1)}, bf16[128,2048]{1,0:T(8,128)(2,1)}, u32[]{:S(2)}, u32[]{:S(2)}) collective-permute-start(bf16[128,2048]{1,0:T(8,128)(2,1)} %get-tuple-element.124.refs_0_), channel_id=1, source_target_pairs={{0,2},{2,64},{64,66},{66,0},{1,3},{3,65},{65,67},{67,1},{4,6},{6,6... | collective-permute-start | bytes 1572872 | tf_op jit(solution)/shard_map/ppermute | solution.py:31
  136.6 26.8 %collective-permute-start.21 = (bf16[128,2048]{1,0:T(8,128)(2,1)}, bf16[128,2048]{1,0:T(8,128)(2,1)}, u32[]{:S(2)}, u32[]{:S(2)}) collective-permute-start(bf16[128,2048]{1,0:T(8,128)(2,1)} %get-tuple-element.124.refs_0_), channel_id=1, source_target_pairs={{0,1},{1,0},{2,3},{3,2},{4,5},{5,4},{6,7},{7,6},{8,9},{9,8},{10,11... | collective-permute-start | bytes 1572872 | tf_op jit(solution)/shard_map/ppermute | solution.py:31
  146.6 16.8 %collective-permute-start.24 = (bf16[128,2048]{1,0:T(8,128)(2,1)}, bf16[128,2048]{1,0:T(8,128)(2,1)}, u32[]{:S(2)}, u32[]{:S(2)}) collective-permute-start(bf16[128,2048]{1,0:T(8,128)(2,1)} %collective-permute-done.20.refs_3_), channel_id=1, source_target_pairs={{0,1},{1,0},{2,3},{3,2},{4,5},{5,4},{6,7},{7,6},{8,9},{9,8},{10,11... | collective-permute-start | bytes 1572872 | tf_op jit(solution)/shard_map/ppermute | solution.py:31
  159.3 4.1 %collective-permute-start.23 = (bf16[128,2048]{1,0:T(8,128)(2,1)}, bf16[128,2048]{1,0:T(8,128)(2,1)}, u32[]{:S(2)}, u32[]{:S(2)}) collective-permute-start(bf16[128,2048]{1,0:T(8,128)(2,1)} %collective-permute-done.19.refs_2_), channel_id=1, source_target_pairs={{0,1},{1,0},{2,3},{3,2},{4,5},{5,4},{6,7},{7,6},{8,9},{9,8},{10,11... | collective-permute-start | bytes 1572872 | tf_op jit(solution)/shard_map/ppermute | solution.py:31
  162.5 2.8 collective-permute-start.22
  192.8 7.9 %collective-permute-start.27 = (bf16[512,2048]{1,0:T(8,128)(2,1)}, bf16[512,2048]{1,0:T(8,128)(2,1)S(1)}, u32[]{:S(2)}, u32[]{:S(2)}) collective-permute-start(bf16[512,2048]{1,0:T(8,128)(2,1)} %rows_out.5), channel_id=1, source_target_pairs={{0,1},{1,0},{2,3},{3,2},{4,5},{5,4},{6,7},{7,6},{8,9},{9,8},{10,11... | collective-permute-start | bytes 6291464 | tf_op jit(solution)/shard_map/ppermute | solution.py:31
  204.7 25.0 %collective-permute-start.28 = (bf16[128,2048]{1,0:T(8,128)(2,1)}, bf16[128,2048]{1,0:T(8,128)(2,1)}, u32[]{:S(2)}, u32[]{:S(2)}) collective-permute-start(bf16[128,2048]{1,0:T(8,128)(2,1)} %get-tuple-element.121), channel_id=1, source_target_pairs={{0,66},{2,0},{64,2},{66,64},{1,67},{3,1},{65,3},{67,65},{4,70},{6,... | collective-permute-start | bytes 1572872 | tf_op jit(solution)/shard_map/ppermute | solution.py:31
  205.5 24.2 %collective-permute-start.30 = (bf16[128,2048]{1,0:T(8,128)(2,1)}, bf16[128,2048]{1,0:T(8,128)(2,1)}, u32[]{:S(2)}, u32[]{:S(2)}) collective-permute-start(bf16[128,2048]{1,0:T(8,128)(2,1)} %get-tuple-element.122), channel_id=1, source_target_pairs={{0,64},{2,66},{64,0},{66,2},{1,65},{3,67},{65,1},{67,3},{4,68},{6,... | collective-permute-start | bytes 1572872 | tf_op jit(solution)/shard_map/ppermute | solution.py:31
  205.7 26.8 %collective-permute-start.29 = (bf16[128,2048]{1,0:T(8,128)(2,1)}, bf16[128,2048]{1,0:T(8,128)(2,1)}, u32[]{:S(2)}, u32[]{:S(2)}) collective-permute-start(bf16[128,2048]{1,0:T(8,128)(2,1)} %get-tuple-element.123), channel_id=1, source_target_pairs={{0,2},{2,64},{64,66},{66,0},{1,3},{3,65},{65,67},{67,1},{4,6},{6,6... | collective-permute-start | bytes 1572872 | tf_op jit(solution)/shard_map/ppermute | solution.py:31
  236.6 26.9 %collective-permute-start.31 = (bf16[512,2048]{1,0:T(8,128)(2,1)}, bf16[512,2048]{1,0:T(8,128)(2,1)}, u32[]{:S(2)}, u32[]{:S(2)}) collective-permute-start(bf16[512,2048]{1,0:T(8,128)(2,1)} %get-tuple-element.133), channel_id=1, source_target_pairs={{0,1},{1,0},{2,3},{3,2},{4,5},{5,4},{6,7},{7,6},{8,9},{9,8},{10,11... | collective-permute-start | bytes 6291464 | tf_op jit(solution)/shard_map/ppermute | solution.py:31
  237.1 13.8 %collective-permute-start.33 = (bf16[128,2048]{1,0:T(8,128)(2,1)}, bf16[128,2048]{1,0:T(8,128)(2,1)S(1)}, u32[]{:S(2)}, u32[]{:S(2)}) collective-permute-start(bf16[128,2048]{1,0:T(8,128)(2,1)} %get-tuple-element.132.refs_0_.refs_8_), channel_id=1, source_target_pairs={{0,2},{2,0},{1,3},{3,1},{4,6},{6,4},{5,7},{7,5},{8,10},{10,8},{9,1... | collective-permute-start | bytes 1572872 | tf_op jit(solution)/shard_map/ppermute | solution.py:31
  237.1 15.3 %collective-permute-start.32 = (bf16[128,2048]{1,0:T(8,128)(2,1)}, bf16[128,2048]{1,0:T(8,128)(2,1)}, u32[]{:S(2)}, u32[]{:S(2)}) collective-permute-start(bf16[128,2048]{1,0:T(8,128)(2,1)} %get-tuple-element.132.refs_0_.refs_8_), channel_id=1, source_target_pairs={{0,1},{1,0},{2,3},{3,2},{4,5},{5,4},{6,7},{7,6},{8,9},{9,8},{10,11... | collective-permute-start | bytes 1572872 | tf_op jit(solution)/shard_map/ppermute | solution.py:31
  250.9 2.4 collective-permute-start.34
  258.3 33.6 %collective-permute-start.41 = (bf16[512,512]{1,0:T(8,128)(2,1)S(1)}, bf16[512,512]{1,0:T(8,128)(2,1)S(1)}, u32[]{:S(2)}, u32[]{:S(2)}) collective-permute-start(bf16[512,512]{1,0:T(8,128)(2,1)S(1)} %get-tuple-element.138), channel_id=1, source_target_pairs={{0,16},{16,32},{32,48},{48,0},{1,17},{17,33},{33,49},{49,1},{2,18}... | collective-permute-start | bytes 1572872 | tf_op jit(solution)/shard_map/ppermute | solution.py:31
  259.9 40.9 %collective-permute-start.40 = (bf16[512,512]{1,0:T(8,128)(2,1)S(1)}, bf16[512,512]{1,0:T(8,128)(2,1)S(1)}, u32[]{:S(2)}, u32[]{:S(2)}) collective-permute-start(bf16[512,512]{1,0:T(8,128)(2,1)S(1)} %get-tuple-element.139), channel_id=1, source_target_pairs={{0,32},{16,48},{32,0},{48,16},{1,33},{17,49},{33,1},{49,17},{2,34}... | collective-permute-start | bytes 1572872 | tf_op jit(solution)/shard_map/ppermute | solution.py:31
  262.4 38.3 %collective-permute-start.42 = (bf16[512,512]{1,0:T(8,128)(2,1)S(1)}, bf16[512,512]{1,0:T(8,128)(2,1)S(1)}, u32[]{:S(2)}, u32[]{:S(2)}) collective-permute-start(bf16[512,512]{1,0:T(8,128)(2,1)S(1)} %get-tuple-element.140), channel_id=1, source_target_pairs={{0,48},{16,0},{32,16},{48,32},{1,49},{17,1},{33,17},{49,33},{2,50}... | collective-permute-start | bytes 1572872 | tf_op jit(solution)/shard_map/ppermute | solution.py:31
  266.9 24.1 %collective-permute-start.35 = (bf16[256,2048]{1,0:T(8,128)(2,1)S(1)}, bf16[256,2048]{1,0:T(8,128)(2,1)S(1)}, u32[]{:S(2)}, u32[]{:S(2)}) collective-permute-start(bf16[256,2048]{1,0:T(8,128)(2,1)S(1)} %get-tuple-element.136), channel_id=1, source_target_pairs={{0,2},{2,0},{1,3},{3,1},{4,6},{6,4},{5,7},{7,5},{8,10},{10,8},{9,1... | collective-permute-start | bytes 3145736 | tf_op jit(solution)/shard_map/ppermute | solution.py:31
  288.7 12.1 %collective-permute-start.39 = (bf16[512,128]{1,0:T(8,128)(2,1)S(1)}, bf16[512,128]{1,0:T(8,128)(2,1)S(1)}, u32[]{:S(2)}, u32[]{:S(2)}) collective-permute-start(bf16[512,128]{1,0:T(8,128)(2,1)S(1)} %get-tuple-element.189), channel_id=1, source_target_pairs={{0,4},{4,8},{8,12},{12,0},{1,5},{5,9},{9,13},{13,1},{2,6},{6,10},{... | collective-permute-start | bytes 393224 | tf_op jit(solution)/shard_map/ppermute | solution.py:31
  291.0 9.8 %collective-permute-start.38 = (bf16[512,128]{1,0:T(8,128)(2,1)S(1)}, bf16[512,128]{1,0:T(8,128)(2,1)S(1)}, u32[]{:S(2)}, u32[]{:S(2)}) collective-permute-start(bf16[512,128]{1,0:T(8,128)(2,1)S(1)} %get-tuple-element.190), channel_id=1, source_target_pairs={{0,8},{4,12},{8,0},{12,4},{1,9},{5,13},{9,1},{13,5},{2,10},{6,14},... | collective-permute-start | bytes 393224 | tf_op jit(solution)/shard_map/ppermute | solution.py:31
  292.0 8.8 %collective-permute-start.37 = (bf16[512,128]{1,0:T(8,128)(2,1)S(1)}, bf16[512,128]{1,0:T(8,128)(2,1)S(1)}, u32[]{:S(2)}, u32[]{:S(2)}) collective-permute-start(bf16[512,128]{1,0:T(8,128)(2,1)S(1)} %get-tuple-element.191), channel_id=1, source_target_pairs={{0,12},{4,0},{8,4},{12,8},{1,13},{5,1},{9,5},{13,9},{2,14},{6,2},{... | collective-permute-start | bytes 393224 | tf_op jit(solution)/shard_map/ppermute | solution.py:31
  304.7 7.1 %collective-permute-start.46 = (bf16[512,256]{1,0:T(8,128)(2,1)S(1)}, bf16[512,256]{1,0:T(8,128)(2,1)S(1)}, u32[]{:S(2)}, u32[]{:S(2)}) collective-permute-start(bf16[512,256]{1,0:T(8,128)(2,1)S(1)} %get-tuple-element.162), channel_id=1, source_target_pairs={{0,32},{16,48},{32,0},{48,16},{1,33},{17,49},{33,1},{49,17},{2,34}... | collective-permute-start | bytes 786440 | tf_op jit(solution)/shard_map/ppermute | solution.py:31
  304.9 17.5 %collective-permute-start.44 = (bf16[512,384]{1,0:T(8,128)(2,1)S(1)}, bf16[512,384]{1,0:T(8,128)(2,1)S(1)}, u32[]{:S(2)}, u32[]{:S(2)}) collective-permute-start(bf16[512,384]{1,0:T(8,128)(2,1)S(1)} %get-tuple-element.154), channel_id=1, source_target_pairs={{0,4},{4,8},{8,12},{12,0},{1,5},{5,9},{9,13},{13,1},{2,6},{6,10},{... | collective-permute-start | bytes 1179656 | tf_op jit(solution)/shard_map/ppermute | solution.py:31
  306.4 26.4 %collective-permute-start.43 = (bf16[512,384]{1,0:T(8,128)(2,1)S(1)}, bf16[512,384]{1,0:T(8,128)(2,1)S(1)}, u32[]{:S(2)}, u32[]{:S(2)}) collective-permute-start(bf16[512,384]{1,0:T(8,128)(2,1)S(1)} %get-tuple-element.155), channel_id=1, source_target_pairs={{0,8},{4,12},{8,0},{12,4},{1,9},{5,13},{9,1},{13,5},{2,10},{6,14},... | collective-permute-start | bytes 1179656 | tf_op jit(solution)/shard_map/ppermute | solution.py:31
  308.6 24.8 %collective-permute-start.45 = (bf16[512,384]{1,0:T(8,128)(2,1)S(1)}, bf16[512,384]{1,0:T(8,128)(2,1)S(1)}, u32[]{:S(2)}, u32[]{:S(2)}) collective-permute-start(bf16[512,384]{1,0:T(8,128)(2,1)S(1)} %get-tuple-element.156), channel_id=1, source_target_pairs={{0,12},{4,0},{8,4},{12,8},{1,13},{5,1},{9,5},{13,9},{2,14},{6,2},{... | collective-permute-start | bytes 1179656 | tf_op jit(solution)/shard_map/ppermute | solution.py:31
  308.9 11.1 %collective-permute-start.47 = (bf16[512,256]{1,0:T(8,128)(2,1)S(1)}, bf16[512,256]{1,0:T(8,128)(2,1)S(1)}, u32[]{:S(2)}, u32[]{:S(2)}) collective-permute-start(bf16[512,256]{1,0:T(8,128)(2,1)S(1)} %get-tuple-element.163), channel_id=1, source_target_pairs={{0,16},{16,32},{32,48},{48,0},{1,17},{17,33},{33,49},{49,1},{2,18}... | collective-permute-start | bytes 786440 | tf_op jit(solution)/shard_map/ppermute | solution.py:31
  311.8 10.7 %collective-permute-start.48 = (bf16[512,256]{1,0:T(8,128)(2,1)S(1)}, bf16[512,256]{1,0:T(8,128)(2,1)S(1)}, u32[]{:S(2)}, u32[]{:S(2)}) collective-permute-start(bf16[512,256]{1,0:T(8,128)(2,1)S(1)} %get-tuple-element.164), channel_id=1, source_target_pairs={{0,48},{16,0},{32,16},{48,32},{1,49},{17,1},{33,17},{49,33},{2,50}... | collective-permute-start | bytes 786440 | tf_op jit(solution)/shard_map/ppermute | solution.py:31
  312.3 28.5 %copy-start.61 = (bf16[512,512]{1,0:T(8,128)(2,1)S(1)}, bf16[512,512]{1,0:T(8,128)(2,1)}, u32[]{:S(2)}) copy-start(bf16[512,512]{1,0:T(8,128)(2,1)} %copy-done.60) | copy-start | bytes 1572868
  334.1 9.6 %collective-permute-start.49 = (bf16[256,2048]{1,0:T(8,128)(2,1)}, bf16[256,2048]{1,0:T(8,128)(2,1)}, u32[]{:S(2)}, u32[]{:S(2)}) collective-permute-start(bf16[256,2048]{1,0:T(8,128)(2,1)} %get-tuple-element.165), channel_id=1, source_target_pairs={{0,1},{1,0},{2,3},{3,2},{4,5},{5,4},{6,7},{7,6},{8,9},{9,8},{10,11... | collective-permute-start | bytes 3145736 | tf_op jit(solution)/shard_map/ppermute | solution.py:31
  338.8 17.3 %collective-permute-start.36 = (bf16[128,2048]{1,0:T(8,128)(2,1)}, bf16[128,2048]{1,0:T(8,128)(2,1)S(1)}, u32[]{:S(2)}, u32[]{:S(2)}) collective-permute-start(bf16[128,2048]{1,0:T(8,128)(2,1)} %add_convert_fusion.2), channel_id=1, source_target_pairs={{0,64},{64,0},{1,65},{65,1},{2,66},{66,2},{3,67},{67,3},{4,68},{68... | collective-permute-start | bytes 1572872 | tf_op jit(solution)/shard_map/ppermute | solution.py:31
  345.0 19.8 %collective-permute-start.50 = (bf16[128,2048]{1,0:T(8,128)(2,1)S(1)}, bf16[128,2048]{1,0:T(8,128)(2,1)S(1)}, u32[]{:S(2)}, u32[]{:S(2)}) collective-permute-start(bf16[128,2048]{1,0:T(8,128)(2,1)S(1)} %add_convert_fusion.1), channel_id=1, source_target_pairs={{0,2},{2,0},{1,3},{3,1},{4,6},{6,4},{5,7},{7,5},{8,10},{10,8},{9,1... | collective-permute-start | bytes 1572872 | tf_op jit(solution)/shard_map/ppermute | solution.py:31
  345.8 5.5 %collective-permute-start.51 = (bf16[128,384]{1,0:T(8,128)(2,1)S(1)}, bf16[128,384]{1,0:T(8,128)(2,1)S(1)}, u32[]{:S(2)}, u32[]{:S(2)}) collective-permute-start(bf16[128,384]{1,0:T(8,128)(2,1)S(1)} %get-tuple-element.186), channel_id=1, source_target_pairs={{0,16},{16,32},{32,48},{48,0},{1,17},{17,33},{33,49},{49,1},{2,18}... | collective-permute-start | bytes 294920 | tf_op jit(solution)/shard_map/ppermute | solution.py:31
  346.1 7.6 %collective-permute-start.53 = (bf16[128,384]{1,0:T(8,128)(2,1)S(1)}, bf16[128,384]{1,0:T(8,128)(2,1)S(1)}, u32[]{:S(2)}, u32[]{:S(2)}) collective-permute-start(bf16[128,384]{1,0:T(8,128)(2,1)S(1)} %get-tuple-element.187), channel_id=1, source_target_pairs={{0,32},{16,48},{32,0},{48,16},{1,33},{17,49},{33,1},{49,17},{2,34}... | collective-permute-start | bytes 294920 | tf_op jit(solution)/shard_map/ppermute | solution.py:31
  349.3 5.8 %collective-permute-start.52 = (bf16[128,384]{1,0:T(8,128)(2,1)S(1)}, bf16[128,384]{1,0:T(8,128)(2,1)S(1)}, u32[]{:S(2)}, u32[]{:S(2)}) collective-permute-start(bf16[128,384]{1,0:T(8,128)(2,1)S(1)} %get-tuple-element.188), channel_id=1, source_target_pairs={{0,48},{16,0},{32,16},{48,32},{1,49},{17,1},{33,17},{49,33},{2,50}... | collective-permute-start | bytes 294920 | tf_op jit(solution)/shard_map/ppermute | solution.py:31
  351.3 19.3 %collective-permute-start.54 = (bf16[128,768]{1,0:T(8,128)(2,1)}, bf16[128,768]{1,0:T(8,128)(2,1)}, u32[]{:S(2)}, u32[]{:S(2)}) collective-permute-start(bf16[128,768]{1,0:T(8,128)(2,1)} %get-tuple-element.183), channel_id=1, source_target_pairs={{0,4},{4,8},{8,12},{12,0},{1,5},{5,9},{9,13},{13,1},{2,6},{6,10},{... | collective-permute-start | bytes 589832 | tf_op jit(solution)/shard_map/ppermute | solution.py:31
  353.8 16.8 %collective-permute-start.56 = (bf16[128,768]{1,0:T(8,128)(2,1)S(1)}, bf16[128,768]{1,0:T(8,128)(2,1)}, u32[]{:S(2)}, u32[]{:S(2)}) collective-permute-start(bf16[128,768]{1,0:T(8,128)(2,1)S(1)} %get-tuple-element.184), channel_id=1, source_target_pairs={{0,8},{4,12},{8,0},{12,4},{1,9},{5,13},{9,1},{13,5},{2,10},{6,14},... | collective-permute-start | bytes 589832 | tf_op jit(solution)/shard_map/ppermute | solution.py:31
  355.2 15.4 %collective-permute-start.55 = (bf16[128,768]{1,0:T(8,128)(2,1)S(1)}, bf16[128,768]{1,0:T(8,128)(2,1)}, u32[]{:S(2)}, u32[]{:S(2)}) collective-permute-start(bf16[128,768]{1,0:T(8,128)(2,1)S(1)} %get-tuple-element.185), channel_id=1, source_target_pairs={{0,12},{4,0},{8,4},{12,8},{1,13},{5,1},{9,5},{13,9},{2,14},{6,2},{... | collective-permute-start | bytes 589832 | tf_op jit(solution)/shard_map/ppermute | solution.py:31
  367.4 19.5 %collective-permute-start.58 = (bf16[64,2176]{1,0:T(8,128)(2,1)S(1)}, bf16[64,2176]{1,0:T(8,128)(2,1)S(1)}, u32[]{:S(2)}, u32[]{:S(2)}) collective-permute-start(bf16[64,2176]{1,0:T(8,128)(2,1)S(1)} %dynamic-slice_bitcast_fusion), channel_id=1, source_target_pairs={{0,64},{64,0},{1,65},{65,1},{2,66},{66,2},{3,67},{67,3},{4,68},{68... | collective-permute-start | bytes 835592 | tf_op jit(solution)/shard_map/ppermute | solution.py:31
  372.3 13.8 %collective-permute-start.57 = (bf16[64,1152]{1,0:T(8,128)(2,1)S(1)}, bf16[64,1152]{1,0:T(8,128)(2,1)S(1)}, u32[]{:S(2)}, u32[]{:S(2)}) collective-permute-start(bf16[64,1152]{1,0:T(8,128)(2,1)S(1)} %dynamic-slice_bitcast_fusion.5), channel_id=1, source_target_pairs={{0,64},{64,0},{1,65},{65,1},{2,66},{66,2},{3,67},{67,3},{4,68},{68... | collective-permute-start | bytes 442376 | tf_op jit(solution)/shard_map/ppermute | solution.py:31
  (78 other events, 597.6 us)
Sparse Core Ops, SparseCore 0:
  16.8 66.2 all-gather.2
  86.0 73.2 all-gather.4
  222.6 114.4 reduce-scatter.1

commit v3 on v2

--- a/solution.py
+++ b/solution.py
@@ -784,14 +784,14 @@
             pltpu.VMEM((n * span, HD), F32),
         ],
         compiler_params=params(40),
-        cost_estimate=cost(110 * 580_000_000 if first else 0, 1 << 20),
+        cost_estimate=cost(120 * 580_000_000 if first else 0, 1 << 20),
         name="attend_back",
     )(*operands)
 
 
 def weight_grads(odd, xs, cots, one, two):
     t, d = xs[0].shape
-    tile = 256
+    tile = 512
     rows = pl.BlockSpec((t, tile), lambda i: (0, i))
     width = one.shape[1] + two.shape[1]
     return pl.pallas_call(
@@ -875,8 +875,10 @@
     cot_near = jnp.concatenate([cotangent, cot_yl], 0)
     cot_far = swap(cot_near, "yh")
     other_mlp = swap(after(pick(shard_mlp, place("yh", 1), 0), kv_block), "yh")
-    mlp_pair = join_sides(pick(shard_mlp, place("yh"), 0), after(other_mlp, first_whole, blocks[1:], cot_near))
-    mlp_whole = lax.all_gather(mlp_pair, ("z", "x"), axis=0, tiled=True)
+    mlp_pair = join_sides(pick(shard_mlp, place("yh"), 0), other_mlp)
+    mlp_whole = lax.all_gather(
+        after(mlp_pair, first_whole, blocks[1:], cot_near), ("z", "x"), axis=0, tiled=True
+    )
     odd = place("yl").astype(jnp.int32).reshape(1, 1)
     mixed, log_total = attend(queries, blocks, window)
 
@@ -939,14 +941,12 @@
     ]
     out_arrived = [shift(out_parts[n], "z", n) for n in (2, 1, 3)]
     query_raw_grad, own_grads = attend_back(
-        (0,), after(queries, mlp_far), blocks[:1], window, log_total, (grad_turned, delta, query_part), turn=[cos, sin]
+        (0,), queries, blocks[:1], window, log_total, (grad_turned, delta, query_part), turn=[cos, sin]
     )
 
     out_sum = total(out_parts[0].astype(F32), after(out_arrived, query_raw_grad)).astype(BF)
-    output = settle(
-        middle, [mlp_own, mlp_arrived[:quarter], after(swap(mlp_far, "yh"), query_raw_grad)], BF
-    )
-    a_parts = wide_parts([scaled_in], after(query_raw_grad, arriving, out_arrived), (0, cut), "x")
+    mlp_across = swap(mlp_far, "yh")
+    a_parts = wide_parts([scaled_in], after(query_raw_grad, arriving, out_arrived, mlp_arrived), (0, cut), "x")
     a_arrived = [shift(a_parts[n], "x", n) for n in (2, 1, 3)]
     kv_raw_grad, *b_parts = last_parts(
         scaled_in, after(query_raw_grad, a_parts), cut, own_grads, arriving, cos, sin, "z"
@@ -960,14 +960,15 @@
     )
     in_own, in_across, in_cores = in_partial
     in_parts = scatter_rows((in_own, in_across, after(in_cores, a_arrived, b_arrived)))
-    input_grad = settle(grad_middle, in_parts, F32)
-
-    mlp_send = pick(mlp_sum.reshape(2, shard, -1), place("yh", 1), 0)
+
+    mlp_there = swap(pick(mlp_sum.reshape(2, shard, -1), place("yh", 1), 0), "yh")
     a_sum = wide_sum_next(total(a_parts[0].astype(F32), a_arrived).astype(BF), "z")
     b_sum = total(b_parts[0].astype(F32), b_arrived).astype(BF)
-    b_sum = wide_sum_next(jnp.concatenate([b_sum, out_sum], 1), "x", hold=[mlp_send])
+    b_sum = wide_sum_next(jnp.concatenate([b_sum, out_sum], 1), "x", hold=[mlp_there, mlp_across])
     sides = jnp.concatenate([a_sum, b_sum], 1)
     other_sides = swap(pick(sides.reshape(2, shard, -1), place("yh", 1), 0), "yh")
+    output = settle(middle, [mlp_own, mlp_arrived[:quarter], after(mlp_across, sides)], BF)
+    input_grad = settle(grad_middle, in_parts[:2] + [after(in_parts[2], sides)], F32)
     query_grad, key_grad, value_grad, out_grad = call(
         finish_attn_kernel, "finish_attn",
         [(query_weight.shape, F32), (key_weight.shape, F32), (value_weight.shape, F32),
@@ -977,7 +978,7 @@
     gate_grad, up_grad, down_grad = call(
         finish_mlp_kernel, "finish_mlp",
         [(gate_weight.shape, F32), (up_weight.shape, F32), (down_weight.shape[::-1], F32)],
-        [side, mlp_sum, swap(mlp_send, "yh")], scalars=1,
+        [side, mlp_sum, mlp_there], scalars=1,
     )
 
     ends = width_q - cut

time: 402 us -> 403 us (level)
    ppermute x59, waiting for transfers between devices: 98.2 us -> 103 us  [shift(): lax.ppermute(block, axis, [(i, (i + distance) % n) for i in range(n)])]
    unnamed x162 -> x112, local copies, waits for them, and re-layouts: 21.1 us -> 18.4 us
  transfers between devices with their start and end apart: 62 -> 62, of which waited for: 25 -> 21; matrix products, arithmetic and copies ran while one was open for 5% -> 5% of each run, Pallas kernels for 26% -> 27%
where the time goes in v3:
time: 403 us; the launch traced here: 395 us
  Pallas kernels  135 us (33%)
  waiting for transfers between devices  105 us (26%)
  starting transfers between devices  84.5 us (21%)
  local copies, waits for them, and re-layouts  27.1 us (7%)
  blocking collectives  16.8 us (4%)
  between operations  15.1 us (4%)
  other arithmetic  12.1 us (3%)
    ppermute x59, waiting for transfers between devices, shift(): lax.ppermute(block, axis, [(i, (i + distance) % n) for i in range(n)])  103 us
    ppermute x59, starting transfers between devices, shift(): lax.ppermute(block, axis, [(i, (i + distance) % n) for i in range(n)])  84.4 us
    pallas_call x2, Pallas kernels, attend_back(): pl.pallas_call(functools.partial(attend_back_kernel, distances, first, la...  27.4 us
    pallas_call x4, Pallas kernels, rows_out(): pl.pallas_call(functools.partial(rows_out_kernel, terms, places), grid=(d...  23.8 us
    pallas_call x1, Pallas kernels, hidden_units(): pl.pallas_call(functools.partial(hidden_kernel, width), out_shape=(jax.Sh...  20.1 us
    unnamed x112, local copies, waits for them, and re-layouts  18.4 us
    pallas_call x1, Pallas kernels, attend(): pl.pallas_call(attend_kernel, out_shape=(jax.ShapeDtypeStruct((span, widt...  17.6 us
    psum x1, blocking collectives, per_device(): gain_parts = lax.psum(gain_parts, ('yh',) + TP)  16.8 us
  transfers between devices with their start and end apart: 62, of which 21 were waited for; matrix products, arithmetic and copies ran while one was open for 5% of the time, Pallas kernels for 27%

profile of v3, /device:TPU:1, one launch (start us, length us, event | category | flops | bytes accessed | tf_op | source)
XLA Modules:
  0.0 395.2 jit_solution(18285840417629851705)
XLA Ops:
  8.1 3.8 collective-permute-start.10
  11.9 2.9 collective-permute-done.10
  16.7 2.8 pack.1
  19.5 2.9 collective-permute-start
  23.0 1.7 dynamic-slice_bitcast_fusion.1
  25.6 2.5 collective-permute-start.5
  28.1 1.7 collective-permute-start.6
  30.5 2.7 collective-permute-done.4
  33.2 1.7 collective-permute-start.7
  35.2 4.2 %collective-permute-start.1 = (bf16[128,2048]{1,0:T(8,128)(2,1)}, bf16[128,2048]{1,0:T(8,128)(2,1)S(1)}, u32[]{:S(2)}, u32[]{:S(2)}) collective-permute-start(bf16[128,2048]{1,0:T(8,128)(2,1)} %get-tuple-element.98.refs_0_.base_ref.refs_4_), channel_id=1, source_target_pairs={{0,1},{1,0},{2,3},{3,2},{4,5},{5,4},{6,7},{7,6},{8,9},{9,8},{10,11... | collective-permute-start | bytes 1572872 | tf_op jit(solution)/shard_map/ppermute | solution.py:31
  39.4 3.3 collective-permute-start.9
  44.4 2.2 collective-permute-done.7
  46.6 7.5 %collective-permute-done.8 = bf16[4,128,256]{2,1,0:T(8,128)(2,1)S(1)} collective-permute-done((bf16[4,128,256]{2,1,0:T(8,128)(2,1)S(1)}, bf16[4,128,256]{2,1,0:T(8,128)(2,1)S(1)}, u32[]{:S(2)}, u32[]{:S(2)}) %collective-permute-start.8) | collective-permute-done | bytes 262176 | tf_op jit(solution)/shard_map/ppermute | solution.py:31
  58.0 3.0 collective-permute-start.26
  61.8 3.0 collective-permute-start.13
  70.0 8.9 %collective-permute-done.14 = bf16[128,2048]{1,0:T(8,128)(2,1)} collective-permute-done((bf16[128,2048]{1,0:T(8,128)(2,1)S(1)}, bf16[128,2048]{1,0:T(8,128)(2,1)}, u32[]{:S(2)}, u32[]{:S(2)}) %collective-permute-start.14) | collective-permute-done | bytes 524320 | tf_op jit(solution)/shard_map/ppermute | solution.py:31
  78.9 1.9 constant_dynamic-update-slice_fusion
  80.8 2.2 all-gather.3.cloned.1.call-done.w_ref.refs_1_.refs_7_.refs_2_
  83.1 3.2 collective-permute-start.15
  86.3 2.2 copy-done.2
  90.0 17.6 %attend.1 = (bf16[512,512]{1,0:T(8,128)(2,1)S(1)}, f32[8,512]{1,0:T(8,128)S(1)}) custom-call(bf16[512,512]{1,0:T(8,128)(2,1)S(1)} %queries.1.q_ref, bf16[512,128]{1,0:T(8,128)(2,1)S(1)} %get-tuple-element.100.refs_0_, bf16[512,128]{1,0:T(8,128)(2,1)} %collective-permute-done.11.refs_1_.refs_0_, bf16[512,128]{1,0:T(8,128)(2,1)} %collective-permute-done.12.refs_2_.refs_1_, ...), custom_call_target="tpu_custom_call" | custom-call | flops 5800000000 | bytes 1048576 | tf_op jit(solution)/shard_map/attend/pallas_call | solution.py:737
  108.8 1.8 rows_out.4
  110.7 1.9 collective-permute-start.16
  116.4 11.8 %collective-permute-done.17.refs_2_ = bf16[128,2048]{1,0:T(8,128)(2,1)S(1)} collective-permute-done((bf16[128,2048]{1,0:T(8,128)(2,1)S(1)}, bf16[128,2048]{1,0:T(8,128)(2,1)S(1)}, u32[]{:S(2)}, u32[]{:S(2)}) %collective-permute-start.17) | collective-permute-done | bytes 524320 | tf_op jit(solution)/shard_map/ppermute | solution.py:31
  130.4 2.3 collective-permute-start.20
  134.2 2.1 collective-permute-start.21
  136.3 7.4 %collective-permute-done.20.refs_3_ = bf16[128,2048]{1,0:T(8,128)(2,1)} collective-permute-done((bf16[128,2048]{1,0:T(8,128)(2,1)}, bf16[128,2048]{1,0:T(8,128)(2,1)}, u32[]{:S(2)}, u32[]{:S(2)}) %collective-permute-start.20) | collective-permute-done | bytes 524320 | tf_op jit(solution)/shard_map/ppermute | solution.py:31
  143.6 12.8 %collective-permute-start.24 = (bf16[128,2048]{1,0:T(8,128)(2,1)}, bf16[128,2048]{1,0:T(8,128)(2,1)}, u32[]{:S(2)}, u32[]{:S(2)}) collective-permute-start(bf16[128,2048]{1,0:T(8,128)(2,1)} %collective-permute-done.20.refs_3_), channel_id=1, source_target_pairs={{0,1},{1,0},{2,3},{3,2},{4,5},{5,4},{6,7},{7,6},{8,9},{9,8},{10,11... | collective-permute-start | bytes 1572872 | tf_op jit(solution)/shard_map/ppermute | solution.py:31
  156.4 3.2 collective-permute-done.18.refs_1_
  160.5 1.9 collective-permute-done.22.refs_5_
  162.4 20.1 %hidden_units.1 = (bf16[1024,768]{1,0:T(8,128)(2,1)}, bf16[1024,1408]{1,0:T(8,128)(2,1)}) custom-call(s32[1,1]{1,0:T(1,128)} %bitcast.18.odd_ref, bf16[128,2048]{1,0:T(8,128)(2,1)} %get-tuple-element.124.refs_0_, bf16[128,2048]{1,0:T(8,128)(2,1)} %collective-permute-done.18.refs_1_, bf16[128,2048]{1,0:T(8,128)(2,1)} %collective-permute-done.19.refs_2_, ...), custom_call_target="tpu_custom_call" | custom-call | flops 8053063680 | bytes 7864320 | tf_op jit(solution)/shard_map/hidden_units/pallas_call | solution.py:610
  182.4 7.4 %rows_out.5 = bf16[512,2048]{1,0:T(8,128)(2,1)} custom-call(bf16[1024,1408]{1,0:T(8,128)(2,1)} %get-tuple-element.120.refs_0_.refs_10_, bf16[2048,2176]{1,0:T(8,128)(2,1)} %all-gather.5.cloned.1.call-done.refs_10_.refs_1_), custom_call_target="tpu_custom_call" | custom-call | flops 2952790016 | bytes 6291456 | tf_op jit(solution)/shard_map/rows_out/pallas_call | solution.py:667
  190.3 7.4 %rows_out.6.one_ref = bf16[512,2048]{1,0:T(8,128)(2,1)} custom-call(bf16[1024,1408]{1,0:T(8,128)(2,1)} %get-tuple-element.120.refs_0_.refs_10_, bf16[2048,2176]{1,0:T(8,128)(2,1)} %all-gather.5.cloned.1.call-done.refs_10_.refs_1_), custom_call_target="tpu_custom_call" | custom-call | flops 2952790016 | bytes 6291456 | tf_op jit(solution)/shard_map/rows_out/pallas_call | solution.py:667
  197.8 1.6 copy-done.7
  199.3 1.5 add_pieces.1
  203.5 15.5 %weight_grads.1 = bf16[2048,2176]{1,0:T(8,128)(2,1)} custom-call(s32[1,1]{1,0:T(1,128)} %bitcast.18.odd_ref, bf16[128,2048]{1,0:T(8,128)(2,1)} %get-tuple-element.124.refs_0_, bf16[128,2048]{1,0:T(8,128)(2,1)} %collective-permute-done.18.refs_1_, bf16[128,2048]{1,0:T(8,128)(2,1)} %collective-permute-done.19.refs_2_, ...), custom_call_target="tpu_custom_call" | custom-call | flops 9126805504 | bytes 17301504 | tf_op jit(solution)/shard_map/weight_grads/pallas_call | solution.py:797
  219.0 7.2 %rows_out.7 = (bf16[512,2048]{1,0:T(8,128)(2,1)}, bf16[512,2048]{1,0:T(8,128)(2,1)}) custom-call(bf16[1024,768]{1,0:T(8,128)(2,1)} %get-tuple-element.125.refs_11_.refs_0_, bf16[2048,2176]{1,0:T(8,128)(2,1)} %all-gather.5.cloned.1.call-done.refs_10_.refs_1_), custom_call_target="tpu_custom_call" | custom-call | flops 3221225472 | bytes 6291456 | tf_op jit(solution)/shard_map/rows_out/pallas_call | solution.py:667
  226.3 3.3 collective-permute-done.29.refs_2_
  229.6 2.9 middle_grad.1
  234.0 13.8 %collective-permute-done.33.refs_2_.refs_10_ = bf16[128,2048]{1,0:T(8,128)(2,1)S(1)} collective-permute-done((bf16[128,2048]{1,0:T(8,128)(2,1)}, bf16[128,2048]{1,0:T(8,128)(2,1)S(1)}, u32[]{:S(2)}, u32[]{:S(2)}) %collective-permute-start.33) | collective-permute-done | bytes 524320 | tf_op jit(solution)/shard_map/ppermute | solution.py:31
  252.3 2.9 wide_parts.2
  255.2 1.6 collective-permute-start.41
  256.8 2.6 collective-permute-start.40
  260.5 2.4 pair_pieces.1
  264.3 20.7 %attend_back.2 = (f32[512,512]{1,0:T(8,128)S(1)}, bf16[1536,128]{1,0:T(8,128)(2,1)S(1)}, bf16[512,512]{1,0:T(8,128)(2,1)S(1)}, f32[8,512]{1,0:T(8,128)S(1)}) custom-call(bf16[512,512]{1,0:T(8,128)(2,1)S(1)} %copy-done.16, bf16[512,128]{1,0:T(8,128)(2,1)} %collective-permute-done.11.refs_1_.refs_0_, bf16[512,128]{1,0:T(8,128)(2,1)} %collective-permute-done.12.refs_2_.refs_1_, ...), custom_call_target="tpu_custom_call" | custom-call | flops 139200004096 | bytes 1048576 | tf_op jit(solution)/shard_map/attend_back/pallas_call | solution.py:774
  285.3 1.6 collective-permute-start.38
  286.8 7.9 %collective-permute-done.40 = bf16[512,512]{1,0:T(8,128)(2,1)S(1)} collective-permute-done((bf16[512,512]{1,0:T(8,128)(2,1)S(1)}, bf16[512,512]{1,0:T(8,128)(2,1)S(1)}, u32[]{:S(2)}, u32[]{:S(2)}) %collective-permute-start.40) | collective-permute-done | bytes 524320 | tf_op jit(solution)/shard_map/ppermute | solution.py:31
  294.8 2.2 collective-permute-start.37
  297.6 6.7 %attend_back.3 = (bf16[512,512]{1,0:T(8,128)(2,1)S(1)}, f32[512,128]{1,0:T(8,128)S(1)}) custom-call(bf16[512,512]{1,0:T(8,128)(2,1)S(1)} %copy-done.16, bf16[512,128]{1,0:T(8,128)(2,1)S(1)} %get-tuple-element.100.refs_0_, s32[1,1]{1,0:T(1,128)} %bitcast.16.refs_4_.refs_3_.refs_1_, s32[1,512]{1,0:T(1,128)S(1)} %bitcast.82, ...), custom_call_target="tpu_custom_call" | custom-call | bytes 1048576 | tf_op jit(solution)/shard_map/attend_back/pallas_call | solution.py:774
  309.3 2.1 collective-permute-start.45
  311.4 3.7 collective-permute-done.49
  316.3 4.9 %rows_grad.1 = (bf16[128,2048]{1,0:T(8,128)(2,1)S(1)}, bf16[128,2048]{1,0:T(8,128)(2,1)S(1)}, bf16[256,2048]{1,0:T(8,128)(2,1)}) custom-call(bf16[512,512]{1,0:T(8,128)(2,1)S(1)} %get-tuple-element.154.refs_1_.dq_ref.refs_0_, bf16[512,128]{1,0:T(8,128)(2,1)S(1)} %get-tuple-element.168.refs_1_, bf16[2048,1024]{1,0:T(8,128)(2,1)S(1)} %copy-done.4, ...), custom_call_target="tpu_custom_call" | custom-call | tf_op jit(solution)/shard_map/rows_grad/pallas_call | solution.py:647
  321.3 3.4 collective-permute-done.50
  325.1 12.0 %collective-permute-done.44 = bf16[512,384]{1,0:T(8,128)(2,1)S(1)} collective-permute-done((bf16[512,384]{1,0:T(8,128)(2,1)S(1)}, bf16[512,384]{1,0:T(8,128)(2,1)S(1)}, u32[]{:S(2)}, u32[]{:S(2)}) %collective-permute-start.44) | collective-permute-done | bytes 393248 | tf_op jit(solution)/shard_map/ppermute | solution.py:31
  338.7 1.7 collective-permute-start.48
  340.3 2.0 collective-permute-start.47
  343.1 3.3 collective-permute-done.46
  346.4 2.3 collective-permute-start.55
  350.3 1.8 collective-permute-start.53
  355.5 3.2 collective-permute-done.53.other_ref
  360.3 1.7 collective-permute-start.58
  362.0 16.8 %psum.7 = f32[2,2,64]{2,1,0:T(2,128)S(1)} all-reduce(f32[2,2,64]{2,1,0:T(2,128)S(1)} %reshape.102), channel_id=1, replica_groups=mesh['yh'=2,'z'=4,'x'=4,'yl'=2,'core'=2] {'yh','yl','core'}, use_global_device_ids=true, to_apply=%region_3.4 | all-reduce | flops 256 | bytes 2048 | tf_op jit(solution)/shard_map/psum | solution.py:995
  380.1 2.3 settle.2
  383.5 2.5 settle.3
  (251 shorter events, 60.4 us)
Async XLA Ops:
  7.2 75.9 %all-gather.3.cloned.1.call-start = ((), (), s32[]{:S(2)}) async-start(), calls=%async_computation.1 | async-start | bytes 4456448 | tf_op jit(solution)/shard_map/all_gather | solution.py:849
  8.1 6.8 %collective-permute-start.10 = (bf16[64,1024]{1,0:T(8,128)(2,1)S(1)}, bf16[64,1024]{1,0:T(8,128)(2,1)S(1)}, u32[]{:S(2)}, u32[]{:S(2)}) collective-permute-start(bf16[64,1024]{1,0:T(8,128)(2,1)S(1)} %pad_maximum_fusion.4), channel_id=1, source_target_pairs={{0,64},{64,0},{1,65},{65,1},{2,66},{66,2},{3,67},{67,3},{4,68},{68... | collective-permute-start | bytes 393224 | tf_op jit(solution)/shard_map/ppermute | solution.py:31
  16.6 145.7 %all-gather.5.cloned.1.call-start = ((), (), s32[]{:S(2)}) async-start(), calls=%async_computation.2 | async-start | bytes 9469952 | tf_op jit(solution)/shard_map/all_gather | solution.py:879
  19.5 5.2 %collective-permute-start = (bf16[64,256]{1,0:T(8,128)(2,1)}, bf16[64,256]{1,0:T(8,128)(2,1)S(1)}, u32[]{:S(2)}, u32[]{:S(2)}) collective-permute-start(bf16[64,256]{1,0:T(8,128)(2,1)} %get-tuple-element.97), channel_id=1, source_target_pairs={{0,64},{64,0},{1,65},{65,1},{2,66},{66,2},{3,67},{67,3},{4,68},{68... | collective-permute-start | bytes 98312 | tf_op jit(solution)/shard_map/ppermute | solution.py:31
  25.6 7.6 %collective-permute-start.5 = (bf16[128,256]{1,0:T(8,128)(2,1)S(1)}, bf16[128,256]{1,0:T(8,128)(2,1)S(1)}, u32[]{:S(2)}, u32[]{:S(2)}) collective-permute-start(bf16[128,256]{1,0:T(8,128)(2,1)S(1)} %pad_maximum_fusion.5), channel_id=1, source_target_pairs={{0,12},{4,0},{8,4},{12,8},{1,13},{5,1},{9,5},{13,9},{2,14},{6,2},{... | collective-permute-start | bytes 196616 | tf_op jit(solution)/shard_map/ppermute | solution.py:31
  28.1 5.0 %collective-permute-start.4 = (bf16[128,256]{1,0:T(8,128)(2,1)S(1)}, bf16[128,256]{1,0:T(8,128)(2,1)S(1)}, u32[]{:S(2)}, u32[]{:S(2)}) collective-permute-start(bf16[128,256]{1,0:T(8,128)(2,1)S(1)} %pad_maximum_fusion.5), channel_id=1, source_target_pairs={{0,4},{4,8},{8,12},{12,0},{1,5},{5,9},{9,13},{13,1},{2,6},{6,10},{... | collective-permute-start | bytes 196616 | tf_op jit(solution)/shard_map/ppermute | solution.py:31
  28.1 5.1 %collective-permute-start.6 = (bf16[128,256]{1,0:T(8,128)(2,1)S(1)}, bf16[128,256]{1,0:T(8,128)(2,1)S(1)}, u32[]{:S(2)}, u32[]{:S(2)}) collective-permute-start(bf16[128,256]{1,0:T(8,128)(2,1)S(1)} %pad_maximum_fusion.5), channel_id=1, source_target_pairs={{0,8},{4,12},{8,0},{12,4},{1,9},{5,13},{9,1},{13,5},{2,10},{6,14},... | collective-permute-start | bytes 196616 | tf_op jit(solution)/shard_map/ppermute | solution.py:31
  29.8 13.7 %collective-permute-start.2 = (bf16[128,2048]{1,0:T(8,128)(2,1)}, bf16[128,2048]{1,0:T(8,128)(2,1)S(1)}, u32[]{:S(2)}, u32[]{:S(2)}) collective-permute-start(bf16[128,2048]{1,0:T(8,128)(2,1)} %get-tuple-element.98.refs_0_.base_ref.refs_4_), channel_id=1, source_target_pairs={{0,2},{2,0},{1,3},{3,1},{4,6},{6,4},{5,7},{7,5},{8,10},{10,8},{9,1... | collective-permute-start | bytes 1572872 | tf_op jit(solution)/shard_map/ppermute | solution.py:31
  33.2 13.3 %collective-permute-start.7 = (bf16[4,128,256]{2,1,0:T(8,128)(2,1)S(1)}, bf16[4,128,256]{2,1,0:T(8,128)(2,1)S(1)}, u32[]{:S(2)}, u32[]{:S(2)}) collective-permute-start(bf16[4,128,256]{2,1,0:T(8,128)(2,1)S(1)} %bitcast_dynamic-update-slice_fusion.4), channel_id=1, source_target_pairs={{0,16},{16,32},{32,48},{48,0},{1,17},{17,33},{33,49},{49,1},{2,18}... | collective-permute-start | bytes 786440 | tf_op jit(solution)/shard_map/ppermute | solution.py:31
  35.2 18.9 %collective-permute-start.1 = (bf16[128,2048]{1,0:T(8,128)(2,1)}, bf16[128,2048]{1,0:T(8,128)(2,1)S(1)}, u32[]{:S(2)}, u32[]{:S(2)}) collective-permute-start(bf16[128,2048]{1,0:T(8,128)(2,1)} %get-tuple-element.98.refs_0_.base_ref.refs_4_), channel_id=1, source_target_pairs={{0,1},{1,0},{2,3},{3,2},{4,5},{5,4},{6,7},{7,6},{8,9},{9,8},{10,11... | collective-permute-start | bytes 1572872 | tf_op jit(solution)/shard_map/ppermute | solution.py:31
  39.4 14.7 %collective-permute-start.9 = (bf16[4,128,256]{2,1,0:T(8,128)(2,1)S(1)}, bf16[4,128,256]{2,1,0:T(8,128)(2,1)S(1)}, u32[]{:S(2)}, u32[]{:S(2)}) collective-permute-start(bf16[4,128,256]{2,1,0:T(8,128)(2,1)S(1)} %bitcast_dynamic-update-slice_fusion.4), channel_id=1, source_target_pairs={{0,32},{16,48},{32,0},{48,16},{1,33},{17,49},{33,1},{49,17},{2,34}... | collective-permute-start | bytes 786440 | tf_op jit(solution)/shard_map/ppermute | solution.py:31
  42.7 11.3 %collective-permute-start.8 = (bf16[4,128,256]{2,1,0:T(8,128)(2,1)S(1)}, bf16[4,128,256]{2,1,0:T(8,128)(2,1)S(1)}, u32[]{:S(2)}, u32[]{:S(2)}) collective-permute-start(bf16[4,128,256]{2,1,0:T(8,128)(2,1)S(1)} %bitcast_dynamic-update-slice_fusion.4), channel_id=1, source_target_pairs={{0,48},{16,0},{32,16},{48,32},{1,49},{17,1},{33,17},{49,33},{2,50}... | collective-permute-start | bytes 786440 | tf_op jit(solution)/shard_map/ppermute | solution.py:31
  43.6 10.6 %collective-permute-start.3 = (bf16[128,2048]{1,0:T(8,128)(2,1)S(1)}, bf16[128,2048]{1,0:T(8,128)(2,1)S(1)}, u32[]{:S(2)}, u32[]{:S(2)}) collective-permute-start(bf16[128,2048]{1,0:T(8,128)(2,1)S(1)} %collective-permute-done.2.refs_2_.refs_6_), channel_id=1, source_target_pairs={{0,1},{1,0},{2,3},{3,2},{4,5},{5,4},{6,7},{7,6},{8,9},{9,8},{10,11... | collective-permute-start | bytes 1572872 | tf_op jit(solution)/shard_map/ppermute | solution.py:31
  58.0 9.2 %collective-permute-start.26 = (bf16[64,2176]{1,0:T(8,128)(2,1)}, bf16[64,2176]{1,0:T(8,128)(2,1)}, u32[]{:S(2)}, u32[]{:S(2)}) collective-permute-start(bf16[64,2176]{1,0:T(8,128)(2,1)} %dynamic-slice_bitcast_fusion.1), channel_id=1, source_target_pairs={{0,64},{64,0},{1,65},{65,1},{2,66},{66,2},{3,67},{67,3},{4,68},{68... | collective-permute-start | bytes 835592 | tf_op jit(solution)/shard_map/ppermute | solution.py:31
  61.8 19.0 %collective-permute-start.13 = (bf16[512,128]{1,0:T(8,128)(2,1)S(1)}, bf16[512,128]{1,0:T(8,128)(2,1)}, u32[]{:S(2)}, u32[]{:S(2)}) collective-permute-start(bf16[512,128]{1,0:T(8,128)(2,1)S(1)} %get-tuple-element.100.refs_0_), channel_id=1, source_target_pairs={{0,12},{4,0},{8,4},{12,8},{1,13},{5,1},{9,5},{13,9},{2,14},{6,2},{... | collective-permute-start | bytes 393224 | tf_op jit(solution)/shard_map/ppermute | solution.py:31
  64.8 16.0 %collective-permute-start.12 = (bf16[512,128]{1,0:T(8,128)(2,1)S(1)}, bf16[512,128]{1,0:T(8,128)(2,1)}, u32[]{:S(2)}, u32[]{:S(2)}) collective-permute-start(bf16[512,128]{1,0:T(8,128)(2,1)S(1)} %get-tuple-element.100.refs_0_), channel_id=1, source_target_pairs={{0,8},{4,12},{8,0},{12,4},{1,9},{5,13},{9,1},{13,5},{2,10},{6,14},... | collective-permute-start | bytes 393224 | tf_op jit(solution)/shard_map/ppermute | solution.py:31
  64.8 16.0 %collective-permute-start.11 = (bf16[512,128]{1,0:T(8,128)(2,1)S(1)}, bf16[512,128]{1,0:T(8,128)(2,1)}, u32[]{:S(2)}, u32[]{:S(2)}) collective-permute-start(bf16[512,128]{1,0:T(8,128)(2,1)S(1)} %get-tuple-element.100.refs_0_), channel_id=1, source_target_pairs={{0,4},{4,8},{8,12},{12,0},{1,5},{5,9},{9,13},{13,1},{2,6},{6,10},{... | collective-permute-start | bytes 393224 | tf_op jit(solution)/shard_map/ppermute | solution.py:31
  65.4 13.5 %collective-permute-start.14 = (bf16[128,2048]{1,0:T(8,128)(2,1)S(1)}, bf16[128,2048]{1,0:T(8,128)(2,1)}, u32[]{:S(2)}, u32[]{:S(2)}) collective-permute-start(bf16[128,2048]{1,0:T(8,128)(2,1)S(1)} %copy-done.14), channel_id=1, source_target_pairs={{0,2},{2,0},{1,3},{3,1},{4,6},{6,4},{5,7},{7,5},{8,10},{10,8},{9,1... | collective-permute-start | bytes 1572872 | tf_op jit(solution)/shard_map/ppermute | solution.py:31
  83.1 266.2 %reduce-scatter.2.cloned.1.call-start = ((), (), s32[]{:S(2)}) async-start(), calls=%async_computation.3 | async-start | bytes 9469952 | tf_op jit(solution)/shard_map/reduce_scatter | solution.py:921
  83.1 25.7 %collective-permute-start.15 = (bf16[256,2048]{1,0:T(8,128)(2,1)}, bf16[256,2048]{1,0:T(8,128)(2,1)S(1)}, u32[]{:S(2)}, u32[]{:S(2)}) collective-permute-start(bf16[256,2048]{1,0:T(8,128)(2,1)} %constant_dynamic-update-slice_fusion), channel_id=1, source_target_pairs={{0,64},{64,0},{1,65},{65,1},{2,66},{66,2},{3,67},{67,3},{4,68},{68... | collective-permute-start | bytes 3145736 | tf_op jit(solution)/shard_map/ppermute | solution.py:31
  110.7 4.2 %collective-permute-start.16 = (bf16[256,2048]{1,0:T(8,128)(2,1)S(1)}, bf16[256,2048]{1,0:T(8,128)(2,1)S(1)}, u32[]{:S(2)}, u32[]{:S(2)}) collective-permute-start(bf16[256,2048]{1,0:T(8,128)(2,1)S(1)} %get-tuple-element.109), channel_id=1, source_target_pairs={{0,1},{1,0},{2,3},{3,2},{4,5},{5,4},{6,7},{7,6},{8,9},{9,8},{10,11... | collective-permute-start | bytes 3145736 | tf_op jit(solution)/shard_map/ppermute | solution.py:31
  114.8 45.6 %collective-permute-start.25 = (bf16[512,2048]{1,0:T(8,128)(2,1)}, bf16[512,2048]{1,0:T(8,128)(2,1)}, u32[]{:S(2)}, u32[]{:S(2)}) collective-permute-start(bf16[512,2048]{1,0:T(8,128)(2,1)} %constant_dynamic-update-slice_fusion.2.refs_8_), channel_id=1, source_target_pairs={{0,1},{1,0},{2,3},{3,2},{4,5},{5,4},{6,7},{7,6},{8,9},{9,8},{10,11... | collective-permute-start | bytes 6291464 | tf_op jit(solution)/shard_map/ppermute | solution.py:31
  115.0 13.2 %collective-permute-start.17 = (bf16[128,2048]{1,0:T(8,128)(2,1)S(1)}, bf16[128,2048]{1,0:T(8,128)(2,1)S(1)}, u32[]{:S(2)}, u32[]{:S(2)}) collective-permute-start(bf16[128,2048]{1,0:T(8,128)(2,1)S(1)} %add_convert_fusion.3), channel_id=1, source_target_pairs={{0,2},{2,0},{1,3},{3,1},{4,6},{6,4},{5,7},{7,5},{8,10},{10,8},{9,1... | collective-permute-start | bytes 1572872 | tf_op jit(solution)/shard_map/ppermute | solution.py:31
  130.4 13.2 %collective-permute-start.20 = (bf16[128,2048]{1,0:T(8,128)(2,1)}, bf16[128,2048]{1,0:T(8,128)(2,1)}, u32[]{:S(2)}, u32[]{:S(2)}) collective-permute-start(bf16[128,2048]{1,0:T(8,128)(2,1)} %get-tuple-element.124.refs_0_), channel_id=1, source_target_pairs={{0,66},{2,0},{64,2},{66,64},{1,67},{3,1},{65,3},{67,65},{4,70},{6,... | collective-permute-start | bytes 1572872 | tf_op jit(solution)/shard_map/ppermute | solution.py:31
  132.7 23.7 %collective-permute-start.19 = (bf16[128,2048]{1,0:T(8,128)(2,1)}, bf16[128,2048]{1,0:T(8,128)(2,1)}, u32[]{:S(2)}, u32[]{:S(2)}) collective-permute-start(bf16[128,2048]{1,0:T(8,128)(2,1)} %get-tuple-element.124.refs_0_), channel_id=1, source_target_pairs={{0,64},{2,66},{64,0},{66,2},{1,65},{3,67},{65,1},{67,3},{4,68},{6,... | collective-permute-start | bytes 1572872 | tf_op jit(solution)/shard_map/ppermute | solution.py:31
  133.5 26.1 %collective-permute-start.18 = (bf16[128,2048]{1,0:T(8,128)(2,1)}, bf16[128,2048]{1,0:T(8,128)(2,1)}, u32[]{:S(2)}, u32[]{:S(2)}) collective-permute-start(bf16[128,2048]{1,0:T(8,128)(2,1)} %get-tuple-element.124.refs_0_), channel_id=1, source_target_pairs={{0,2},{2,64},{64,66},{66,0},{1,3},{3,65},{65,67},{67,1},{4,6},{6,6... | collective-permute-start | bytes 1572872 | tf_op jit(solution)/shard_map/ppermute | solution.py:31
  134.2 26.3 %collective-permute-start.21 = (bf16[128,2048]{1,0:T(8,128)(2,1)}, bf16[128,2048]{1,0:T(8,128)(2,1)}, u32[]{:S(2)}, u32[]{:S(2)}) collective-permute-start(bf16[128,2048]{1,0:T(8,128)(2,1)} %get-tuple-element.124.refs_0_), channel_id=1, source_target_pairs={{0,1},{1,0},{2,3},{3,2},{4,5},{5,4},{6,7},{7,6},{8,9},{9,8},{10,11... | collective-permute-start | bytes 1572872 | tf_op jit(solution)/shard_map/ppermute | solution.py:31
  143.6 16.9 %collective-permute-start.24 = (bf16[128,2048]{1,0:T(8,128)(2,1)}, bf16[128,2048]{1,0:T(8,128)(2,1)}, u32[]{:S(2)}, u32[]{:S(2)}) collective-permute-start(bf16[128,2048]{1,0:T(8,128)(2,1)} %collective-permute-done.20.refs_3_), channel_id=1, source_target_pairs={{0,1},{1,0},{2,3},{3,2},{4,5},{5,4},{6,7},{7,6},{8,9},{9,8},{10,11... | collective-permute-start | bytes 1572872 | tf_op jit(solution)/shard_map/ppermute | solution.py:31
  156.4 4.1 %collective-permute-start.23 = (bf16[128,2048]{1,0:T(8,128)(2,1)}, bf16[128,2048]{1,0:T(8,128)(2,1)}, u32[]{:S(2)}, u32[]{:S(2)}) collective-permute-start(bf16[128,2048]{1,0:T(8,128)(2,1)} %collective-permute-done.19.refs_2_), channel_id=1, source_target_pairs={{0,1},{1,0},{2,3},{3,2},{4,5},{5,4},{6,7},{7,6},{8,9},{9,8},{10,11... | collective-permute-start | bytes 1572872 | tf_op jit(solution)/shard_map/ppermute | solution.py:31
  159.6 2.8 collective-permute-start.22
  189.8 7.9 %collective-permute-start.27 = (bf16[512,2048]{1,0:T(8,128)(2,1)}, bf16[512,2048]{1,0:T(8,128)(2,1)S(1)}, u32[]{:S(2)}, u32[]{:S(2)}) collective-permute-start(bf16[512,2048]{1,0:T(8,128)(2,1)} %rows_out.5), channel_id=1, source_target_pairs={{0,1},{1,0},{2,3},{3,2},{4,5},{5,4},{6,7},{7,6},{8,9},{9,8},{10,11... | collective-permute-start | bytes 6291464 | tf_op jit(solution)/shard_map/ppermute | solution.py:31
  201.8 24.4 %collective-permute-start.28 = (bf16[128,2048]{1,0:T(8,128)(2,1)}, bf16[128,2048]{1,0:T(8,128)(2,1)}, u32[]{:S(2)}, u32[]{:S(2)}) collective-permute-start(bf16[128,2048]{1,0:T(8,128)(2,1)} %get-tuple-element.121), channel_id=1, source_target_pairs={{0,66},{2,0},{64,2},{66,64},{1,67},{3,1},{65,3},{67,65},{4,70},{6,... | collective-permute-start | bytes 1572872 | tf_op jit(solution)/shard_map/ppermute | solution.py:31
  202.7 23.6 %collective-permute-start.30 = (bf16[128,2048]{1,0:T(8,128)(2,1)}, bf16[128,2048]{1,0:T(8,128)(2,1)}, u32[]{:S(2)}, u32[]{:S(2)}) collective-permute-start(bf16[128,2048]{1,0:T(8,128)(2,1)} %get-tuple-element.122), channel_id=1, source_target_pairs={{0,64},{2,66},{64,0},{66,2},{1,65},{3,67},{65,1},{67,3},{4,68},{6,... | collective-permute-start | bytes 1572872 | tf_op jit(solution)/shard_map/ppermute | solution.py:31
  203.0 26.6 %collective-permute-start.29 = (bf16[128,2048]{1,0:T(8,128)(2,1)}, bf16[128,2048]{1,0:T(8,128)(2,1)}, u32[]{:S(2)}, u32[]{:S(2)}) collective-permute-start(bf16[128,2048]{1,0:T(8,128)(2,1)} %get-tuple-element.123), channel_id=1, source_target_pairs={{0,2},{2,64},{64,66},{66,0},{1,3},{3,65},{65,67},{67,1},{4,6},{6,6... | collective-permute-start | bytes 1572872 | tf_op jit(solution)/shard_map/ppermute | solution.py:31
  233.5 27.1 %collective-permute-start.31 = (bf16[512,2048]{1,0:T(8,128)(2,1)}, bf16[512,2048]{1,0:T(8,128)(2,1)}, u32[]{:S(2)}, u32[]{:S(2)}) collective-permute-start(bf16[512,2048]{1,0:T(8,128)(2,1)} %get-tuple-element.133), channel_id=1, source_target_pairs={{0,1},{1,0},{2,3},{3,2},{4,5},{5,4},{6,7},{7,6},{8,9},{9,8},{10,11... | collective-permute-start | bytes 6291464 | tf_op jit(solution)/shard_map/ppermute | solution.py:31
  234.0 13.9 %collective-permute-start.33 = (bf16[128,2048]{1,0:T(8,128)(2,1)}, bf16[128,2048]{1,0:T(8,128)(2,1)S(1)}, u32[]{:S(2)}, u32[]{:S(2)}) collective-permute-start(bf16[128,2048]{1,0:T(8,128)(2,1)} %get-tuple-element.132.refs_0_.refs_8_), channel_id=1, source_target_pairs={{0,2},{2,0},{1,3},{3,1},{4,6},{6,4},{5,7},{7,5},{8,10},{10,8},{9,1... | collective-permute-start | bytes 1572872 | tf_op jit(solution)/shard_map/ppermute | solution.py:31
  234.0 15.3 %collective-permute-start.32 = (bf16[128,2048]{1,0:T(8,128)(2,1)}, bf16[128,2048]{1,0:T(8,128)(2,1)}, u32[]{:S(2)}, u32[]{:S(2)}) collective-permute-start(bf16[128,2048]{1,0:T(8,128)(2,1)} %get-tuple-element.132.refs_0_.refs_8_), channel_id=1, source_target_pairs={{0,1},{1,0},{2,3},{3,2},{4,5},{5,4},{6,7},{7,6},{8,9},{9,8},{10,11... | collective-permute-start | bytes 1572872 | tf_op jit(solution)/shard_map/ppermute | solution.py:31
  247.8 2.4 collective-permute-start.34
  255.2 30.1 %collective-permute-start.41 = (bf16[512,512]{1,0:T(8,128)(2,1)S(1)}, bf16[512,512]{1,0:T(8,128)(2,1)S(1)}, u32[]{:S(2)}, u32[]{:S(2)}) collective-permute-start(bf16[512,512]{1,0:T(8,128)(2,1)S(1)} %get-tuple-element.138), channel_id=1, source_target_pairs={{0,16},{16,32},{32,48},{48,0},{1,17},{17,33},{33,49},{49,1},{2,18}... | collective-permute-start | bytes 1572872 | tf_op jit(solution)/shard_map/ppermute | solution.py:31
  256.8 38.0 %collective-permute-start.40 = (bf16[512,512]{1,0:T(8,128)(2,1)S(1)}, bf16[512,512]{1,0:T(8,128)(2,1)S(1)}, u32[]{:S(2)}, u32[]{:S(2)}) collective-permute-start(bf16[512,512]{1,0:T(8,128)(2,1)S(1)} %get-tuple-element.139), channel_id=1, source_target_pairs={{0,32},{16,48},{32,0},{48,16},{1,33},{17,49},{33,1},{49,17},{2,34}... | collective-permute-start | bytes 1572872 | tf_op jit(solution)/shard_map/ppermute | solution.py:31
  259.4 45.0 %collective-permute-start.42 = (bf16[512,512]{1,0:T(8,128)(2,1)S(1)}, bf16[512,512]{1,0:T(8,128)(2,1)S(1)}, u32[]{:S(2)}, u32[]{:S(2)}) collective-permute-start(bf16[512,512]{1,0:T(8,128)(2,1)S(1)} %get-tuple-element.140), channel_id=1, source_target_pairs={{0,48},{16,0},{32,16},{48,32},{1,49},{17,1},{33,17},{49,33},{2,50}... | collective-permute-start | bytes 1572872 | tf_op jit(solution)/shard_map/ppermute | solution.py:31
  263.9 33.6 %copy-start.44 = (bf16[64,1024]{1,0:T(8,128)(2,1)S(1)}, bf16[64,1024]{1,0:T(8,128)(2,1)}, u32[]{:S(2)}) copy-start(bf16[64,1024]{1,0:T(8,128)(2,1)} %copy-done.43) | copy-start | bytes 393220
  263.9 33.6 %copy-start.46 = (bf16[64,1024]{1,0:T(8,128)(2,1)S(1)}, bf16[64,1024]{1,0:T(8,128)(2,1)}, u32[]{:S(2)}) copy-start(bf16[64,1024]{1,0:T(8,128)(2,1)} %copy-done.45) | copy-start | bytes 393220
  264.0 40.4 %collective-permute-start.35 = (bf16[256,2048]{1,0:T(8,128)(2,1)S(1)}, bf16[256,2048]{1,0:T(8,128)(2,1)S(1)}, u32[]{:S(2)}, u32[]{:S(2)}) collective-permute-start(bf16[256,2048]{1,0:T(8,128)(2,1)S(1)} %get-tuple-element.136), channel_id=1, source_target_pairs={{0,2},{2,0},{1,3},{3,1},{4,6},{6,4},{5,7},{7,5},{8,10},{10,8},{9,1... | collective-permute-start | bytes 3145736 | tf_op jit(solution)/shard_map/ppermute | solution.py:31
  285.1 19.3 %collective-permute-start.39 = (bf16[512,128]{1,0:T(8,128)(2,1)S(1)}, bf16[512,128]{1,0:T(8,128)(2,1)S(1)}, u32[]{:S(2)}, u32[]{:S(2)}) collective-permute-start(bf16[512,128]{1,0:T(8,128)(2,1)S(1)} %get-tuple-element.189), channel_id=1, source_target_pairs={{0,4},{4,8},{8,12},{12,0},{1,5},{5,9},{9,13},{13,1},{2,6},{6,10},{... | collective-permute-start | bytes 393224 | tf_op jit(solution)/shard_map/ppermute | solution.py:31
  285.3 19.1 %collective-permute-start.38 = (bf16[512,128]{1,0:T(8,128)(2,1)S(1)}, bf16[512,128]{1,0:T(8,128)(2,1)S(1)}, u32[]{:S(2)}, u32[]{:S(2)}) collective-permute-start(bf16[512,128]{1,0:T(8,128)(2,1)S(1)} %get-tuple-element.190), channel_id=1, source_target_pairs={{0,8},{4,12},{8,0},{12,4},{1,9},{5,13},{9,1},{13,5},{2,10},{6,14},... | collective-permute-start | bytes 393224 | tf_op jit(solution)/shard_map/ppermute | solution.py:31
  294.8 9.6 %collective-permute-start.37 = (bf16[512,128]{1,0:T(8,128)(2,1)S(1)}, bf16[512,128]{1,0:T(8,128)(2,1)S(1)}, u32[]{:S(2)}, u32[]{:S(2)}) collective-permute-start(bf16[512,128]{1,0:T(8,128)(2,1)S(1)} %get-tuple-element.191), channel_id=1, source_target_pairs={{0,12},{4,0},{8,4},{12,8},{1,13},{5,1},{9,5},{13,9},{2,14},{6,2},{... | collective-permute-start | bytes 393224 | tf_op jit(solution)/shard_map/ppermute | solution.py:31
  306.8 8.3 %collective-permute-start.49 = (bf16[512,256]{1,0:T(8,128)(2,1)S(1)}, bf16[512,256]{1,0:T(8,128)(2,1)S(1)}, u32[]{:S(2)}, u32[]{:S(2)}) collective-permute-start(bf16[512,256]{1,0:T(8,128)(2,1)S(1)} %get-tuple-element.157), channel_id=1, source_target_pairs={{0,32},{16,48},{32,0},{48,16},{1,33},{17,49},{33,1},{49,17},{2,34}... | collective-permute-start | bytes 786440 | tf_op jit(solution)/shard_map/ppermute | solution.py:31
  308.6 16.5 %collective-permute-start.43 = (bf16[512,384]{1,0:T(8,128)(2,1)S(1)}, bf16[512,384]{1,0:T(8,128)(2,1)S(1)}, u32[]{:S(2)}, u32[]{:S(2)}) collective-permute-start(bf16[512,384]{1,0:T(8,128)(2,1)S(1)} %get-tuple-element.151), channel_id=1, source_target_pairs={{0,8},{4,12},{8,0},{12,4},{1,9},{5,13},{9,1},{13,5},{2,10},{6,14},... | collective-permute-start | bytes 1179656 | tf_op jit(solution)/shard_map/ppermute | solution.py:31
  308.7 28.4 %collective-permute-start.44 = (bf16[512,384]{1,0:T(8,128)(2,1)S(1)}, bf16[512,384]{1,0:T(8,128)(2,1)S(1)}, u32[]{:S(2)}, u32[]{:S(2)}) collective-permute-start(bf16[512,384]{1,0:T(8,128)(2,1)S(1)} %get-tuple-element.152), channel_id=1, source_target_pairs={{0,4},{4,8},{8,12},{12,0},{1,5},{5,9},{9,13},{13,1},{2,6},{6,10},{... | collective-permute-start | bytes 1179656 | tf_op jit(solution)/shard_map/ppermute | solution.py:31
  309.3 27.8 %collective-permute-start.45 = (bf16[512,384]{1,0:T(8,128)(2,1)S(1)}, bf16[512,384]{1,0:T(8,128)(2,1)S(1)}, u32[]{:S(2)}, u32[]{:S(2)}) collective-permute-start(bf16[512,384]{1,0:T(8,128)(2,1)S(1)} %get-tuple-element.153), channel_id=1, source_target_pairs={{0,12},{4,0},{8,4},{12,8},{1,13},{5,1},{9,5},{13,9},{2,14},{6,2},{... | collective-permute-start | bytes 1179656 | tf_op jit(solution)/shard_map/ppermute | solution.py:31
  311.4 13.3 %collective-permute-start.50 = (bf16[512,256]{1,0:T(8,128)(2,1)S(1)}, bf16[512,256]{1,0:T(8,128)(2,1)S(1)}, u32[]{:S(2)}, u32[]{:S(2)}) collective-permute-start(bf16[512,256]{1,0:T(8,128)(2,1)S(1)} %get-tuple-element.158), channel_id=1, source_target_pairs={{0,16},{16,32},{32,48},{48,0},{1,17},{17,33},{33,49},{49,1},{2,18}... | collective-permute-start | bytes 786440 | tf_op jit(solution)/shard_map/ppermute | solution.py:31
  315.1 9.8 %collective-permute-start.51 = (bf16[512,256]{1,0:T(8,128)(2,1)S(1)}, bf16[512,256]{1,0:T(8,128)(2,1)S(1)}, u32[]{:S(2)}, u32[]{:S(2)}) collective-permute-start(bf16[512,256]{1,0:T(8,128)(2,1)S(1)} %get-tuple-element.159), channel_id=1, source_target_pairs={{0,48},{16,0},{32,16},{48,32},{1,49},{17,1},{33,17},{49,33},{2,50}... | collective-permute-start | bytes 786440 | tf_op jit(solution)/shard_map/ppermute | solution.py:31
  324.7 30.8 %collective-permute-start.36 = (bf16[128,2048]{1,0:T(8,128)(2,1)}, bf16[128,2048]{1,0:T(8,128)(2,1)}, u32[]{:S(2)}, u32[]{:S(2)}) collective-permute-start(bf16[128,2048]{1,0:T(8,128)(2,1)} %add_convert_fusion.2), channel_id=1, source_target_pairs={{0,64},{64,0},{1,65},{65,1},{2,66},{66,2},{3,67},{67,3},{4,68},{68... | collective-permute-start | bytes 1572872 | tf_op jit(solution)/shard_map/ppermute | solution.py:31
  337.1 13.2 %collective-permute-start.56 = (bf16[256,2048]{1,0:T(8,128)(2,1)}, bf16[256,2048]{1,0:T(8,128)(2,1)S(1)}, u32[]{:S(2)}, u32[]{:S(2)}) collective-permute-start(bf16[256,2048]{1,0:T(8,128)(2,1)} %get-tuple-element.171), channel_id=1, source_target_pairs={{0,1},{1,0},{2,3},{3,2},{4,5},{5,4},{6,7},{7,6},{8,9},{9,8},{10,11... | collective-permute-start | bytes 3145736 | tf_op jit(solution)/shard_map/ppermute | solution.py:31
  338.6 7.8 %collective-permute-start.46 = (bf16[128,384]{1,0:T(8,128)(2,1)S(1)}, bf16[128,384]{1,0:T(8,128)(2,1)S(1)}, u32[]{:S(2)}, u32[]{:S(2)}) collective-permute-start(bf16[128,384]{1,0:T(8,128)(2,1)S(1)} %get-tuple-element.186), channel_id=1, source_target_pairs={{0,16},{16,32},{32,48},{48,0},{1,17},{17,33},{33,49},{49,1},{2,18}... | collective-permute-start | bytes 294920 | tf_op jit(solution)/shard_map/ppermute | solution.py:31
  338.7 7.7 %collective-permute-start.48 = (bf16[128,384]{1,0:T(8,128)(2,1)S(1)}, bf16[128,384]{1,0:T(8,128)(2,1)S(1)}, u32[]{:S(2)}, u32[]{:S(2)}) collective-permute-start(bf16[128,384]{1,0:T(8,128)(2,1)S(1)} %get-tuple-element.187), channel_id=1, source_target_pairs={{0,32},{16,48},{32,0},{48,16},{1,33},{17,49},{33,1},{49,17},{2,34}... | collective-permute-start | bytes 294920 | tf_op jit(solution)/shard_map/ppermute | solution.py:31
  340.3 8.3 %collective-permute-start.47 = (bf16[128,384]{1,0:T(8,128)(2,1)S(1)}, bf16[128,384]{1,0:T(8,128)(2,1)S(1)}, u32[]{:S(2)}, u32[]{:S(2)}) collective-permute-start(bf16[128,384]{1,0:T(8,128)(2,1)S(1)} %get-tuple-element.188), channel_id=1, source_target_pairs={{0,48},{16,0},{32,16},{48,32},{1,49},{17,1},{33,17},{49,33},{2,50}... | collective-permute-start | bytes 294920 | tf_op jit(solution)/shard_map/ppermute | solution.py:31
  346.4 9.0 %collective-permute-start.52 = (bf16[128,768]{1,0:T(8,128)(2,1)}, bf16[128,768]{1,0:T(8,128)(2,1)}, u32[]{:S(2)}, u32[]{:S(2)}) collective-permute-start(bf16[128,768]{1,0:T(8,128)(2,1)} %get-tuple-element.183), channel_id=1, source_target_pairs={{0,4},{4,8},{8,12},{12,0},{1,5},{5,9},{9,13},{13,1},{2,6},{6,10},{... | collective-permute-start | bytes 589832 | tf_op jit(solution)/shard_map/ppermute | solution.py:31
  346.4 12.3 %collective-permute-start.55 = (bf16[128,768]{1,0:T(8,128)(2,1)}, bf16[128,768]{1,0:T(8,128)(2,1)}, u32[]{:S(2)}, u32[]{:S(2)}) collective-permute-start(bf16[128,768]{1,0:T(8,128)(2,1)} %get-tuple-element.184), channel_id=1, source_target_pairs={{0,8},{4,12},{8,0},{12,4},{1,9},{5,13},{9,1},{13,5},{2,10},{6,14},... | collective-permute-start | bytes 589832 | tf_op jit(solution)/shard_map/ppermute | solution.py:31
  348.7 10.0 %collective-permute-start.54 = (bf16[128,768]{1,0:T(8,128)(2,1)}, bf16[128,768]{1,0:T(8,128)(2,1)}, u32[]{:S(2)}, u32[]{:S(2)}) collective-permute-start(bf16[128,768]{1,0:T(8,128)(2,1)} %get-tuple-element.185), channel_id=1, source_target_pairs={{0,12},{4,0},{8,4},{12,8},{1,13},{5,1},{9,5},{13,9},{2,14},{6,2},{... | collective-permute-start | bytes 589832 | tf_op jit(solution)/shard_map/ppermute | solution.py:31
  350.3 8.4 %collective-permute-start.53 = (bf16[64,2176]{1,0:T(8,128)(2,1)S(1)}, bf16[64,2176]{1,0:T(8,128)(2,1)S(1)}, u32[]{:S(2)}, u32[]{:S(2)}) collective-permute-start(bf16[64,2176]{1,0:T(8,128)(2,1)S(1)} %dynamic-slice_bitcast_fusion), channel_id=1, source_target_pairs={{0,64},{64,0},{1,65},{65,1},{2,66},{66,2},{3,67},{67,3},{4,68},{68... | collective-permute-start | bytes 835592 | tf_op jit(solution)/shard_map/ppermute | solution.py:31
  355.4 23.5 %collective-permute-start.57 = (bf16[128,2048]{1,0:T(8,128)(2,1)}, bf16[128,2048]{1,0:T(8,128)(2,1)}, u32[]{:S(2)}, u32[]{:S(2)}) collective-permute-start(bf16[128,2048]{1,0:T(8,128)(2,1)} %add_convert_fusion), channel_id=1, source_target_pairs={{0,2},{2,0},{1,3},{3,1},{4,6},{6,4},{5,7},{7,5},{8,10},{10,8},{9,1... | collective-permute-start | bytes 1572872 | tf_op jit(solution)/shard_map/ppermute | solution.py:31
  360.3 27.2 %collective-permute-start.58 = (bf16[64,1152]{1,0:T(8,128)(2,1)S(1)}, bf16[64,1152]{1,0:T(8,128)(2,1)S(1)}, u32[]{:S(2)}, u32[]{:S(2)}) collective-permute-start(bf16[64,1152]{1,0:T(8,128)(2,1)S(1)} %dynamic-slice_bitcast_fusion.5), channel_id=1, source_target_pairs={{0,64},{64,0},{1,65},{65,1},{2,66},{66,2},{3,67},{67,3},{4,68},{68... | collective-permute-start | bytes 442376 | tf_op jit(solution)/shard_map/ppermute | solution.py:31
  (53 other events, 491.6 us)
Sparse Core Ops, SparseCore 0:
  16.8 66.2 all-gather.2
  85.2 73.1 all-gather.4
  219.1 120.3 reduce-scatter.1

commit v4 on v3

--- a/solution.py
+++ b/solution.py
@@ -219,7 +219,7 @@
 
 def finish_attn_kernel(side_ref, pair_ref, other_ref, q_ref, k_ref, v_ref, o_ref):
     rows = pl.ds(pl.multiple_of(side_ref[0, 0] * HD, HD), HD)
-    both = pair_ref[rows, :].astype(F32) + other_ref[...].astype(F32)
+    both = pair_ref[rows, :].astype(F32) + other_ref[:, : pair_ref.shape[1]].astype(F32)
     width = q_ref.shape[1]
     q_ref[...] = both[:, :width]
     k_ref[...] = both[:, width : width + HD]
@@ -784,7 +784,7 @@
             pltpu.VMEM((n * span, HD), F32),
         ],
         compiler_params=params(40),
-        cost_estimate=cost(120 * 580_000_000 if first else 0, 1 << 20),
+        cost_estimate=cost(114 * 580_000_000 if first else 0, 1 << 20),
         name="attend_back",
     )(*operands)
 
@@ -941,12 +941,12 @@
     ]
     out_arrived = [shift(out_parts[n], "z", n) for n in (2, 1, 3)]
     query_raw_grad, own_grads = attend_back(
-        (0,), queries, blocks[:1], window, log_total, (grad_turned, delta, query_part), turn=[cos, sin]
+        (0,), after(queries, mlp_far), blocks[:1], window, log_total, (grad_turned, delta, query_part), turn=[cos, sin]
     )
 
     out_sum = total(out_parts[0].astype(F32), after(out_arrived, query_raw_grad)).astype(BF)
     mlp_across = swap(mlp_far, "yh")
-    a_parts = wide_parts([scaled_in], after(query_raw_grad, arriving, out_arrived, mlp_arrived), (0, cut), "x")
+    a_parts = wide_parts([scaled_in], after(query_raw_grad, arriving, out_arrived), (0, cut), "x")
     a_arrived = [shift(a_parts[n], "x", n) for n in (2, 1, 3)]
     kv_raw_grad, *b_parts = last_parts(
         scaled_in, after(query_raw_grad, a_parts), cut, own_grads, arriving, cos, sin, "z"
@@ -966,7 +966,19 @@
     b_sum = total(b_parts[0].astype(F32), b_arrived).astype(BF)
     b_sum = wide_sum_next(jnp.concatenate([b_sum, out_sum], 1), "x", hold=[mlp_there, mlp_across])
     sides = jnp.concatenate([a_sum, b_sum], 1)
-    other_sides = swap(pick(sides.reshape(2, shard, -1), place("yh", 1), 0), "yh")
+
+    attn_weights = jnp.concatenate([pair_first[:, :width_q], pair_kv[:, : 2 * width_k]], 1).astype(F32)
+    gain_parts = jnp.stack(
+        [
+            jnp.sum(attn_weights * sides[:, : width_q + 2 * width_k].astype(F32), 1),
+            jnp.sum(
+                mlp_pair[:, :both_width].astype(F32) * mlp_sum[:, :both_width].astype(F32), 1
+            ),
+        ],
+        1,
+    )
+    sent = jnp.concatenate([sides, jnp.pad(gain_parts.astype(BF), ((0, 0), (0, 126)))], 1)
+    other_sides = swap(pick(sent.reshape(2, shard, -1), place("yh", 1), 0), "yh")
     output = settle(middle, [mlp_own, mlp_arrived[:quarter], after(mlp_across, sides)], BF)
     input_grad = settle(grad_middle, in_parts[:2] + [after(in_parts[2], sides)], F32)
     query_grad, key_grad, value_grad, out_grad = call(
@@ -981,19 +993,9 @@
         [side, mlp_sum, mlp_there], scalars=1,
     )
 
-    ends = width_q - cut
-    attn_weights = jnp.concatenate([pair_first[:, :width_q], pair_kv[:, : 2 * width_k]], 1).astype(F32)
-    gain_parts = jnp.stack(
-        [
-            jnp.sum(attn_weights * sides[:, : cut + ends + 2 * width_k].astype(F32), 1),
-            jnp.sum(
-                mlp_pair[:, :both_width].astype(F32) * mlp_sum[:, :both_width].astype(F32),
-                1,
-            ),
-        ]
-    )
-    gain_parts = lax.psum(gain_parts, ("yh",) + TP)
-    own_gains = pick(gain_parts.reshape(2, 2, shard), place("yh"), 1)
+    own_gains = pick(gain_parts.reshape(2, shard, 2), place("yh"), 0)
+    own_gains = own_gains + other_sides[:, sides.shape[1] : sides.shape[1] + 2].astype(F32)
+    own_gains = lax.psum(own_gains.T, TP)
     return (
         output,
         input_grad,

time: 403 us -> 409 us (1.015)
  waiting for transfers between devices: 105 us -> 90.7 us
  local copies, waits for them, and re-layouts: 27.1 us -> 38 us
  other arithmetic: 12.1 us -> 20.8 us
    ppermute x59, waiting for transfers between devices: 103 us -> 88.4 us  [shift(): lax.ppermute(block, axis, [(i, (i + distance) % n) for i in range(n)])]
    unnamed x112 -> x152, local copies, waits for them, and re-layouts: 18.4 us -> 26.2 us
  transfers between devices with their start and end apart: 62 -> 62, of which waited for: 21 -> 23; matrix products, arithmetic and copies ran while one was open for 5% -> 8% of each run, Pallas kernels for 27% -> 26%
where the time goes in v4:
time: 409 us; the launch traced here: 401 us
  Pallas kernels  134 us (33%)
  waiting for transfers between devices  90.7 us (22%)
  starting transfers between devices  88.3 us (22%)
  local copies, waits for them, and re-layouts  38 us (9%)
  other arithmetic  20.8 us (5%)
  between operations  15.2 us (4%)
  blocking collectives  13.8 us (3%)
    ppermute x59, waiting for transfers between devices, shift(): lax.ppermute(block, axis, [(i, (i + distance) % n) for i in range(n)])  88.4 us
    ppermute x59, starting transfers between devices, shift(): lax.ppermute(block, axis, [(i, (i + distance) % n) for i in range(n)])  88.2 us
    pallas_call x2, Pallas kernels, attend_back(): pl.pallas_call(functools.partial(attend_back_kernel, distances, first, la...  27.1 us
    unnamed x152, local copies, waits for them, and re-layouts  26.2 us
    pallas_call x4, Pallas kernels, rows_out(): pl.pallas_call(functools.partial(rows_out_kernel, terms, places), grid=(d...  23.8 us
    pallas_call x1, Pallas kernels, hidden_units(): pl.pallas_call(functools.partial(hidden_kernel, width), out_shape=(jax.Sh...  20.1 us
    pallas_call x1, Pallas kernels, attend(): pl.pallas_call(attend_kernel, out_shape=(jax.ShapeDtypeStruct((span, widt...  17.5 us
    pallas_call x1, Pallas kernels, weight_grads(): pl.pallas_call(weight_grads_kernel, grid=(d // tile,), out_shape=jax.Shap...  15.4 us
  transfers between devices with their start and end apart: 62, of which 23 were waited for; matrix products, arithmetic and copies ran while one was open for 8% of the time, Pallas kernels for 26%

profile of v4, /device:TPU:1, one launch (start us, length us, event | category | flops | bytes accessed | tf_op | source)
XLA Modules:
  0.0 401.0 jit_solution(1291549215669867059)
XLA Ops:
  8.1 3.8 collective-permute-start.10
  11.9 2.9 collective-permute-done.10
  17.3 2.8 pack.1
  20.1 2.9 collective-permute-start
  23.7 1.7 dynamic-slice_bitcast_fusion.1
  26.2 2.5 collective-permute-start.5
  28.7 1.7 collective-permute-start.6
  31.1 2.7 collective-permute-done.4
  33.8 1.7 collective-permute-start.7
  35.8 4.2 %collective-permute-start.1 = (bf16[128,2048]{1,0:T(8,128)(2,1)}, bf16[128,2048]{1,0:T(8,128)(2,1)S(1)}, u32[]{:S(2)}, u32[]{:S(2)}) collective-permute-start(bf16[128,2048]{1,0:T(8,128)(2,1)} %get-tuple-element.99.refs_0_.base_ref.refs_4_), channel_id=1, source_target_pairs={{0,1},{1,0},{2,3},{3,2},{4,5},{5,4},{6,7},{7,6},{8,9},{9,8},{10,11... | collective-permute-start | bytes 1572872 | tf_op jit(solution)/shard_map/ppermute | solution.py:31
  40.0 3.1 collective-permute-start.9
  45.0 2.2 collective-permute-done.7
  47.3 7.4 %collective-permute-done.8 = bf16[4,128,256]{2,1,0:T(8,128)(2,1)S(1)} collective-permute-done((bf16[4,128,256]{2,1,0:T(8,128)(2,1)S(1)}, bf16[4,128,256]{2,1,0:T(8,128)(2,1)S(1)}, u32[]{:S(2)}, u32[]{:S(2)}) %collective-permute-start.8) | collective-permute-done | bytes 262176 | tf_op jit(solution)/shard_map/ppermute | solution.py:31
  58.5 3.0 collective-permute-start.26
  62.3 3.0 collective-permute-start.13
  67.9 1.8 bitcast_select_fusion.1
  70.4 1.8 pad_maximum_fusion.1
  72.2 7.2 %collective-permute-done.14 = bf16[128,2048]{1,0:T(8,128)(2,1)} collective-permute-done((bf16[128,2048]{1,0:T(8,128)(2,1)S(1)}, bf16[128,2048]{1,0:T(8,128)(2,1)}, u32[]{:S(2)}, u32[]{:S(2)}) %collective-permute-start.14) | collective-permute-done | bytes 524320 | tf_op jit(solution)/shard_map/ppermute | solution.py:31
  79.4 1.9 constant_dynamic-update-slice_fusion
  81.3 2.3 all-gather.3.cloned.1.call-done.w_ref.refs_1_.refs_7_.refs_2_
  83.7 3.2 collective-permute-start.15
  86.9 2.2 copy-done.2
  90.6 17.5 %attend.1 = (bf16[512,512]{1,0:T(8,128)(2,1)S(1)}, f32[8,512]{1,0:T(8,128)S(1)}) custom-call(bf16[512,512]{1,0:T(8,128)(2,1)S(1)} %queries.1.q_ref, bf16[512,128]{1,0:T(8,128)(2,1)S(1)} %get-tuple-element.101.refs_0_, bf16[512,128]{1,0:T(8,128)(2,1)} %collective-permute-done.11.refs_1_.refs_0_, bf16[512,128]{1,0:T(8,128)(2,1)} %collective-permute-done.12.refs_2_.refs_1_, ...), custom_call_target="tpu_custom_call" | custom-call | flops 5800000000 | bytes 1048576 | tf_op jit(solution)/shard_map/attend/pallas_call | solution.py:737
  109.4 1.8 rows_out.4
  111.2 2.0 collective-permute-start.16
  117.1 11.8 %collective-permute-done.17.refs_2_ = bf16[128,2048]{1,0:T(8,128)(2,1)S(1)} collective-permute-done((bf16[128,2048]{1,0:T(8,128)(2,1)S(1)}, bf16[128,2048]{1,0:T(8,128)(2,1)S(1)}, u32[]{:S(2)}, u32[]{:S(2)}) %collective-permute-start.17) | collective-permute-done | bytes 524320 | tf_op jit(solution)/shard_map/ppermute | solution.py:31
  131.1 2.3 collective-permute-start.20
  134.9 1.9 collective-permute-start.21
  136.8 7.6 %collective-permute-done.20.refs_3_ = bf16[128,2048]{1,0:T(8,128)(2,1)} collective-permute-done((bf16[128,2048]{1,0:T(8,128)(2,1)}, bf16[128,2048]{1,0:T(8,128)(2,1)}, u32[]{:S(2)}, u32[]{:S(2)}) %collective-permute-start.20) | collective-permute-done | bytes 524320 | tf_op jit(solution)/shard_map/ppermute | solution.py:31
  144.4 12.7 %collective-permute-start.24 = (bf16[128,2048]{1,0:T(8,128)(2,1)}, bf16[128,2048]{1,0:T(8,128)(2,1)}, u32[]{:S(2)}, u32[]{:S(2)}) collective-permute-start(bf16[128,2048]{1,0:T(8,128)(2,1)} %collective-permute-done.20.refs_3_), channel_id=1, source_target_pairs={{0,1},{1,0},{2,3},{3,2},{4,5},{5,4},{6,7},{7,6},{8,9},{9,8},{10,11... | collective-permute-start | bytes 1572872 | tf_op jit(solution)/shard_map/ppermute | solution.py:31
  157.1 3.2 collective-permute-done.18.refs_1_
  161.2 1.9 collective-permute-done.22.refs_5_
  163.0 20.1 %hidden_units.1 = (bf16[1024,768]{1,0:T(8,128)(2,1)}, bf16[1024,1408]{1,0:T(8,128)(2,1)}) custom-call(s32[1,1]{1,0:T(1,128)} %bitcast.18.odd_ref, bf16[128,2048]{1,0:T(8,128)(2,1)} %get-tuple-element.125.refs_0_, bf16[128,2048]{1,0:T(8,128)(2,1)} %collective-permute-done.18.refs_1_, bf16[128,2048]{1,0:T(8,128)(2,1)} %collective-permute-done.19.refs_2_, ...), custom_call_target="tpu_custom_call" | custom-call | flops 8053063680 | bytes 7864320 | tf_op jit(solution)/shard_map/hidden_units/pallas_call | solution.py:610
  183.1 7.4 %rows_out.5 = bf16[512,2048]{1,0:T(8,128)(2,1)} custom-call(bf16[1024,1408]{1,0:T(8,128)(2,1)} %get-tuple-element.121.refs_0_.refs_10_, bf16[2048,2176]{1,0:T(8,128)(2,1)} %all-gather.5.cloned.1.call-done.refs_10_.refs_1_), custom_call_target="tpu_custom_call" | custom-call | flops 2952790016 | bytes 6291456 | tf_op jit(solution)/shard_map/rows_out/pallas_call | solution.py:667
  191.0 7.4 %rows_out.6.one_ref = bf16[512,2048]{1,0:T(8,128)(2,1)} custom-call(bf16[1024,1408]{1,0:T(8,128)(2,1)} %get-tuple-element.121.refs_0_.refs_10_, bf16[2048,2176]{1,0:T(8,128)(2,1)} %all-gather.5.cloned.1.call-done.refs_10_.refs_1_), custom_call_target="tpu_custom_call" | custom-call | flops 2952790016 | bytes 6291456 | tf_op jit(solution)/shard_map/rows_out/pallas_call | solution.py:667
  204.1 15.4 %weight_grads.1 = bf16[2048,2176]{1,0:T(8,128)(2,1)} custom-call(s32[1,1]{1,0:T(1,128)} %bitcast.18.odd_ref, bf16[128,2048]{1,0:T(8,128)(2,1)} %get-tuple-element.125.refs_0_, bf16[128,2048]{1,0:T(8,128)(2,1)} %collective-permute-done.18.refs_1_, bf16[128,2048]{1,0:T(8,128)(2,1)} %collective-permute-done.19.refs_2_, ...), custom_call_target="tpu_custom_call" | custom-call | flops 9126805504 | bytes 17301504 | tf_op jit(solution)/shard_map/weight_grads/pallas_call | solution.py:797
  219.6 7.2 %rows_out.7 = (bf16[512,2048]{1,0:T(8,128)(2,1)}, bf16[512,2048]{1,0:T(8,128)(2,1)}) custom-call(bf16[1024,768]{1,0:T(8,128)(2,1)} %get-tuple-element.126.refs_11_.refs_0_, bf16[2048,2176]{1,0:T(8,128)(2,1)} %all-gather.5.cloned.1.call-done.refs_10_.refs_1_), custom_call_target="tpu_custom_call" | custom-call | flops 3221225472 | bytes 6291456 | tf_op jit(solution)/shard_map/rows_out/pallas_call | solution.py:667
  226.8 3.3 collective-permute-done.29.refs_2_
  230.1 2.8 middle_grad.1
  234.5 13.8 %collective-permute-done.33.refs_2_.refs_10_ = bf16[128,2048]{1,0:T(8,128)(2,1)S(1)} collective-permute-done((bf16[128,2048]{1,0:T(8,128)(2,1)}, bf16[128,2048]{1,0:T(8,128)(2,1)S(1)}, u32[]{:S(2)}, u32[]{:S(2)}) %collective-permute-start.33) | collective-permute-done | bytes 524320 | tf_op jit(solution)/shard_map/ppermute | solution.py:31
  251.7 2.7 wide_parts.2
  256.1 2.6 collective-permute-start.40
  260.0 2.2 pair_pieces.1
  264.4 20.4 %attend_back.2 = (f32[512,512]{1,0:T(8,128)S(1)}, bf16[1536,128]{1,0:T(8,128)(2,1)S(1)}, bf16[512,512]{1,0:T(8,128)(2,1)S(1)}, f32[8,512]{1,0:T(8,128)S(1)}) custom-call(bf16[512,512]{1,0:T(8,128)(2,1)S(1)} %copy-done.19, bf16[512,128]{1,0:T(8,128)(2,1)} %collective-permute-done.11.refs_1_.refs_0_, bf16[512,128]{1,0:T(8,128)(2,1)} %collective-permute-done.12.refs_2_.refs_1_, ...), custom_call_target="tpu_custom_call" | custom-call | flops 132239998976 | bytes 1048576 | tf_op jit(solution)/shard_map/attend_back/pallas_call | solution.py:774
  291.0 6.7 %attend_back.3 = (bf16[512,512]{1,0:T(8,128)(2,1)S(1)}, f32[512,128]{1,0:T(8,128)S(1)}) custom-call(bf16[512,512]{1,0:T(8,128)(2,1)S(1)} %copy-done.19, bf16[512,128]{1,0:T(8,128)(2,1)S(1)} %get-tuple-element.101.refs_0_, s32[1,1]{1,0:T(1,128)} %bitcast.16.refs_4_.refs_3_.refs_1_, s32[1,512]{1,0:T(1,128)S(1)} %bitcast.78, ...), custom_call_target="tpu_custom_call" | custom-call | bytes 1048576 | tf_op jit(solution)/shard_map/attend_back/pallas_call | solution.py:774
  297.8 2.1 wide_parts.3
  300.6 1.7 copy-done.9
  302.4 1.7 last_parts.1
  307.1 2.3 collective-permute-start.43
  310.2 1.9 collective-permute-start.45
  315.7 2.2 copy-done.5
  320.0 4.0 rows_grad.1
  324.0 2.1 collective-permute-start.51
  326.6 5.5 %collective-permute-done.51 = bf16[512,256]{1,0:T(8,128)(2,1)S(1)} collective-permute-done((bf16[512,256]{1,0:T(8,128)(2,1)S(1)}, bf16[512,256]{1,0:T(8,128)(2,1)S(1)}, u32[]{:S(2)}, u32[]{:S(2)}) %collective-permute-start.51) | collective-permute-done | bytes 262176 | tf_op jit(solution)/shard_map/ppermute | solution.py:31
  332.1 4.4 %collective-permute-done.44 = bf16[512,384]{1,0:T(8,128)(2,1)S(1)} collective-permute-done((bf16[512,384]{1,0:T(8,128)(2,1)}, bf16[512,384]{1,0:T(8,128)(2,1)S(1)}, u32[]{:S(2)}, u32[]{:S(2)}) %collective-permute-start.44) | collective-permute-done | bytes 393248 | tf_op jit(solution)/shard_map/ppermute | solution.py:31
  339.8 2.8 collective-permute-start.48
  345.7 2.0 collective-permute-done.48
  347.7 1.8 collective-permute-start.55
  356.0 5.9 %collective-permute-done.53.other_ref = bf16[64,2176]{1,0:T(8,128)(2,1)S(1)} collective-permute-done((bf16[64,2176]{1,0:T(8,128)(2,1)}, bf16[64,2176]{1,0:T(8,128)(2,1)S(1)}, u32[]{:S(2)}, u32[]{:S(2)}) %collective-permute-start.53) | collective-permute-done | bytes 278560 | tf_op jit(solution)/shard_map/ppermute | solution.py:31
  361.8 2.1 fusion.3
  365.9 1.7 fusion.5
  371.4 2.2 settle.2
  373.7 2.5 settle.3
  377.9 13.8 %psum.7 = f32[2,64]{0,1:T(8,128)S(1)} all-reduce(f32[2,64]{0,1:T(8,128)S(1)} %add_bitcast_fusion), channel_id=1, replica_groups=mesh['yh'=2,'z'=4,'x'=4,'yl'=2,'core'=2] {'yl','core'}, use_global_device_ids=true, to_apply=%region_3.4 | all-reduce | flops 128 | bytes 1024 | tf_op jit(solution)/shard_map/psum | solution.py:998
  (300 shorter events, 82.3 us)
Async XLA Ops:
  7.2 76.4 %all-gather.3.cloned.1.call-start = ((), (), s32[]{:S(2)}) async-start(), calls=%async_computation.1 | async-start | bytes 4456448 | tf_op jit(solution)/shard_map/all_gather | solution.py:849
  8.1 6.8 %collective-permute-start.10 = (bf16[64,1024]{1,0:T(8,128)(2,1)S(1)}, bf16[64,1024]{1,0:T(8,128)(2,1)S(1)}, u32[]{:S(2)}, u32[]{:S(2)}) collective-permute-start(bf16[64,1024]{1,0:T(8,128)(2,1)S(1)} %pad_maximum_fusion.4), channel_id=1, source_target_pairs={{0,64},{64,0},{1,65},{65,1},{2,66},{66,2},{3,67},{67,3},{4,68},{68... | collective-permute-start | bytes 393224 | tf_op jit(solution)/shard_map/ppermute | solution.py:31
  17.3 145.7 %all-gather.5.cloned.1.call-start = ((), (), s32[]{:S(2)}) async-start(), calls=%async_computation.2 | async-start | bytes 9469952 | tf_op jit(solution)/shard_map/all_gather | solution.py:879
  20.1 5.2 %collective-permute-start = (bf16[64,256]{1,0:T(8,128)(2,1)}, bf16[64,256]{1,0:T(8,128)(2,1)S(1)}, u32[]{:S(2)}, u32[]{:S(2)}) collective-permute-start(bf16[64,256]{1,0:T(8,128)(2,1)} %get-tuple-element.98), channel_id=1, source_target_pairs={{0,64},{64,0},{1,65},{65,1},{2,66},{66,2},{3,67},{67,3},{4,68},{68... | collective-permute-start | bytes 98312 | tf_op jit(solution)/shard_map/ppermute | solution.py:31
  26.1 28.6 %copy-start.11 = (bf16[128,2048]{1,0:T(8,128)(2,1)S(1)}, bf16[128,2048]{1,0:T(8,128)(2,1)}, u32[]{:S(2)}) copy-start(bf16[128,2048]{1,0:T(8,128)(2,1)} %get-tuple-element.99.refs_0_.base_ref.refs_4_) | copy-start | bytes 1572868
  26.2 7.6 %collective-permute-start.5 = (bf16[128,256]{1,0:T(8,128)(2,1)S(1)}, bf16[128,256]{1,0:T(8,128)(2,1)S(1)}, u32[]{:S(2)}, u32[]{:S(2)}) collective-permute-start(bf16[128,256]{1,0:T(8,128)(2,1)S(1)} %pad_maximum_fusion.5), channel_id=1, source_target_pairs={{0,12},{4,0},{8,4},{12,8},{1,13},{5,1},{9,5},{13,9},{2,14},{6,2},{... | collective-permute-start | bytes 196616 | tf_op jit(solution)/shard_map/ppermute | solution.py:31
  28.7 5.0 %collective-permute-start.4 = (bf16[128,256]{1,0:T(8,128)(2,1)S(1)}, bf16[128,256]{1,0:T(8,128)(2,1)S(1)}, u32[]{:S(2)}, u32[]{:S(2)}) collective-permute-start(bf16[128,256]{1,0:T(8,128)(2,1)S(1)} %pad_maximum_fusion.5), channel_id=1, source_target_pairs={{0,4},{4,8},{8,12},{12,0},{1,5},{5,9},{9,13},{13,1},{2,6},{6,10},{... | collective-permute-start | bytes 196616 | tf_op jit(solution)/shard_map/ppermute | solution.py:31
  28.7 5.1 %collective-permute-start.6 = (bf16[128,256]{1,0:T(8,128)(2,1)S(1)}, bf16[128,256]{1,0:T(8,128)(2,1)S(1)}, u32[]{:S(2)}, u32[]{:S(2)}) collective-permute-start(bf16[128,256]{1,0:T(8,128)(2,1)S(1)} %pad_maximum_fusion.5), channel_id=1, source_target_pairs={{0,8},{4,12},{8,0},{12,4},{1,9},{5,13},{9,1},{13,5},{2,10},{6,14},... | collective-permute-start | bytes 196616 | tf_op jit(solution)/shard_map/ppermute | solution.py:31
  30.5 13.8 %collective-permute-start.2 = (bf16[128,2048]{1,0:T(8,128)(2,1)}, bf16[128,2048]{1,0:T(8,128)(2,1)S(1)}, u32[]{:S(2)}, u32[]{:S(2)}) collective-permute-start(bf16[128,2048]{1,0:T(8,128)(2,1)} %get-tuple-element.99.refs_0_.base_ref.refs_4_), channel_id=1, source_target_pairs={{0,2},{2,0},{1,3},{3,1},{4,6},{6,4},{5,7},{7,5},{8,10},{10,8},{9,1... | collective-permute-start | bytes 1572872 | tf_op jit(solution)/shard_map/ppermute | solution.py:31
  33.8 13.4 %collective-permute-start.7 = (bf16[4,128,256]{2,1,0:T(8,128)(2,1)S(1)}, bf16[4,128,256]{2,1,0:T(8,128)(2,1)S(1)}, u32[]{:S(2)}, u32[]{:S(2)}) collective-permute-start(bf16[4,128,256]{2,1,0:T(8,128)(2,1)S(1)} %bitcast_dynamic-update-slice_fusion.4), channel_id=1, source_target_pairs={{0,16},{16,32},{32,48},{48,0},{1,17},{17,33},{33,49},{49,1},{2,18}... | collective-permute-start | bytes 786440 | tf_op jit(solution)/shard_map/ppermute | solution.py:31
  35.8 18.9 %collective-permute-start.1 = (bf16[128,2048]{1,0:T(8,128)(2,1)}, bf16[128,2048]{1,0:T(8,128)(2,1)S(1)}, u32[]{:S(2)}, u32[]{:S(2)}) collective-permute-start(bf16[128,2048]{1,0:T(8,128)(2,1)} %get-tuple-element.99.refs_0_.base_ref.refs_4_), channel_id=1, source_target_pairs={{0,1},{1,0},{2,3},{3,2},{4,5},{5,4},{6,7},{7,6},{8,9},{9,8},{10,11... | collective-permute-start | bytes 1572872 | tf_op jit(solution)/shard_map/ppermute | solution.py:31
  40.0 14.6 %collective-permute-start.9 = (bf16[4,128,256]{2,1,0:T(8,128)(2,1)S(1)}, bf16[4,128,256]{2,1,0:T(8,128)(2,1)S(1)}, u32[]{:S(2)}, u32[]{:S(2)}) collective-permute-start(bf16[4,128,256]{2,1,0:T(8,128)(2,1)S(1)} %bitcast_dynamic-update-slice_fusion.4), channel_id=1, source_target_pairs={{0,32},{16,48},{32,0},{48,16},{1,33},{17,49},{33,1},{49,17},{2,34}... | collective-permute-start | bytes 786440 | tf_op jit(solution)/shard_map/ppermute | solution.py:31
  43.1 11.5 %collective-permute-start.8 = (bf16[4,128,256]{2,1,0:T(8,128)(2,1)S(1)}, bf16[4,128,256]{2,1,0:T(8,128)(2,1)S(1)}, u32[]{:S(2)}, u32[]{:S(2)}) collective-permute-start(bf16[4,128,256]{2,1,0:T(8,128)(2,1)S(1)} %bitcast_dynamic-update-slice_fusion.4), channel_id=1, source_target_pairs={{0,48},{16,0},{32,16},{48,32},{1,49},{17,1},{33,17},{49,33},{2,50}... | collective-permute-start | bytes 786440 | tf_op jit(solution)/shard_map/ppermute | solution.py:31
  44.2 10.5 %collective-permute-start.3 = (bf16[128,2048]{1,0:T(8,128)(2,1)S(1)}, bf16[128,2048]{1,0:T(8,128)(2,1)S(1)}, u32[]{:S(2)}, u32[]{:S(2)}) collective-permute-start(bf16[128,2048]{1,0:T(8,128)(2,1)S(1)} %collective-permute-done.2.refs_2_.refs_6_), channel_id=1, source_target_pairs={{0,1},{1,0},{2,3},{3,2},{4,5},{5,4},{6,7},{7,6},{8,9},{9,8},{10,11... | collective-permute-start | bytes 1572872 | tf_op jit(solution)/shard_map/ppermute | solution.py:31
  58.5 239.2 %copy-start.8 = (bf16[512,2048]{1,0:T(8,128)(2,1)}, bf16[512,2048]{1,0:T(8,128)(2,1)S(1)}, u32[]{:S(2)}) copy-start(bf16[512,2048]{1,0:T(8,128)(2,1)S(1)} %get-tuple-element.100.x_ref.refs_0_.left_ref) | copy-start | bytes 6291460
  58.5 9.3 %collective-permute-start.26 = (bf16[64,2176]{1,0:T(8,128)(2,1)}, bf16[64,2176]{1,0:T(8,128)(2,1)}, u32[]{:S(2)}, u32[]{:S(2)}) collective-permute-start(bf16[64,2176]{1,0:T(8,128)(2,1)} %dynamic-slice_bitcast_fusion.1), channel_id=1, source_target_pairs={{0,64},{64,0},{1,65},{65,1},{2,66},{66,2},{3,67},{67,3},{4,68},{68... | collective-permute-start | bytes 835592 | tf_op jit(solution)/shard_map/ppermute | solution.py:31
  62.3 19.0 %collective-permute-start.13 = (bf16[512,128]{1,0:T(8,128)(2,1)S(1)}, bf16[512,128]{1,0:T(8,128)(2,1)}, u32[]{:S(2)}, u32[]{:S(2)}) collective-permute-start(bf16[512,128]{1,0:T(8,128)(2,1)S(1)} %get-tuple-element.101.refs_0_), channel_id=1, source_target_pairs={{0,12},{4,0},{8,4},{12,8},{1,13},{5,1},{9,5},{13,9},{2,14},{6,2},{... | collective-permute-start | bytes 393224 | tf_op jit(solution)/shard_map/ppermute | solution.py:31
  65.4 16.0 %collective-permute-start.12 = (bf16[512,128]{1,0:T(8,128)(2,1)S(1)}, bf16[512,128]{1,0:T(8,128)(2,1)}, u32[]{:S(2)}, u32[]{:S(2)}) collective-permute-start(bf16[512,128]{1,0:T(8,128)(2,1)S(1)} %get-tuple-element.101.refs_0_), channel_id=1, source_target_pairs={{0,8},{4,12},{8,0},{12,4},{1,9},{5,13},{9,1},{13,5},{2,10},{6,14},... | collective-permute-start | bytes 393224 | tf_op jit(solution)/shard_map/ppermute | solution.py:31
  65.4 16.0 %collective-permute-start.11 = (bf16[512,128]{1,0:T(8,128)(2,1)S(1)}, bf16[512,128]{1,0:T(8,128)(2,1)}, u32[]{:S(2)}, u32[]{:S(2)}) collective-permute-start(bf16[512,128]{1,0:T(8,128)(2,1)S(1)} %get-tuple-element.101.refs_0_), channel_id=1, source_target_pairs={{0,4},{4,8},{8,12},{12,0},{1,5},{5,9},{9,13},{13,1},{2,6},{6,10},{... | collective-permute-start | bytes 393224 | tf_op jit(solution)/shard_map/ppermute | solution.py:31
  66.0 13.5 %collective-permute-start.14 = (bf16[128,2048]{1,0:T(8,128)(2,1)S(1)}, bf16[128,2048]{1,0:T(8,128)(2,1)}, u32[]{:S(2)}, u32[]{:S(2)}) collective-permute-start(bf16[128,2048]{1,0:T(8,128)(2,1)S(1)} %copy-done.17), channel_id=1, source_target_pairs={{0,2},{2,0},{1,3},{3,1},{4,6},{6,4},{5,7},{7,5},{8,10},{10,8},{9,1... | collective-permute-start | bytes 1572872 | tf_op jit(solution)/shard_map/ppermute | solution.py:31
  83.6 268.0 %reduce-scatter.2.cloned.1.call-start = ((), (), s32[]{:S(2)}) async-start(), calls=%async_computation.3 | async-start | bytes 9469952 | tf_op jit(solution)/shard_map/reduce_scatter | solution.py:921
  83.7 25.7 %collective-permute-start.15 = (bf16[256,2048]{1,0:T(8,128)(2,1)}, bf16[256,2048]{1,0:T(8,128)(2,1)S(1)}, u32[]{:S(2)}, u32[]{:S(2)}) collective-permute-start(bf16[256,2048]{1,0:T(8,128)(2,1)} %constant_dynamic-update-slice_fusion), channel_id=1, source_target_pairs={{0,64},{64,0},{1,65},{65,1},{2,66},{66,2},{3,67},{67,3},{4,68},{68... | collective-permute-start | bytes 3145736 | tf_op jit(solution)/shard_map/ppermute | solution.py:31
  111.2 4.3 %collective-permute-start.16 = (bf16[256,2048]{1,0:T(8,128)(2,1)S(1)}, bf16[256,2048]{1,0:T(8,128)(2,1)S(1)}, u32[]{:S(2)}, u32[]{:S(2)}) collective-permute-start(bf16[256,2048]{1,0:T(8,128)(2,1)S(1)} %get-tuple-element.110), channel_id=1, source_target_pairs={{0,1},{1,0},{2,3},{3,2},{4,5},{5,4},{6,7},{7,6},{8,9},{9,8},{10,11... | collective-permute-start | bytes 3145736 | tf_op jit(solution)/shard_map/ppermute | solution.py:31
  115.3 45.8 %collective-permute-start.25 = (bf16[512,2048]{1,0:T(8,128)(2,1)}, bf16[512,2048]{1,0:T(8,128)(2,1)}, u32[]{:S(2)}, u32[]{:S(2)}) collective-permute-start(bf16[512,2048]{1,0:T(8,128)(2,1)} %constant_dynamic-update-slice_fusion.2.refs_8_), channel_id=1, source_target_pairs={{0,1},{1,0},{2,3},{3,2},{4,5},{5,4},{6,7},{7,6},{8,9},{9,8},{10,11... | collective-permute-start | bytes 6291464 | tf_op jit(solution)/shard_map/ppermute | solution.py:31
  115.6 13.3 %collective-permute-start.17 = (bf16[128,2048]{1,0:T(8,128)(2,1)S(1)}, bf16[128,2048]{1,0:T(8,128)(2,1)S(1)}, u32[]{:S(2)}, u32[]{:S(2)}) collective-permute-start(bf16[128,2048]{1,0:T(8,128)(2,1)S(1)} %add_convert_fusion.3), channel_id=1, source_target_pairs={{0,2},{2,0},{1,3},{3,1},{4,6},{6,4},{5,7},{7,5},{8,10},{10,8},{9,1... | collective-permute-start | bytes 1572872 | tf_op jit(solution)/shard_map/ppermute | solution.py:31
  131.1 13.3 %collective-permute-start.20 = (bf16[128,2048]{1,0:T(8,128)(2,1)}, bf16[128,2048]{1,0:T(8,128)(2,1)}, u32[]{:S(2)}, u32[]{:S(2)}) collective-permute-start(bf16[128,2048]{1,0:T(8,128)(2,1)} %get-tuple-element.125.refs_0_), channel_id=1, source_target_pairs={{0,66},{2,0},{64,2},{66,64},{1,67},{3,1},{65,3},{67,65},{4,70},{6,... | collective-permute-start | bytes 1572872 | tf_op jit(solution)/shard_map/ppermute | solution.py:31
  133.4 23.7 %collective-permute-start.19 = (bf16[128,2048]{1,0:T(8,128)(2,1)}, bf16[128,2048]{1,0:T(8,128)(2,1)}, u32[]{:S(2)}, u32[]{:S(2)}) collective-permute-start(bf16[128,2048]{1,0:T(8,128)(2,1)} %get-tuple-element.125.refs_0_), channel_id=1, source_target_pairs={{0,64},{2,66},{64,0},{66,2},{1,65},{3,67},{65,1},{67,3},{4,68},{6,... | collective-permute-start | bytes 1572872 | tf_op jit(solution)/shard_map/ppermute | solution.py:31
  134.2 26.0 %collective-permute-start.18 = (bf16[128,2048]{1,0:T(8,128)(2,1)}, bf16[128,2048]{1,0:T(8,128)(2,1)}, u32[]{:S(2)}, u32[]{:S(2)}) collective-permute-start(bf16[128,2048]{1,0:T(8,128)(2,1)} %get-tuple-element.125.refs_0_), channel_id=1, source_target_pairs={{0,2},{2,64},{64,66},{66,0},{1,3},{3,65},{65,67},{67,1},{4,6},{6,6... | collective-permute-start | bytes 1572872 | tf_op jit(solution)/shard_map/ppermute | solution.py:31
  134.9 26.3 %collective-permute-start.21 = (bf16[128,2048]{1,0:T(8,128)(2,1)}, bf16[128,2048]{1,0:T(8,128)(2,1)}, u32[]{:S(2)}, u32[]{:S(2)}) collective-permute-start(bf16[128,2048]{1,0:T(8,128)(2,1)} %get-tuple-element.125.refs_0_), channel_id=1, source_target_pairs={{0,1},{1,0},{2,3},{3,2},{4,5},{5,4},{6,7},{7,6},{8,9},{9,8},{10,11... | collective-permute-start | bytes 1572872 | tf_op jit(solution)/shard_map/ppermute | solution.py:31
  144.4 16.8 %collective-permute-start.24 = (bf16[128,2048]{1,0:T(8,128)(2,1)}, bf16[128,2048]{1,0:T(8,128)(2,1)}, u32[]{:S(2)}, u32[]{:S(2)}) collective-permute-start(bf16[128,2048]{1,0:T(8,128)(2,1)} %collective-permute-done.20.refs_3_), channel_id=1, source_target_pairs={{0,1},{1,0},{2,3},{3,2},{4,5},{5,4},{6,7},{7,6},{8,9},{9,8},{10,11... | collective-permute-start | bytes 1572872 | tf_op jit(solution)/shard_map/ppermute | solution.py:31
  157.1 4.1 %collective-permute-start.23 = (bf16[128,2048]{1,0:T(8,128)(2,1)}, bf16[128,2048]{1,0:T(8,128)(2,1)}, u32[]{:S(2)}, u32[]{:S(2)}) collective-permute-start(bf16[128,2048]{1,0:T(8,128)(2,1)} %collective-permute-done.19.refs_2_), channel_id=1, source_target_pairs={{0,1},{1,0},{2,3},{3,2},{4,5},{5,4},{6,7},{7,6},{8,9},{9,8},{10,11... | collective-permute-start | bytes 1572872 | tf_op jit(solution)/shard_map/ppermute | solution.py:31
  160.3 2.8 collective-permute-start.22
  190.5 7.9 %collective-permute-start.27 = (bf16[512,2048]{1,0:T(8,128)(2,1)}, bf16[512,2048]{1,0:T(8,128)(2,1)S(1)}, u32[]{:S(2)}, u32[]{:S(2)}) collective-permute-start(bf16[512,2048]{1,0:T(8,128)(2,1)} %rows_out.5), channel_id=1, source_target_pairs={{0,1},{1,0},{2,3},{3,2},{4,5},{5,4},{6,7},{7,6},{8,9},{9,8},{10,11... | collective-permute-start | bytes 6291464 | tf_op jit(solution)/shard_map/ppermute | solution.py:31
  202.4 24.4 %collective-permute-start.28 = (bf16[128,2048]{1,0:T(8,128)(2,1)}, bf16[128,2048]{1,0:T(8,128)(2,1)}, u32[]{:S(2)}, u32[]{:S(2)}) collective-permute-start(bf16[128,2048]{1,0:T(8,128)(2,1)} %get-tuple-element.122), channel_id=1, source_target_pairs={{0,66},{2,0},{64,2},{66,64},{1,67},{3,1},{65,3},{67,65},{4,70},{6,... | collective-permute-start | bytes 1572872 | tf_op jit(solution)/shard_map/ppermute | solution.py:31
  203.2 23.6 %collective-permute-start.30 = (bf16[128,2048]{1,0:T(8,128)(2,1)}, bf16[128,2048]{1,0:T(8,128)(2,1)}, u32[]{:S(2)}, u32[]{:S(2)}) collective-permute-start(bf16[128,2048]{1,0:T(8,128)(2,1)} %get-tuple-element.123), channel_id=1, source_target_pairs={{0,64},{2,66},{64,0},{66,2},{1,65},{3,67},{65,1},{67,3},{4,68},{6,... | collective-permute-start | bytes 1572872 | tf_op jit(solution)/shard_map/ppermute | solution.py:31
  203.6 26.5 %collective-permute-start.29 = (bf16[128,2048]{1,0:T(8,128)(2,1)}, bf16[128,2048]{1,0:T(8,128)(2,1)}, u32[]{:S(2)}, u32[]{:S(2)}) collective-permute-start(bf16[128,2048]{1,0:T(8,128)(2,1)} %get-tuple-element.124), channel_id=1, source_target_pairs={{0,2},{2,64},{64,66},{66,0},{1,3},{3,65},{65,67},{67,1},{4,6},{6,6... | collective-permute-start | bytes 1572872 | tf_op jit(solution)/shard_map/ppermute | solution.py:31
  233.9 26.0 %collective-permute-start.31 = (bf16[512,2048]{1,0:T(8,128)(2,1)}, bf16[512,2048]{1,0:T(8,128)(2,1)}, u32[]{:S(2)}, u32[]{:S(2)}) collective-permute-start(bf16[512,2048]{1,0:T(8,128)(2,1)} %get-tuple-element.134), channel_id=1, source_target_pairs={{0,1},{1,0},{2,3},{3,2},{4,5},{5,4},{6,7},{7,6},{8,9},{9,8},{10,11... | collective-permute-start | bytes 6291464 | tf_op jit(solution)/shard_map/ppermute | solution.py:31
  234.4 13.9 %collective-permute-start.33 = (bf16[128,2048]{1,0:T(8,128)(2,1)}, bf16[128,2048]{1,0:T(8,128)(2,1)S(1)}, u32[]{:S(2)}, u32[]{:S(2)}) collective-permute-start(bf16[128,2048]{1,0:T(8,128)(2,1)} %get-tuple-element.133.refs_0_.refs_8_), channel_id=1, source_target_pairs={{0,2},{2,0},{1,3},{3,1},{4,6},{6,4},{5,7},{7,5},{8,10},{10,8},{9,1... | collective-permute-start | bytes 1572872 | tf_op jit(solution)/shard_map/ppermute | solution.py:31
  234.4 14.6 %collective-permute-start.32 = (bf16[128,2048]{1,0:T(8,128)(2,1)}, bf16[128,2048]{1,0:T(8,128)(2,1)}, u32[]{:S(2)}, u32[]{:S(2)}) collective-permute-start(bf16[128,2048]{1,0:T(8,128)(2,1)} %get-tuple-element.133.refs_0_.refs_8_), channel_id=1, source_target_pairs={{0,1},{1,0},{2,3},{3,2},{4,5},{5,4},{6,7},{7,6},{8,9},{9,8},{10,11... | collective-permute-start | bytes 1572872 | tf_op jit(solution)/shard_map/ppermute | solution.py:31
  248.3 2.4 collective-permute-start.34
  254.5 33.9 %collective-permute-start.41 = (bf16[512,512]{1,0:T(8,128)(2,1)S(1)}, bf16[512,512]{1,0:T(8,128)(2,1)S(1)}, u32[]{:S(2)}, u32[]{:S(2)}) collective-permute-start(bf16[512,512]{1,0:T(8,128)(2,1)S(1)} %get-tuple-element.139), channel_id=1, source_target_pairs={{0,16},{16,32},{32,48},{48,0},{1,17},{17,33},{33,49},{49,1},{2,18}... | collective-permute-start | bytes 1572872 | tf_op jit(solution)/shard_map/ppermute | solution.py:31
  256.1 41.6 %collective-permute-start.40 = (bf16[512,512]{1,0:T(8,128)(2,1)S(1)}, bf16[512,512]{1,0:T(8,128)(2,1)S(1)}, u32[]{:S(2)}, u32[]{:S(2)}) collective-permute-start(bf16[512,512]{1,0:T(8,128)(2,1)S(1)} %get-tuple-element.140), channel_id=1, source_target_pairs={{0,32},{16,48},{32,0},{48,16},{1,33},{17,49},{33,1},{49,17},{2,34}... | collective-permute-start | bytes 1572872 | tf_op jit(solution)/shard_map/ppermute | solution.py:31
  258.7 39.0 %collective-permute-start.42 = (bf16[512,512]{1,0:T(8,128)(2,1)S(1)}, bf16[512,512]{1,0:T(8,128)(2,1)S(1)}, u32[]{:S(2)}, u32[]{:S(2)}) collective-permute-start(bf16[512,512]{1,0:T(8,128)(2,1)S(1)} %get-tuple-element.141), channel_id=1, source_target_pairs={{0,48},{16,0},{32,16},{48,32},{1,49},{17,1},{33,17},{49,33},{2,50}... | collective-permute-start | bytes 1572872 | tf_op jit(solution)/shard_map/ppermute | solution.py:31
  263.2 23.9 %collective-permute-start.35 = (bf16[256,2048]{1,0:T(8,128)(2,1)S(1)}, bf16[256,2048]{1,0:T(8,128)(2,1)S(1)}, u32[]{:S(2)}, u32[]{:S(2)}) collective-permute-start(bf16[256,2048]{1,0:T(8,128)(2,1)S(1)} %get-tuple-element.137), channel_id=1, source_target_pairs={{0,2},{2,0},{1,3},{3,1},{4,6},{6,4},{5,7},{7,5},{8,10},{10,8},{9,1... | collective-permute-start | bytes 3145736 | tf_op jit(solution)/shard_map/ppermute | solution.py:31
  284.9 12.8 %collective-permute-start.39 = (bf16[512,128]{1,0:T(8,128)(2,1)S(1)}, bf16[512,128]{1,0:T(8,128)(2,1)S(1)}, u32[]{:S(2)}, u32[]{:S(2)}) collective-permute-start(bf16[512,128]{1,0:T(8,128)(2,1)S(1)} %get-tuple-element.193), channel_id=1, source_target_pairs={{0,4},{4,8},{8,12},{12,0},{1,5},{5,9},{9,13},{13,1},{2,6},{6,10},{... | collective-permute-start | bytes 393224 | tf_op jit(solution)/shard_map/ppermute | solution.py:31
  287.1 10.7 %collective-permute-start.38 = (bf16[512,128]{1,0:T(8,128)(2,1)S(1)}, bf16[512,128]{1,0:T(8,128)(2,1)S(1)}, u32[]{:S(2)}, u32[]{:S(2)}) collective-permute-start(bf16[512,128]{1,0:T(8,128)(2,1)S(1)} %get-tuple-element.194), channel_id=1, source_target_pairs={{0,8},{4,12},{8,0},{12,4},{1,9},{5,13},{9,1},{13,5},{2,10},{6,14},... | collective-permute-start | bytes 393224 | tf_op jit(solution)/shard_map/ppermute | solution.py:31
  288.4 9.4 %collective-permute-start.37 = (bf16[512,128]{1,0:T(8,128)(2,1)S(1)}, bf16[512,128]{1,0:T(8,128)(2,1)S(1)}, u32[]{:S(2)}, u32[]{:S(2)}) collective-permute-start(bf16[512,128]{1,0:T(8,128)(2,1)S(1)} %get-tuple-element.195), channel_id=1, source_target_pairs={{0,12},{4,0},{8,4},{12,8},{1,13},{5,1},{9,5},{13,9},{2,14},{6,2},{... | collective-permute-start | bytes 393224 | tf_op jit(solution)/shard_map/ppermute | solution.py:31
  306.2 17.8 %collective-permute-start.49 = (bf16[512,256]{1,0:T(8,128)(2,1)}, bf16[512,256]{1,0:T(8,128)(2,1)}, u32[]{:S(2)}, u32[]{:S(2)}) collective-permute-start(bf16[512,256]{1,0:T(8,128)(2,1)} %get-tuple-element.159), channel_id=1, source_target_pairs={{0,32},{16,48},{32,0},{48,16},{1,33},{17,49},{33,1},{49,17},{2,34}... | collective-permute-start | bytes 786440 | tf_op jit(solution)/shard_map/ppermute | solution.py:31
  307.1 25.0 %collective-permute-start.43 = (bf16[512,384]{1,0:T(8,128)(2,1)}, bf16[512,384]{1,0:T(8,128)(2,1)S(1)}, u32[]{:S(2)}, u32[]{:S(2)}) collective-permute-start(bf16[512,384]{1,0:T(8,128)(2,1)} %get-tuple-element.153), channel_id=1, source_target_pairs={{0,8},{4,12},{8,0},{12,4},{1,9},{5,13},{9,1},{13,5},{2,10},{6,14},... | collective-permute-start | bytes 1179656 | tf_op jit(solution)/shard_map/ppermute | solution.py:31
  309.4 27.1 %collective-permute-start.44 = (bf16[512,384]{1,0:T(8,128)(2,1)}, bf16[512,384]{1,0:T(8,128)(2,1)S(1)}, u32[]{:S(2)}, u32[]{:S(2)}) collective-permute-start(bf16[512,384]{1,0:T(8,128)(2,1)} %copy-done.52), channel_id=1, source_target_pairs={{0,4},{4,8},{8,12},{12,0},{1,5},{5,9},{9,13},{13,1},{2,6},{6,10},{... | collective-permute-start | bytes 1179656 | tf_op jit(solution)/shard_map/ppermute | solution.py:31
  310.2 26.3 %collective-permute-start.45 = (bf16[512,384]{1,0:T(8,128)(2,1)}, bf16[512,384]{1,0:T(8,128)(2,1)S(1)}, u32[]{:S(2)}, u32[]{:S(2)}) collective-permute-start(bf16[512,384]{1,0:T(8,128)(2,1)} %get-tuple-element.155), channel_id=1, source_target_pairs={{0,12},{4,0},{8,4},{12,8},{1,13},{5,1},{9,5},{13,9},{2,14},{6,2},{... | collective-permute-start | bytes 1179656 | tf_op jit(solution)/shard_map/ppermute | solution.py:31
  314.7 11.7 %collective-permute-start.50 = (bf16[512,256]{1,0:T(8,128)(2,1)}, bf16[512,256]{1,0:T(8,128)(2,1)S(1)}, u32[]{:S(2)}, u32[]{:S(2)}) collective-permute-start(bf16[512,256]{1,0:T(8,128)(2,1)} %copy-done.55), channel_id=1, source_target_pairs={{0,16},{16,32},{32,48},{48,0},{1,17},{17,33},{33,49},{49,1},{2,18}... | collective-permute-start | bytes 786440 | tf_op jit(solution)/shard_map/ppermute | solution.py:31
  324.0 8.1 %collective-permute-start.51 = (bf16[512,256]{1,0:T(8,128)(2,1)S(1)}, bf16[512,256]{1,0:T(8,128)(2,1)S(1)}, u32[]{:S(2)}, u32[]{:S(2)}) collective-permute-start(bf16[512,256]{1,0:T(8,128)(2,1)S(1)} %copy-done.54), channel_id=1, source_target_pairs={{0,48},{16,0},{32,16},{48,32},{1,49},{17,1},{33,17},{49,33},{2,50}... | collective-permute-start | bytes 786440 | tf_op jit(solution)/shard_map/ppermute | solution.py:31
  326.4 29.5 %collective-permute-start.36 = (bf16[128,2048]{1,0:T(8,128)(2,1)}, bf16[128,2048]{1,0:T(8,128)(2,1)}, u32[]{:S(2)}, u32[]{:S(2)}) collective-permute-start(bf16[128,2048]{1,0:T(8,128)(2,1)} %add_convert_fusion.2), channel_id=1, source_target_pairs={{0,64},{64,0},{1,65},{65,1},{2,66},{66,2},{3,67},{67,3},{4,68},{68... | collective-permute-start | bytes 1572872 | tf_op jit(solution)/shard_map/ppermute | solution.py:31
  336.5 14.2 %collective-permute-start.56 = (bf16[256,2048]{1,0:T(8,128)(2,1)S(1)}, bf16[256,2048]{1,0:T(8,128)(2,1)S(1)}, u32[]{:S(2)}, u32[]{:S(2)}) collective-permute-start(bf16[256,2048]{1,0:T(8,128)(2,1)S(1)} %get-tuple-element.173), channel_id=1, source_target_pairs={{0,1},{1,0},{2,3},{3,2},{4,5},{5,4},{6,7},{7,6},{8,9},{9,8},{10,11... | collective-permute-start | bytes 3145736 | tf_op jit(solution)/shard_map/ppermute | solution.py:31
  339.3 5.7 %collective-permute-start.46 = (bf16[128,384]{1,0:T(8,128)(2,1)S(1)}, bf16[128,384]{1,0:T(8,128)(2,1)S(1)}, u32[]{:S(2)}, u32[]{:S(2)}) collective-permute-start(bf16[128,384]{1,0:T(8,128)(2,1)S(1)} %get-tuple-element.190), channel_id=1, source_target_pairs={{0,16},{16,32},{32,48},{48,0},{1,17},{17,33},{33,49},{49,1},{2,18}... | collective-permute-start | bytes 294920 | tf_op jit(solution)/shard_map/ppermute | solution.py:31
  339.8 7.9 %collective-permute-start.48 = (bf16[128,384]{1,0:T(8,128)(2,1)S(1)}, bf16[128,384]{1,0:T(8,128)(2,1)S(1)}, u32[]{:S(2)}, u32[]{:S(2)}) collective-permute-start(bf16[128,384]{1,0:T(8,128)(2,1)S(1)} %get-tuple-element.191), channel_id=1, source_target_pairs={{0,32},{16,48},{32,0},{48,16},{1,33},{17,49},{33,1},{49,17},{2,34}... | collective-permute-start | bytes 294920 | tf_op jit(solution)/shard_map/ppermute | solution.py:31
  342.6 6.9 %collective-permute-start.47 = (bf16[128,384]{1,0:T(8,128)(2,1)S(1)}, bf16[128,384]{1,0:T(8,128)(2,1)S(1)}, u32[]{:S(2)}, u32[]{:S(2)}) collective-permute-start(bf16[128,384]{1,0:T(8,128)(2,1)S(1)} %get-tuple-element.192), channel_id=1, source_target_pairs={{0,48},{16,0},{32,16},{48,32},{1,49},{17,1},{33,17},{49,33},{2,50}... | collective-permute-start | bytes 294920 | tf_op jit(solution)/shard_map/ppermute | solution.py:31
  345.0 10.7 %collective-permute-start.52 = (bf16[128,768]{1,0:T(8,128)(2,1)}, bf16[128,768]{1,0:T(8,128)(2,1)}, u32[]{:S(2)}, u32[]{:S(2)}) collective-permute-start(bf16[128,768]{1,0:T(8,128)(2,1)} %get-tuple-element.187), channel_id=1, source_target_pairs={{0,4},{4,8},{8,12},{12,0},{1,5},{5,9},{9,13},{13,1},{2,6},{6,10},{... | collective-permute-start | bytes 589832 | tf_op jit(solution)/shard_map/ppermute | solution.py:31
  347.7 14.2 %collective-permute-start.55 = (bf16[128,768]{1,0:T(8,128)(2,1)}, bf16[128,768]{1,0:T(8,128)(2,1)}, u32[]{:S(2)}, u32[]{:S(2)}) collective-permute-start(bf16[128,768]{1,0:T(8,128)(2,1)} %get-tuple-element.188), channel_id=1, source_target_pairs={{0,8},{4,12},{8,0},{12,4},{1,9},{5,13},{9,1},{13,5},{2,10},{6,14},... | collective-permute-start | bytes 589832 | tf_op jit(solution)/shard_map/ppermute | solution.py:31
  349.5 12.4 %collective-permute-start.54 = (bf16[128,768]{1,0:T(8,128)(2,1)}, bf16[128,768]{1,0:T(8,128)(2,1)}, u32[]{:S(2)}, u32[]{:S(2)}) collective-permute-start(bf16[128,768]{1,0:T(8,128)(2,1)} %get-tuple-element.189), channel_id=1, source_target_pairs={{0,12},{4,0},{8,4},{12,8},{1,13},{5,1},{9,5},{13,9},{2,14},{6,2},{... | collective-permute-start | bytes 589832 | tf_op jit(solution)/shard_map/ppermute | solution.py:31
  353.3 8.5 %collective-permute-start.53 = (bf16[64,2176]{1,0:T(8,128)(2,1)}, bf16[64,2176]{1,0:T(8,128)(2,1)S(1)}, u32[]{:S(2)}, u32[]{:S(2)}) collective-permute-start(bf16[64,2176]{1,0:T(8,128)(2,1)} %dynamic-slice_bitcast_fusion), channel_id=1, source_target_pairs={{0,64},{64,0},{1,65},{65,1},{2,66},{66,2},{3,67},{67,3},{4,68},{68... | collective-permute-start | bytes 835592 | tf_op jit(solution)/shard_map/ppermute | solution.py:31
  355.7 15.7 %collective-permute-start.57 = (bf16[128,2048]{1,0:T(8,128)(2,1)}, bf16[128,2048]{1,0:T(8,128)(2,1)}, u32[]{:S(2)}, u32[]{:S(2)}) collective-permute-start(bf16[128,2048]{1,0:T(8,128)(2,1)} %add_convert_fusion), channel_id=1, source_target_pairs={{0,2},{2,0},{1,3},{3,1},{4,6},{6,4},{5,7},{7,5},{8,10},{10,8},{9,1... | collective-permute-start | bytes 1572872 | tf_op jit(solution)/shard_map/ppermute | solution.py:31
  369.2 8.0 %collective-permute-start.58 = (bf16[64,1280]{1,0:T(8,128)(2,1)S(1)}, bf16[64,1280]{1,0:T(8,128)(2,1)S(1)}, u32[]{:S(2)}, u32[]{:S(2)}) collective-permute-start(bf16[64,1280]{1,0:T(8,128)(2,1)S(1)} %dynamic-slice_bitcast_fusion.5), channel_id=1, source_target_pairs={{0,64},{64,0},{1,65},{65,1},{2,66},{66,2},{3,67},{67,3},{4,68},{68... | collective-permute-start | bytes 491528 | tf_op jit(solution)/shard_map/ppermute | solution.py:31
  (73 other events, 542.1 us)
Sparse Core Ops, SparseCore 0:
  17.4 66.1 all-gather.2
  85.7 73.1 all-gather.4
  219.6 118.5 reduce-scatter.1
